TPU v7x, 32 devices: a whole 2x2x4 slice. The times are simulated.
32 devices in a mesh: pipe: 4 (over y, x), dp: 8 (over z, core).
Axes of the slice: x: 2, y: 2, z: 4, core: 2. Of those that a mesh axis runs over, the one named last changes fastest.
Arguments:
- clips: bfloat16 [32, 4, 7, 7, 512], P('dp'), may hold values from -6 to 6
- boxes: int32 [32, 6], P('dp'), may hold values from 0 to 7, as said below
- spatial_w: bfloat16 [4, 4608, 1152], P('pipe'), may hold values from -0.09375 to 0.09375
- temporal_w: bfloat16 [4, 3456, 512], P('pipe'), may hold values from -0.109375 to 0.109375
- spatial_gain: float32 [4, 1152], P('pipe'), may hold values from 0.5 to 1.5
- spatial_shift: float32 [4, 1152], P('pipe'), may hold values from -3 to 3
- temporal_gain: float32 [4, 512], P('pipe'), may hold values from 0.5 to 1.5
- temporal_shift: float32 [4, 512], P('pipe'), may hold values from -3 to 3
- cotangent: bfloat16 [32, 4, 7, 7, 512], P('dp'), may hold values from -6 to 6
Outputs:
- activations: bfloat16 [4, 32, 4, 7, 7, 512], P('pipe', 'dp')
- input_grads: bfloat16 [4, 32, 4, 7, 7, 512], P('pipe', 'dp')
- spatial_w_grad: float32 [4, 4608, 1152], P('pipe', 'dp')
- temporal_w_grad: float32 [4, 3456, 512], P('pipe', 'dp')
- spatial_gain_grad: float32 [4, 1152], P('pipe')
- spatial_shift_grad: float32 [4, 1152], P('pipe')
- temporal_gain_grad: float32 [4, 512], P('pipe')
- temporal_shift_grad: float32 [4, 512], P('pipe')
Inputs may be any that keep to these rules, and one draw needn't show every extreme that they name: `boxes`: row c gives clip c's valid box: first and end frame, first and end row, first and end column, ends exclusive; at least 2 frames, 3 rows and 3 columns are valid.
All inputs are finite; a program needn't handle non-finite values.
Results may differ from a plain program's by a relative error of at most 0.025.
Values may be sent and summed in bfloat16 or wider, within the bound.
A program may use at most 320 MiB of HBM per device.

v0:
```python
import jax
import jax.numpy as jnp
from jax import lax
from jax.sharding import PartitionSpec as P

MB = 4


eps_norm = 1e-05


def from_behind(block, axis, distance):
    devices = range(lax.axis_size(axis))
    route = [(i - distance, i) for i in devices if i - distance in devices]
    return lax.ppermute(block, axis, route)


def valid_mask(limits, frames, height, breadth):
    frame_idx = lax.broadcasted_iota(jnp.int32, (1, frames, 1, 1), 1)
    row_idx = lax.broadcasted_iota(jnp.int32, (1, 1, height, 1), 2)
    column_idx = lax.broadcasted_iota(jnp.int32, (1, 1, 1, breadth), 3)
    bounds = limits[:, :, None, None, None]
    inside = (frame_idx >= bounds[:, 0]) & (frame_idx < bounds[:, 1])
    inside = inside & (row_idx >= bounds[:, 2]) & (row_idx < bounds[:, 3])
    inside = inside & (column_idx >= bounds[:, 4]) & (column_idx < bounds[:, 5])
    return inside.astype(jnp.float32)[..., None]


def spatial_columns(activity):
    height, breadth = (activity.shape[2], activity.shape[3])
    padded = jnp.pad(activity, ((0, 0), (0, 0), (1, 1), (1, 1), (0, 0)))
    pieces = [
        padded[:, :, row_off : row_off + height, col_off : col_off + breadth, :]
        for row_off in range(3)
        for col_off in range(3)
    ]
    return jnp.concatenate(pieces, axis=-1)


def temporal_columns(activity):
    frames = activity.shape[1]
    padded = jnp.pad(activity, ((0, 0), (1, 1), (0, 0), (0, 0), (0, 0)))
    return jnp.concatenate([padded[:, offset : offset + frames] for offset in range(3)], axis=-1)


def columns_back(builder, grad_columns, layout):
    unused, undo_cols = jax.vjp(builder, jnp.zeros(layout, jnp.float32))
    return undo_cols(grad_columns.reshape(layout[:4] + (-1,)))[0]


def silu_slope(values):
    sigmoid_v = jax.nn.sigmoid(values)
    return sigmoid_v * (1.0 + values * (1.0 - sigmoid_v))


def left_product(former, latter):
    return lax.dot_general(
        former, latter, (((0,), (0,)), ((), ())), preferred_element_type=jnp.float32
    )


def right_product(former, latter):
    return lax.dot_general(
        former, latter, (((1,), (1,)), ((), ())), preferred_element_type=jnp.float32
    )


def norm_forward(values, keep_col):
    counted, summed = lax.psum((jnp.sum(keep_col), jnp.sum(keep_col * values, axis=0)), "dp")
    center = summed / counted
    deviation = values - center
    spread = lax.psum(jnp.sum(keep_col * deviation * deviation, axis=0), "dp") / counted
    factor = lax.rsqrt(spread + eps_norm)
    return ((values - center) * factor, factor, counted)


def norm_backward(slope_in, normed, factor, gain, keep_col, counted):
    shift_sum, gain_sum = lax.psum(
        (jnp.sum(slope_in, axis=0), jnp.sum(slope_in * normed, axis=0)), "dp"
    )
    result = keep_col * (gain * factor) * (slope_in - (shift_sum + normed * gain_sum) / counted)
    return (result, gain_sum, shift_sum)


def body(
    clips,
    boxes,
    spatial_w,
    temporal_w,
    spatial_gain,
    spatial_shift,
    temporal_gain,
    temporal_shift,
    cotangent,
):
    section = lax.axis_index("pipe")
    sections = lax.axis_size("pipe")
    skipping = (section % 2).astype(jnp.float32)
    w_spatial = spatial_w[0]
    w_temporal = temporal_w[0]
    g_spatial = spatial_gain[0]
    b_spatial = spatial_shift[0]
    g_temporal = temporal_gain[0]
    b_temporal = temporal_shift[0]
    per_micro = clips.shape[0] // MB
    frames, height, breadth, channels = (
        clips.shape[1],
        clips.shape[2],
        clips.shape[3],
        clips.shape[4],
    )
    layout = (per_micro, frames, height, breadth, channels)
    pixels = per_micro * frames * height * breadth
    periods = MB + sections - 1
    recv_act = jnp.zeros(layout, jnp.bfloat16)
    recv_skip = jnp.zeros(layout, jnp.bfloat16)
    activ_out = jnp.zeros(clips.shape, jnp.bfloat16)
    records = []
    for period in range(periods):
        micro_idx = period - section
        active = (micro_idx >= 0) & (micro_idx < MB)
        offset = jnp.clip(micro_idx, 0, MB - 1) * per_micro
        own_act = lax.dynamic_slice_in_dim(clips, offset, per_micro, 0)
        act_in = jnp.where(section == 0, own_act, recv_act)
        keep_col = valid_mask(
            lax.dynamic_slice_in_dim(boxes, offset, per_micro, 0), frames, height, breadth
        ).reshape(pixels, 1)
        columns = spatial_columns(act_in).reshape(pixels, -1)
        spatial_out = jnp.dot(columns, w_spatial, preferred_element_type=jnp.float32)
        normed_a, factor_a, counted = norm_forward(spatial_out, keep_col)
        hidden = (keep_col * jax.nn.silu(g_spatial * normed_a + b_spatial)).astype(jnp.bfloat16)
        stacked = temporal_columns(hidden.reshape(layout[:4] + (-1,))).reshape(pixels, -1)
        temporal_out = jnp.dot(stacked, w_temporal, preferred_element_type=jnp.float32)
        normed_b, factor_b, unused = norm_forward(temporal_out, keep_col)
        preact = (
            g_temporal * normed_b
            + b_temporal
            + skipping * recv_skip.reshape(pixels, -1).astype(jnp.float32)
        )
        result = (keep_col * jax.nn.silu(preact)).astype(jnp.bfloat16).reshape(layout)
        activ_out = jnp.where(
            active, lax.dynamic_update_slice_in_dim(activ_out, result, offset, 0), activ_out
        )
        records.append((act_in, hidden, normed_a, factor_a, normed_b, factor_b, preact, counted))
        if period + 1 < periods:
            recv_act, recv_skip = from_behind((result, act_in), "pipe", 1)
    saved_all = jax.tree.map(lambda *pieces: jnp.stack(pieces), *records)
    recv_grad = jnp.zeros(layout, jnp.bfloat16)
    recv_skip_grad = jnp.zeros(layout, jnp.bfloat16)
    acc_spatial = jnp.zeros(w_spatial.shape, jnp.float32)
    acc_temporal = jnp.zeros(w_temporal.shape, jnp.float32)
    gain_a_acc = jnp.zeros(g_spatial.shape, jnp.float32)
    shift_a_acc = jnp.zeros(g_spatial.shape, jnp.float32)
    gain_b_acc = jnp.zeros(g_temporal.shape, jnp.float32)
    shift_b_acc = jnp.zeros(g_temporal.shape, jnp.float32)
    grads_out = jnp.zeros(clips.shape, jnp.bfloat16)
    for period in range(periods):
        micro_idx = period - (sections - 1 - section)
        active = ((micro_idx >= 0) & (micro_idx < MB)).astype(jnp.float32)
        position = jnp.clip(micro_idx, 0, MB - 1)
        offset = position * per_micro
        act_in, hidden, normed_a, factor_a, normed_b, factor_b, preact, counted = jax.tree.map(
            lambda pieces: lax.dynamic_index_in_dim(pieces, position + section, 0, False), saved_all
        )
        keep_col = valid_mask(
            lax.dynamic_slice_in_dim(boxes, offset, per_micro, 0), frames, height, breadth
        ).reshape(pixels, 1)
        own_grad = lax.dynamic_slice_in_dim(cotangent, offset, per_micro, 0)
        out_grad = (
            jnp.where(section == sections - 1, own_grad, recv_grad)
            .reshape(pixels, -1)
            .astype(jnp.float32)
        )
        slope_b = out_grad * keep_col * silu_slope(preact)
        skip_grad = (skipping * slope_b).astype(jnp.bfloat16).reshape(layout)
        grad_temporal, gain_b_sum, shift_b_sum = norm_backward(
            slope_b, normed_b, factor_b, g_temporal, keep_col, counted
        )
        grad_temporal = grad_temporal.astype(jnp.bfloat16)
        stacked = temporal_columns(hidden.reshape(layout[:4] + (-1,))).reshape(pixels, -1)
        grad_hidden = columns_back(
            temporal_columns,
            right_product(grad_temporal, w_temporal),
            layout[:4] + (hidden.shape[1],),
        ).reshape(pixels, -1)
        slope_a = keep_col * grad_hidden * silu_slope(g_spatial * normed_a + b_spatial)
        grad_spatial, gain_a_sum, shift_a_sum = norm_backward(
            slope_a, normed_a, factor_a, g_spatial, keep_col, counted
        )
        grad_spatial = grad_spatial.astype(jnp.bfloat16)
        columns = spatial_columns(act_in).reshape(pixels, -1)
        acc_temporal = acc_temporal + active * left_product(stacked, grad_temporal)
        acc_spatial = acc_spatial + active * left_product(columns, grad_spatial)
        grad_act = columns_back(spatial_columns, right_product(grad_spatial, w_spatial), layout)
        grad_in = (grad_act + recv_skip_grad.astype(jnp.float32)).astype(jnp.bfloat16)
        grads_out = jnp.where(
            active > 0, lax.dynamic_update_slice_in_dim(grads_out, grad_in, offset, 0), grads_out
        )
        gain_a_acc = gain_a_acc + active * gain_a_sum
        shift_a_acc = shift_a_acc + active * shift_a_sum
        gain_b_acc = gain_b_acc + active * gain_b_sum
        shift_b_acc = shift_b_acc + active * shift_b_sum
        if period + 1 < periods:
            recv_grad, recv_skip_grad = from_behind((grad_in, skip_grad), "pipe", -1)
    sum_spatial, sum_temporal = (
        lax.psum_scatter(acc_spatial, "dp", scatter_dimension=0, tiled=True),
        lax.psum_scatter(acc_temporal, "dp", scatter_dimension=0, tiled=True),
    )
    return (
        activ_out[None],
        grads_out[None],
        sum_spatial[None],
        sum_temporal[None],
        gain_a_acc[None],
        shift_a_acc[None],
        gain_b_acc[None],
        shift_b_acc[None],
    )


def solution(mesh):
    placed = (
        P("dp", None, None, None, None),
        P("dp", None),
        P("pipe", None, None),
        P("pipe", None, None),
        P("pipe", None),
        P("pipe", None),
        P("pipe", None),
        P("pipe", None),
        P("dp", None, None, None, None),
    )
    return jax.shard_map(
        body,
        mesh=mesh,
        in_specs=placed,
        out_specs=(
            P("pipe", "dp", None, None, None, None),
            P("pipe", "dp", None, None, None, None),
            P("pipe", "dp", None),
            P("pipe", "dp", None),
            P("pipe", None),
            P("pipe", None),
            P("pipe", None),
            P("pipe", None),
        ),
        check_vma=False,
    )
```

profile of v0, /device:TPU:0, one launch (start us, length us, event | category | flops | bytes accessed | tf_op | source)
XLA Modules:
  0.0 2252.2 jit_solution(7445031733790208757)
XLA Ops:
  51.0 17.7 all-reduce.132
  288.5 15.0 all-reduce.131
  307.3 14.6 psum.469
  419.6 14.8 all-reduce.130
  438.4 14.6 psum.474
  469.1 14.5 psum.475
  551.4 14.8 all-reduce.129
  570.1 14.6 psum.479
  683.3 14.8 all-reduce.128
  702.0 15.0 psum.484
  815.5 14.8 all-reduce.127
  834.1 14.6 psum.489
  934.1 14.8 all-reduce.126
  952.8 14.6 psum.494
  1078.5 27.1 %all-reduce.124 = (f32[1152]{0:T(1024)}, f32[1152]{0:T(1024)}) all-reduce(f32[1152]{0:T(1024)} %fusion.196, f32[1152]{0:T(1024)} %get-tuple-element.155), channel_id=1, replica_groups=mesh['pipe'=4,'dp'=8] {'dp'}, use_global_device_ids=true, to_apply=%region_77.78 | all-reduce | flops 2304 | bytes 18432 | tf_op jit(solution)/shard_map/psum | solution.py:78
  1409.2 14.5 all-reduce.123
  1435.2 27.1 %all-reduce.122 = (f32[1152]{0:T(1024)}, f32[1152]{0:T(1024)}) all-reduce(f32[1152]{0:T(1024)} %fusion.190, f32[1152]{0:T(1024)} %get-tuple-element.148), channel_id=1, replica_groups=mesh['pipe'=4,'dp'=8] {'dp'}, use_global_device_ids=true, to_apply=%region_85.86 | all-reduce | flops 2304 | bytes 18432 | tf_op jit(solution)/shard_map/psum | solution.py:78
  1511.1 14.6 all-reduce.121
  1537.2 27.1 %all-reduce.120 = (f32[1152]{0:T(1024)}, f32[1152]{0:T(1024)}) all-reduce(f32[1152]{0:T(1024)} %fusion.184, f32[1152]{0:T(1024)} %get-tuple-element.139), channel_id=1, replica_groups=mesh['pipe'=4,'dp'=8] {'dp'}, use_global_device_ids=true, to_apply=%region_93.94 | all-reduce | flops 2304 | bytes 18432 | tf_op jit(solution)/shard_map/psum | solution.py:78
  1603.3 14.6 all-reduce.119
  1629.4 27.2 %all-reduce.118 = (f32[1152]{0:T(1024)}, f32[1152]{0:T(1024)}) all-reduce(f32[1152]{0:T(1024)} %fusion.178, f32[1152]{0:T(1024)} %get-tuple-element.130), channel_id=1, replica_groups=mesh['pipe'=4,'dp'=8] {'dp'}, use_global_device_ids=true, to_apply=%region_101.102 | all-reduce | flops 2304 | bytes 18432 | tf_op jit(solution)/shard_map/psum | solution.py:78
  1694.4 14.6 all-reduce.117
  1720.5 27.3 %all-reduce.116 = (f32[1152]{0:T(1024)}, f32[1152]{0:T(1024)}) all-reduce(f32[1152]{0:T(1024)} %fusion.172, f32[1152]{0:T(1024)} %get-tuple-element.121), channel_id=1, replica_groups=mesh['pipe'=4,'dp'=8] {'dp'}, use_global_device_ids=true, to_apply=%region_109.110 | all-reduce | flops 2304 | bytes 18432 | tf_op jit(solution)/shard_map/psum | solution.py:78
  1785.5 14.6 all-reduce.115
  1811.6 27.5 %all-reduce.114 = (f32[1152]{0:T(1024)}, f32[1152]{0:T(1024)}) all-reduce(f32[1152]{0:T(1024)} %fusion.166, f32[1152]{0:T(1024)} %get-tuple-element.112), channel_id=1, replica_groups=mesh['pipe'=4,'dp'=8] {'dp'}, use_global_device_ids=true, to_apply=%region_117.118 | all-reduce | flops 2304 | bytes 18432 | tf_op jit(solution)/shard_map/psum | solution.py:78
  1886.0 19.7 multiply_add_fusion
  1905.9 20.9 fusion.4
  1926.9 14.5 fusion.3
  1941.5 19.9 fusion.2
  1989.1 27.3 %all-reduce.112 = (f32[1152]{0:T(1024)}, f32[1152]{0:T(1024)}) all-reduce(f32[1152]{0:T(1024)} %fusion.160, f32[1152]{0:T(1024)} %get-tuple-element.99), channel_id=1, replica_groups=mesh['pipe'=4,'dp'=8] {'dp'}, use_global_device_ids=true, to_apply=%region_125.126 | all-reduce | flops 2304 | bytes 18432 | tf_op jit(solution)/shard_map/psum | solution.py:78
  2016.4 19.7 fusion
  2065.8 179.4 %reduce-scatter.3.cloned.1.call-done = f32[576,1152]{1,0:T(8,128)} async-done(((f32[4608,1152]{1,0:T(8,128)}), f32[576,1152]{1,0:T(8,128)}) %reduce-scatter.3.cloned.1.call-update) | async-done | bytes 2654224 | tf_op jit(solution)/shard_map/reduce_scatter | solution.py:206
  (1256 shorter events, 1487.4 us)
Async XLA Ops:
  7.2 91.9 %copy-start = (bf16[1,3456,512]{2,1,0:T(8,128)(2,1)S(1)}, bf16[1,3456,512]{2,1,0:T(8,128)(2,1)}, u32[]{:S(2)}) copy-start(bf16[1,3456,512]{2,1,0:T(8,128)(2,1)} %param.12) | copy-start | bytes 10616836
  7.2 2058.6 %reduce-scatter.5.cloned.1.call-start = ((), (), s32[]{:S(2)}) async-start(), calls=%async_computation.3 | async-start | bytes 7962624 | tf_op jit(solution)/shard_map/reduce_scatter | solution.py:207
  11.7 247.4 %collective-permute-start.1 = (bf16[1,4,7,7,512]{4,3,2,1,0:T(8,128)(2,1)}, bf16[1,4,7,7,512]{4,3,2,1,0:T(8,128)(2,1)}, u32[]{:S(2)}, u32[]{:S(2)}) collective-permute-start(bf16[1,4,7,7,512]{4,3,2,1,0:T(8,128)(2,1)} %copy_select_fusion.13), channel_id=1, source_target_pairs={{0,8},{8,16},{16,24},{1,9},{9,17},{17,25},{2,10},{10,18},{18,26},{... | collective-permute-start | bytes 602120 | tf_op jit(solution)/shard_map/ppermute | solution.py:15
  140.2 111.8 %collective-permute-start = (bf16[1,4,7,7,512]{4,3,2,1,0:T(8,128)(2,1)}, bf16[1,4,7,7,512]{4,3,2,1,0:T(8,128)(2,1)}, u32[]{:S(2)}, u32[]{:S(2)}) collective-permute-start(bf16[1,4,7,7,512]{4,3,2,1,0:T(8,128)(2,1)} %reshape.3897), channel_id=1, source_target_pairs={{0,8},{8,16},{16,24},{1,9},{9,17},{17,25},{2,10},{10,18},{18,26},{... | collective-permute-start | bytes 602120 | tf_op jit(solution)/shard_map/ppermute | solution.py:15
  253.7 136.4 %collective-permute-start.3 = (bf16[1,4,7,7,512]{4,3,2,1,0:T(8,128)(2,1)}, bf16[1,4,7,7,512]{4,3,2,1,0:T(8,128)(2,1)}, u32[]{:S(2)}, u32[]{:S(2)}) collective-permute-start(bf16[1,4,7,7,512]{4,3,2,1,0:T(8,128)(2,1)} %get-tuple-element.98), channel_id=1, source_target_pairs={{0,8},{8,16},{16,24},{1,9},{9,17},{17,25},{2,10},{10,18},{18,26},{... | collective-permute-start | bytes 602120 | tf_op jit(solution)/shard_map/ppermute | solution.py:15
  375.7 6.9 collective-permute-start.2
  383.5 138.5 %collective-permute-start.5 = (bf16[1,4,7,7,512]{4,3,2,1,0:T(8,128)(2,1)}, bf16[1,4,7,7,512]{4,3,2,1,0:T(8,128)(2,1)}, u32[]{:S(2)}, u32[]{:S(2)}) collective-permute-start(bf16[1,4,7,7,512]{4,3,2,1,0:T(8,128)(2,1)} %get-tuple-element.96), channel_id=1, source_target_pairs={{0,8},{8,16},{16,24},{1,9},{9,17},{17,25},{2,10},{10,18},{18,26},{... | collective-permute-start | bytes 602120 | tf_op jit(solution)/shard_map/ppermute | solution.py:15
  507.1 7.3 collective-permute-start.4
  515.3 138.5 %collective-permute-start.7 = (bf16[1,4,7,7,512]{4,3,2,1,0:T(8,128)(2,1)}, bf16[1,4,7,7,512]{4,3,2,1,0:T(8,128)(2,1)}, u32[]{:S(2)}, u32[]{:S(2)}) collective-permute-start(bf16[1,4,7,7,512]{4,3,2,1,0:T(8,128)(2,1)} %get-tuple-element.94), channel_id=1, source_target_pairs={{0,8},{8,16},{16,24},{1,9},{9,17},{17,25},{2,10},{10,18},{18,26},{... | collective-permute-start | bytes 602120 | tf_op jit(solution)/shard_map/ppermute | solution.py:15
  638.5 7.8 collective-permute-start.6
  647.1 138.9 %collective-permute-start.9 = (bf16[1,4,7,7,512]{4,3,2,1,0:T(8,128)(2,1)}, bf16[1,4,7,7,512]{4,3,2,1,0:T(8,128)(2,1)}, u32[]{:S(2)}, u32[]{:S(2)}) collective-permute-start(bf16[1,4,7,7,512]{4,3,2,1,0:T(8,128)(2,1)} %get-tuple-element.92), channel_id=1, source_target_pairs={{0,8},{8,16},{16,24},{1,9},{9,17},{17,25},{2,10},{10,18},{18,26},{... | collective-permute-start | bytes 602120 | tf_op jit(solution)/shard_map/ppermute | solution.py:15
  770.8 7.7 collective-permute-start.8
  779.4 130.3 %collective-permute-start.11 = (bf16[1,4,7,7,512]{4,3,2,1,0:T(8,128)(2,1)}, bf16[1,4,7,7,512]{4,3,2,1,0:T(8,128)(2,1)}, u32[]{:S(2)}, u32[]{:S(2)}) collective-permute-start(bf16[1,4,7,7,512]{4,3,2,1,0:T(8,128)(2,1)} %get-tuple-element.90), channel_id=1, source_target_pairs={{0,8},{8,16},{16,24},{1,9},{9,17},{17,25},{2,10},{10,18},{18,26},{... | collective-permute-start | bytes 602120 | tf_op jit(solution)/shard_map/ppermute | solution.py:15
  902.2 11.0 collective-permute-start.10
  1117.3 356.7 %collective-permute-start.13 = (bf16[1,4,7,7,512]{4,3,2,1,0:T(8,128)(2,1)}, bf16[1,4,7,7,512]{4,3,2,1,0:T(8,128)(2,1)}, u32[]{:S(2)}, u32[]{:S(2)}) collective-permute-start(bf16[1,4,7,7,512]{4,3,2,1,0:T(8,128)(2,1)} %get-tuple-element.146), channel_id=1, source_target_pairs={{8,0},{16,8},{24,16},{9,1},{17,9},{25,17},{10,2},{18,10},{26,18},{... | collective-permute-start | bytes 602120 | tf_op jit(solution)/shard_map/ppermute | solution.py:15
  1125.0 270.2 %collective-permute-start.12 = (bf16[1,4,7,7,512]{4,3,2,1,0:T(8,128)(2,1)}, bf16[1,4,7,7,512]{4,3,2,1,0:T(8,128)(2,1)}, u32[]{:S(2)}, u32[]{:S(2)}) collective-permute-start(bf16[1,4,7,7,512]{4,3,2,1,0:T(8,128)(2,1)} %get-tuple-element.154), channel_id=1, source_target_pairs={{8,0},{16,8},{24,16},{9,1},{17,9},{25,17},{10,2},{18,10},{26,18},{... | collective-permute-start | bytes 602120 | tf_op jit(solution)/shard_map/ppermute | solution.py:15
  1472.5 103.7 %collective-permute-start.15 = (bf16[1,4,7,7,512]{4,3,2,1,0:T(8,128)(2,1)}, bf16[1,4,7,7,512]{4,3,2,1,0:T(8,128)(2,1)}, u32[]{:S(2)}, u32[]{:S(2)}) collective-permute-start(bf16[1,4,7,7,512]{4,3,2,1,0:T(8,128)(2,1)} %get-tuple-element.137), channel_id=1, source_target_pairs={{8,0},{16,8},{24,16},{9,1},{17,9},{25,17},{10,2},{18,10},{26,18},{... | collective-permute-start | bytes 602120 | tf_op jit(solution)/shard_map/ppermute | solution.py:15
  1476.6 20.4 collective-permute-start.14
  1574.6 94.0 %collective-permute-start.17 = (bf16[1,4,7,7,512]{4,3,2,1,0:T(8,128)(2,1)}, bf16[1,4,7,7,512]{4,3,2,1,0:T(8,128)(2,1)}, u32[]{:S(2)}, u32[]{:S(2)}) collective-permute-start(bf16[1,4,7,7,512]{4,3,2,1,0:T(8,128)(2,1)} %get-tuple-element.128), channel_id=1, source_target_pairs={{8,0},{16,8},{24,16},{9,1},{17,9},{25,17},{10,2},{18,10},{26,18},{... | collective-permute-start | bytes 602120 | tf_op jit(solution)/shard_map/ppermute | solution.py:15
  1578.6 10.8 collective-permute-start.16
  1667.1 92.7 %collective-permute-start.19 = (bf16[1,4,7,7,512]{4,3,2,1,0:T(8,128)(2,1)}, bf16[1,4,7,7,512]{4,3,2,1,0:T(8,128)(2,1)}, u32[]{:S(2)}, u32[]{:S(2)}) collective-permute-start(bf16[1,4,7,7,512]{4,3,2,1,0:T(8,128)(2,1)} %get-tuple-element.119), channel_id=1, source_target_pairs={{8,0},{16,8},{24,16},{9,1},{17,9},{25,17},{10,2},{18,10},{26,18},{... | collective-permute-start | bytes 602120 | tf_op jit(solution)/shard_map/ppermute | solution.py:15
  1671.1 9.5 collective-permute-start.18
  1758.2 91.4 %collective-permute-start.21 = (bf16[1,4,7,7,512]{4,3,2,1,0:T(8,128)(2,1)}, bf16[1,4,7,7,512]{4,3,2,1,0:T(8,128)(2,1)}, u32[]{:S(2)}, u32[]{:S(2)}) collective-permute-start(bf16[1,4,7,7,512]{4,3,2,1,0:T(8,128)(2,1)} %get-tuple-element.110), channel_id=1, source_target_pairs={{8,0},{16,8},{24,16},{9,1},{17,9},{25,17},{10,2},{18,10},{26,18},{... | collective-permute-start | bytes 602120 | tf_op jit(solution)/shard_map/ppermute | solution.py:15
  1762.2 9.5 collective-permute-start.20
  1852.1 8.8 collective-permute-start.22
  1905.8 339.4 %reduce-scatter.3.cloned.1.call-start = ((), (), s32[]{:S(2)}) async-start(), calls=%async_computation.2 | async-start | bytes 23887872 | tf_op jit(solution)/shard_map/reduce_scatter | solution.py:206
  1905.8 21.0 copy-start.3
  1905.9 20.9 copy-start.7
  1905.9 20.9 copy-start.17
  1905.9 20.9 copy-start.220
  1905.9 20.9 copy-start.228
  2049.0 11.3 collective-permute-start.23
  (256 other events, 1279.7 us)
Sparse Core Ops, SparseCore 0:
  1905.9 75.9 reduce-scatter.4
  2036.2 208.9 reduce-scatter.2
where the time goes:
time: 2280 us; the launch traced here: 2250 us
  blocking collectives  701 us (31%)
  local copies, waits for them, and re-layouts  605 us (27%)
  matrix products  341 us (15%)
  other arithmetic  329 us (14%)
  waiting for transfers between devices  198 us (9%)
  starting transfers between devices  60.6 us (3%)
    psum x14, blocking collectives, norm_backward(): lax.psum((jnp.sum(slope_in, axis=0), jnp.sum(slope_in * normed, axis=0)),...  292 us
    psum x14, blocking collectives, norm_forward(): lax.psum((jnp.sum(keep_col), jnp.sum(keep_col * values, axis=0)), 'dp')  207 us
    psum x14, blocking collectives, norm_forward(): lax.psum(jnp.sum(keep_col * deviation * deviation, axis=0), 'dp') / counted  202 us
    reduce_scatter x1, waiting for transfers between devices, body(): lax.psum_scatter(acc_spatial, 'dp', scatter_dimension=0, tiled=True)  179 us
    dot_general x14, matrix products, left_product(): lax.dot_general(former, latter, (((0,), (0,)), ((), ())), preferred_eleme...  165 us
    unnamed x639, local copies, waits for them, and re-layouts  157 us
    concatenate x77, local copies, waits for them, and re-layouts, spatial_columns(): return jnp.concatenate(pieces, axis=-1)  119 us
    dot_general x14, matrix products, right_product(): lax.dot_general(former, latter, (((1,), (1,)), ((), ())), preferred_eleme...  91.4 us
  transfers between devices with their start and end apart: 26, of which 9 were waited for; matrix products, arithmetic and copies ran while one was open for 49% of the time, Pallas kernels for 0%

commit v1 on v0

v1 whole, which is shorter than its diff:
```python
import functools

import jax
import jax.numpy as jnp
from jax import lax
from jax.experimental import pallas as pl
from jax.experimental.pallas import tpu as pltpu
from jax.sharding import PartitionSpec as P

MB = 4
eps_norm = 1e-05
bf16 = jnp.bfloat16
f32 = jnp.float32
MESH = pl.DeviceIdType.MESH


def silu(x):
    return x / (1.0 + jnp.exp(-x))


def silu_slope(x):
    s = 1.0 / (1.0 + jnp.exp(-x))
    return s * (1.0 + x * (1.0 - s))


def lane_chunks(width, body):
    def step(i, carry):
        body(i, pl.ds(pl.multiple_of(i * 128, 128), 128))
        return carry

    lax.fori_loop(0, width // 128, step, 0)


def relay_kernel(
    dims,
    clips,
    boxes,
    w_s_hbm,
    w_t_hbm,
    g_s,
    b_s,
    g_t,
    b_t,
    cotangent,
    o_act,
    o_grad,
    o_in,
    o_hidden,
    o_gu,
    o_gr,
    o_gain_s,
    o_shift_s,
    o_gain_t,
    o_shift_t,
    w_s,
    w_t,
    w_s_back,
    w_t_back,
    cols,
    a_in,
    skip_in,
    a_out,
    ga_in,
    gs_in,
    gs_out,
    ig_out,
    hidden,
    gr,
    gu,
    uh,
    rh,
    gp,
    gq,
    keep,
    fact_s,
    fact_t,
    cnt,
    x_s,
    x_t,
    x_bt,
    x_bs,
    x_send,
    x_recv,
    w_sem,
    load_sem,
    store_sem,
    pipe_send,
    pipe_recv,
):
    cm, frames, height, width = dims
    rows = cm * frames * height * width
    d = a_in.shape[2]
    m_ch = hidden.shape[2]
    section = lax.axis_index("pipe")
    me = lax.axis_index("dp")
    n_pipe = lax.axis_size("pipe")
    n_dp = lax.axis_size("dp")
    first = section == 0
    last = section == n_pipe - 1
    odd = lax.rem(section, 2) == 1
    even_inner = jnp.logical_and(jnp.logical_not(odd), jnp.logical_not(last))
    skipping = odd.astype(f32)

    load_ws = pltpu.make_async_copy(w_s_hbm, w_s, w_sem.at[0])
    load_wt = pltpu.make_async_copy(w_t_hbm, w_t, w_sem.at[1])
    load_ws.start()
    load_wt.start()

    def load_clip(m):
        return pltpu.make_async_copy(clips.at[m], a_in.at[m], load_sem.at[m])

    def load_cot(m):
        return pltpu.make_async_copy(cotangent.at[m], ga_in.at[m], load_sem.at[m])

    @pl.when(first)
    def _():
        for m in range(MB):
            load_clip(m).start()

    @pl.when(last)
    def _():
        for m in range(MB):
            load_cot(m).start()

    for ref in (o_gain_s, o_shift_s, o_gain_t, o_shift_t, skip_in, gs_in):
        ref[...] = jnp.zeros_like(ref)

    barrier = pltpu.get_barrier_semaphore()

    def greet(j, carry):
        pl.semaphore_signal(
            barrier, 1, device_id={"dp": lax.rem(me + j, n_dp)}, device_id_type=MESH
        )
        return carry

    lax.fori_loop(1, n_dp, greet, 0)

    @pl.when(jnp.logical_not(first))
    def _():
        pl.semaphore_signal(barrier, 1, device_id={"pipe": section - 1}, device_id_type=MESH)

    @pl.when(jnp.logical_not(last))
    def _():
        pl.semaphore_signal(barrier, 1, device_id={"pipe": section + 1}, device_id_type=MESH)

    def make_keep(m, carry):
        n_rows = frames * height * width
        pieces = []
        for c in range(cm):
            shape = (frames, height, width, 128)
            t = lax.broadcasted_iota(jnp.int32, shape, 0)
            h = lax.broadcasted_iota(jnp.int32, shape, 1)
            w = lax.broadcasted_iota(jnp.int32, shape, 2)
            box = [boxes[m * cm + c, i] for i in range(6)]
            inside = (t >= box[0]) & (t < box[1]) & (h >= box[2]) & (h < box[3])
            inside = inside & (w >= box[4]) & (w < box[5])
            pieces.append(jnp.where(inside, 1.0, 0.0).astype(f32).reshape(n_rows, 128))
        mask = jnp.concatenate(pieces, axis=0) if cm > 1 else pieces[0]
        keep[m] = mask
        cnt[m] = jnp.sum(mask, axis=0, keepdims=True)
        return carry

    lax.fori_loop(0, MB, make_keep, 0)
    pl.semaphore_wait(barrier, n_dp + 1 - jnp.where(first, 1, 0) - jnp.where(last, 1, 0))

    def share(kind, buf, m):
        def send(j, carry):
            pltpu.make_async_remote_copy(
                src_ref=buf.at[m, me],
                dst_ref=buf.at[m, me],
                send_sem=x_send.at[kind, m],
                recv_sem=x_recv.at[kind, m],
                device_id={"dp": lax.rem(me + j, n_dp)},
                device_id_type=MESH,
            ).start()
            return carry

        lax.fori_loop(1, n_dp, send, 0)

    def shared(kind, buf, m):
        others = buf.at[m, pl.ds(0, n_dp - 1)]
        pltpu.make_async_copy(others, others, x_send.at[kind, m]).wait()
        pltpu.make_async_copy(others, others, x_recv.at[kind, m]).wait()

    def to_pipe(kind, src, dst, m, step):
        return pltpu.make_async_remote_copy(
            src_ref=src.at[m],
            dst_ref=dst.at[m],
            send_sem=pipe_send.at[kind, m],
            recv_sem=pipe_recv.at[kind, m],
            device_id={"pipe": section + step},
            device_id_type=MESH,
        )

    def store(kind, src, dst, m):
        return pltpu.make_async_copy(src.at[m], dst.at[m], store_sem.at[kind, m])

    def shift_space(x, dh, dw):
        if dw:
            x = pltpu.roll(x, (-dw) % rows, 0)
        return shift_rows(x, dh)

    def shift_rows(x, dh):
        if not dh:
            return x
        y = x.reshape(cm * frames, height * width, 128)
        zero = jnp.zeros((cm * frames, width, 128), f32)
        if dh > 0:
            y = jnp.concatenate([y[:, width:], zero], axis=1)
        else:
            y = jnp.concatenate([zero, y[:, :-width]], axis=1)
        return y.reshape(rows, 128)

    def shift_time(x, dt):
        if not dt:
            return x
        y = x.reshape(cm, frames * height * width, 128)
        step = height * width
        zero = jnp.zeros((cm, step, 128), f32)
        if dt > 0:
            y = jnp.concatenate([y[:, step:], zero], axis=1)
        else:
            y = jnp.concatenate([zero, y[:, :-step]], axis=1)
        return y.reshape(rows, 128)

    def local_sums(m, value, buf, c, channels):
        mask = keep[m]
        n_here = cnt[m]
        total = jnp.sum(mask * value, axis=0, keepdims=True)
        dev = mask * (value - total / n_here)
        spread = jnp.sum(dev * dev, axis=0, keepdims=True)
        buf[m, me, :, pl.ds(pl.multiple_of(c * 128, 128), 128)] = total
        buf[m, me, :, pl.ds(pl.multiple_of(channels + c * 128, 128), 128)] = spread

    def merged(m, buf, c, channels):
        counts = buf[m, :, :, 2 * channels :]
        sums = buf[m, :, :, pl.ds(pl.multiple_of(c * 128, 128), 128)]
        spreads = buf[m, :, :, pl.ds(pl.multiple_of(channels + c * 128, 128), 128)]
        n = jnp.sum(counts, axis=0)
        mean = jnp.sum(sums, axis=0) / n
        off = sums / counts - mean[None]
        var = jnp.sum(spreads + counts * off * off, axis=0) / n
        return n, mean, lax.rsqrt(var + eps_norm)

    def forward_spatial(m):
        @pl.when(first)
        def _():
            load_clip(m).wait()

        @pl.when(jnp.logical_not(first))
        def _():
            to_pipe(0, a_out, a_in, m, 1).wait_recv()

        @pl.when(even_inner)
        def _():
            to_pipe(1, a_in, skip_in, m, 1).start()

        store(2, a_in, o_in, m).start()

        def column(i, s):
            x = a_in[m, :, s].astype(f32)
            for dw in (-1, 0, 1):
                y = shift_space(x, 0, dw)
                for dh in (-1, 0, 1):
                    tap = (dh + 1) * 3 + dw + 1
                    at = pl.ds(pl.multiple_of(tap * d + i * 128, 128), 128)
                    cols[:, at] = shift_rows(y, dh).astype(bf16)

        lane_chunks(d, column)

        @pl.when(m == 0)
        def _():
            load_ws.wait()

        uh[m] = jnp.dot(cols[:, : 9 * d], w_s[...], preferred_element_type=f32)
        x_s[m, me, :, 2 * m_ch :] = cnt[m]
        lane_chunks(m_ch, lambda i, s: local_sums(m, uh[m, :, s], x_s, i, m_ch))
        share(0, x_s, m)

    def forward_temporal(m):
        shared(0, x_s, m)

        def column(i, s):
            n, mean, rstd = merged(m, x_s, i, m_ch)
            fact_s[m, :, s] = rstd
            normed = (uh[m, :, s] - mean) * rstd
            uh[m, :, s] = normed
            value = keep[m] * silu(g_s[:, s] * normed + b_s[:, s])
            value = value.astype(bf16)
            hidden[m, :, s] = value
            value = value.astype(f32)
            for dt in (-1, 0, 1):
                at = pl.ds(pl.multiple_of((dt + 1) * m_ch + i * 128, 128), 128)
                cols[:, at] = shift_time(value, dt).astype(bf16)

        lane_chunks(m_ch, column)
        store(3, hidden, o_hidden, m).start()

        @pl.when(m == 0)
        def _():
            load_wt.wait()

        rh[m] = jnp.dot(cols[:, : 3 * m_ch], w_t[...], preferred_element_type=f32)
        x_t[m, me, :, 2 * d :] = cnt[m]
        lane_chunks(d, lambda i, s: local_sums(m, rh[m, :, s], x_t, i, d))
        share(1, x_t, m)

    def preact(m, s, normed):
        return g_t[:, s] * normed + b_t[:, s] + skipping * skip_in[m, :, s].astype(f32)

    def forward_out(m):
        shared(1, x_t, m)

        @pl.when(odd)
        def _():
            to_pipe(1, a_in, skip_in, m, 1).wait_recv()

        def column(i, s):
            n, mean, rstd = merged(m, x_t, i, d)
            fact_t[m, :, s] = rstd
            normed = (rh[m, :, s] - mean) * rstd
            rh[m, :, s] = normed
            a_out[m, :, s] = (keep[m] * silu(preact(m, s, normed))).astype(bf16)

        lane_chunks(d, column)

        @pl.when(jnp.logical_not(last))
        def _():
            to_pipe(0, a_out, a_in, m, 1).start()

        store(0, a_out, o_act, m).start()

    def backward_in(m):
        @pl.when(last)
        def _():
            load_cot(m).wait()

        @pl.when(jnp.logical_not(last))
        def _():
            to_pipe(2, ig_out, ga_in, m, -1).wait_recv()

        def column(i, s):
            normed = rh[m, :, s]
            slope = ga_in[m, :, s].astype(f32) * keep[m] * silu_slope(preact(m, s, normed))
            gp[m, :, s] = slope
            gs_out[m, :, s] = slope.astype(bf16)
            x_bt[m, me, :, s] = jnp.sum(slope, axis=0, keepdims=True)
            at = pl.ds(pl.multiple_of(d + i * 128, 128), 128)
            x_bt[m, me, :, at] = jnp.sum(slope * normed, axis=0, keepdims=True)

        lane_chunks(d, column)
        share(2, x_bt, m)

        @pl.when(odd)
        def _():
            to_pipe(3, gs_out, gs_in, m, -1).start()

    def totals(buf, m, s, i, channels):
        at = pl.ds(pl.multiple_of(channels + i * 128, 128), 128)
        return jnp.sum(buf[m, :, :, s], axis=0), jnp.sum(buf[m, :, :, at], axis=0)

    def backward_temporal(m):
        shared(2, x_bt, m)
        n = jnp.sum(x_t[m, :, :, 2 * d :], axis=0)

        def column(i, s):
            shift_sum, gain_sum = totals(x_bt, m, s, i, d)
            o_shift_t[:, s] += shift_sum
            o_gain_t[:, s] += gain_sum
            scale = g_t[:, s] * fact_t[m, :, s]
            value = keep[m] * scale * (gp[m, :, s] - (shift_sum + rh[m, :, s] * gain_sum) / n)
            value = value.astype(bf16)
            gr[m, :, s] = value
            value = value.astype(f32)
            for dt in (-1, 0, 1):
                at = pl.ds(pl.multiple_of((dt + 1) * d + i * 128, 128), 128)
                cols[:, at] = shift_time(value, -dt).astype(bf16)

        lane_chunks(d, column)
        store(4, gr, o_gr, m).start()
        gq[...] = jnp.dot(cols[:, : 3 * d], w_t_back[...], preferred_element_type=f32)

        def sums(i, s):
            normed = uh[m, :, s]
            slope = keep[m] * gq[:, s] * silu_slope(g_s[:, s] * normed + b_s[:, s])
            gq[:, s] = slope
            x_bs[m, me, :, s] = jnp.sum(slope, axis=0, keepdims=True)
            at = pl.ds(pl.multiple_of(m_ch + i * 128, 128), 128)
            x_bs[m, me, :, at] = jnp.sum(slope * normed, axis=0, keepdims=True)

        lane_chunks(m_ch, sums)
        share(3, x_bs, m)

    def backward_spatial(m):
        shared(3, x_bs, m)
        n = jnp.sum(x_t[m, :, :, 2 * d :], axis=0)

        def column(i, s):
            shift_sum, gain_sum = totals(x_bs, m, s, i, m_ch)
            o_shift_s[:, s] += shift_sum
            o_gain_s[:, s] += gain_sum
            scale = g_s[:, s] * fact_s[m, :, s]
            value = keep[m] * scale * (gq[:, s] - (shift_sum + uh[m, :, s] * gain_sum) / n)
            value = value.astype(bf16)
            gu[m, :, s] = value
            value = value.astype(f32)
            for dw in (-1, 0, 1):
                y = shift_space(value, 0, -dw)
                for dh in (-1, 0, 1):
                    tap = (dh + 1) * 3 + dw + 1
                    at = pl.ds(pl.multiple_of(tap * m_ch + i * 128, 128), 128)
                    cols[:, at] = shift_rows(y, -dh).astype(bf16)

        lane_chunks(m_ch, column)
        store(5, gu, o_gu, m).start()

        @pl.when(even_inner)
        def _():
            to_pipe(3, gs_out, gs_in, m, -1).wait_recv()

        with_skip = even_inner.astype(f32)
        half = d // 2
        for part in range(2):
            s = slice(part * half, (part + 1) * half)
            value = jnp.dot(cols[...], w_s_back[:, s], preferred_element_type=f32)
            ig_out[m, :, s] = (value + with_skip * gs_in[m, :, s].astype(f32)).astype(bf16)

        @pl.when(jnp.logical_not(first))
        def _():
            to_pipe(2, ig_out, ga_in, m, -1).start()

        store(1, ig_out, o_grad, m).start()

    def turn_weights():
        def spatial(tap, carry):
            src = pl.ds(pl.multiple_of(tap * d, 128), d)
            dst = pl.ds(pl.multiple_of(tap * m_ch, 128), m_ch)
            w_s_back[dst, :] = w_s[src, :].T
            return carry

        lax.fori_loop(0, 9, spatial, 0)

        def temporal(tap, carry):
            src = pl.ds(pl.multiple_of(tap * m_ch, 128), m_ch)
            dst = pl.ds(pl.multiple_of(tap * d, 128), d)
            w_t_back[dst, :] = w_t[src, :].T
            return carry

        lax.fori_loop(0, 3, temporal, 0)

    wait_back = jnp.where(last, 1, MB)

    def step(s, carry):
        mf = s
        mb = s - wait_back
        do_f = mf < MB
        do_b = jnp.logical_and(mb >= 0, mb < MB)
        mf = jnp.minimum(mf, MB - 1)
        mb = jnp.clip(mb, 0, MB - 1)

        @pl.when(do_f)
        def _():
            forward_spatial(mf)

        @pl.when(s == wait_back)
        def _():
            turn_weights()

        @pl.when(do_b)
        def _():
            backward_in(mb)

        @pl.when(do_f)
        def _():
            forward_temporal(mf)

        @pl.when(do_b)
        def _():
            backward_temporal(mb)

        @pl.when(do_f)
        def _():
            forward_out(mf)

        @pl.when(do_b)
        def _():
            backward_spatial(mb)

        return carry

    lax.fori_loop(0, 2 * MB, step, 0)

    def finish(m, carry):
        for kind, (src, dst) in enumerate(
            (
                (a_out, o_act),
                (ig_out, o_grad),
                (a_in, o_in),
                (hidden, o_hidden),
                (gr, o_gr),
                (gu, o_gu),
            )
        ):
            store(kind, src, dst, m).wait()

        @pl.when(jnp.logical_not(last))
        def _():
            to_pipe(0, a_out, a_in, m, 1).wait_send()

        @pl.when(even_inner)
        def _():
            to_pipe(1, a_in, skip_in, m, 1).wait_send()

        @pl.when(jnp.logical_not(first))
        def _():
            to_pipe(2, ig_out, ga_in, m, -1).wait_send()

        @pl.when(odd)
        def _():
            to_pipe(3, gs_out, gs_in, m, -1).wait_send()

        return carry

    lax.fori_loop(0, MB, finish, 0)


def relay(dims, n_dp, clips, boxes, w_s, w_t, g_s, b_s, g_t, b_t, cotangent):
    cm, frames, height, width = dims
    rows = cm * frames * height * width
    d, m_ch = w_t.shape[1], w_s.shape[1]
    shape = jax.ShapeDtypeStruct
    vmem = pl.BlockSpec(memory_space=pltpu.VMEM)
    hbm = pl.BlockSpec(memory_space=pl.ANY)
    smem = pl.BlockSpec(memory_space=pltpu.SMEM)
    dma = pltpu.SemaphoreType.DMA
    narrow = pltpu.VMEM((MB, rows, d), bf16)
    wide = pltpu.VMEM((MB, rows, m_ch), bf16)
    return pl.pallas_call(
        functools.partial(relay_kernel, dims),
        out_shape=(
            shape((MB, rows, d), bf16),
            shape((MB, rows, d), bf16),
            shape((MB, rows, d), bf16),
            shape((MB, rows, m_ch), bf16),
            shape((MB, rows, m_ch), bf16),
            shape((MB, rows, d), bf16),
            shape((1, m_ch), f32),
            shape((1, m_ch), f32),
            shape((1, d), f32),
            shape((1, d), f32),
        ),
        in_specs=[hbm, smem, hbm, hbm, vmem, vmem, vmem, vmem, hbm],
        out_specs=[hbm] * 6 + [vmem] * 4,
        scratch_shapes=[
            pltpu.VMEM(w_s.shape, bf16),
            pltpu.VMEM(w_t.shape, bf16),
            pltpu.VMEM((9 * m_ch, d), bf16),
            pltpu.VMEM((3 * d, m_ch), bf16),
            pltpu.VMEM((rows, 9 * m_ch), bf16),
            narrow,
            narrow,
            narrow,
            narrow,
            narrow,
            narrow,
            narrow,
            wide,
            narrow,
            wide,
            pltpu.VMEM((MB, rows, m_ch), f32),
            pltpu.VMEM((MB, rows, d), f32),
            pltpu.VMEM((MB, rows, d), f32),
            pltpu.VMEM((rows, m_ch), f32),
            pltpu.VMEM((MB, rows, 128), f32),
            pltpu.VMEM((MB, 1, m_ch), f32),
            pltpu.VMEM((MB, 1, d), f32),
            pltpu.VMEM((MB, 1, 128), f32),
            pltpu.VMEM((MB, n_dp, 1, 2 * m_ch + 128), f32),
            pltpu.VMEM((MB, n_dp, 1, 2 * d + 128), f32),
            pltpu.VMEM((MB, n_dp, 1, 2 * d), f32),
            pltpu.VMEM((MB, n_dp, 1, 2 * m_ch), f32),
            dma((4, MB)),
            dma((4, MB)),
            dma((2,)),
            dma((MB,)),
            dma((6, MB)),
            dma((4, MB)),
            dma((4, MB)),
        ],
        compiler_params=pltpu.CompilerParams(
            collective_id=0, has_side_effects=True, vmem_limit_bytes=62 * 2**20
        ),
    )(clips, boxes, w_s, w_t, g_s, b_s, g_t, b_t, cotangent)


def spatial_columns(activity):
    height, breadth = (activity.shape[2], activity.shape[3])
    padded = jnp.pad(activity, ((0, 0), (0, 0), (1, 1), (1, 1), (0, 0)))
    pieces = [
        padded[:, :, row_off : row_off + height, col_off : col_off + breadth, :]
        for row_off in range(3)
        for col_off in range(3)
    ]
    return jnp.concatenate(pieces, axis=-1)


def temporal_columns(activity):
    frames = activity.shape[1]
    padded = jnp.pad(activity, ((0, 0), (1, 1), (0, 0), (0, 0), (0, 0)))
    return jnp.concatenate([padded[:, offset : offset + frames] for offset in range(3)], axis=-1)


def left_product(former, latter):
    return lax.dot_general(
        former, latter, (((0,), (0,)), ((), ())), preferred_element_type=jnp.float32
    )


def body(
    clips,
    boxes,
    spatial_w,
    temporal_w,
    spatial_gain,
    spatial_shift,
    temporal_gain,
    temporal_shift,
    cotangent,
):
    n_clips, frames, height, breadth, d = clips.shape
    cm = n_clips // MB
    width = (breadth // 8 + 1) * 8
    rows = cm * frames * height * width
    m_ch = spatial_w.shape[2]

    def padded(x):
        x = jnp.pad(x, ((0, 0), (0, 0), (0, 0), (0, width - breadth), (0, 0)))
        return x.reshape(MB, rows, d)

    act, grad, a_in, hidden, gu, gr, gain_s, shift_s, gain_t, shift_t = relay(
        (cm, frames, height, width),
        lax.axis_size("dp"),
        padded(clips),
        boxes,
        spatial_w[0],
        temporal_w[0],
        spatial_gain,
        spatial_shift,
        temporal_gain,
        temporal_shift,
        padded(cotangent),
    )

    def frames_of(x):
        return x.reshape(n_clips, frames, height, width, x.shape[-1])[:, :, :, :breadth]

    cells = n_clips * frames * height * breadth
    cols = spatial_columns(frames_of(a_in)).reshape(cells, -1)
    grad_s = left_product(cols, frames_of(gu).reshape(cells, -1))
    stacked = temporal_columns(frames_of(hidden)).reshape(cells, -1)
    grad_t = left_product(stacked, frames_of(gr).reshape(cells, -1))
    grad_s = lax.psum_scatter(grad_s, "dp", scatter_dimension=0, tiled=True)
    grad_t = lax.psum_scatter(grad_t, "dp", scatter_dimension=0, tiled=True)
    return (
        frames_of(act)[None],
        frames_of(grad)[None],
        grad_s[None],
        grad_t[None],
        gain_s,
        shift_s,
        gain_t,
        shift_t,
    )


def solution(mesh):
    clip_spec = P("dp", None, None, None, None)
    weight_spec = P("pipe", None, None)
    channel_spec = P("pipe", None)
    return jax.shard_map(
        body,
        mesh=mesh,
        in_specs=(
            clip_spec,
            P("dp", None),
            weight_spec,
            weight_spec,
            channel_spec,
            channel_spec,
            channel_spec,
            channel_spec,
            clip_spec,
        ),
        out_specs=(
            P("pipe", "dp", None, None, None, None),
            P("pipe", "dp", None, None, None, None),
            P("pipe", "dp", None),
            P("pipe", "dp", None),
            channel_spec,
            channel_spec,
            channel_spec,
            channel_spec,
        ),
        check_vma=False,
    )
```

time: 2280 us -> 549 us (0.24); the launches traced: 2250 us -> 549 us
  blocking collectives: 701 us -> 0 us
  local copies, waits for them, and re-layouts: 605 us -> 15 us
  other arithmetic: 329 us -> 0 us
  matrix products: 341 us -> 31 us
  Pallas kernels: 0 us -> 226 us
  waiting for transfers between devices: 198 us -> 263 us
  starting transfers between devices: 60.6 us -> 0.08 us
    psum x42 -> x0, blocking collectives: 701 us -> none  [the longest x14 292 us: norm_backward(): lax.psum((jnp.sum(slope_in, axis=0), jnp.sum(slope_in * normed, axis=0)),...]
    pallas_call x0 -> x1, Pallas kernels: none -> 226 us  [relay(): pl.pallas_call(functools.partial(relay_kernel, dims), out_shape=(shape((M...]
    dot_general x28 -> x0, matrix products: 176 us -> none  [the longest x14 91.4 us: right_product(): lax.dot_general(former, latter, (((1,), (1,)), ((), ())), preferred_eleme...]
    unnamed x639 -> x30, local copies, waits for them, and re-layouts: 157 us -> 8.03 us
    dot_general x14 -> x2, matrix products: 165 us -> 31 us  [left_product(): lax.dot_general(former, latter, (((0,), (0,)), ((), ())), preferred_eleme...]
    concatenate x77 -> x1, local copies, waits for them, and re-layouts: 119 us -> 0.24 us  [spatial_columns(): return jnp.concatenate(pieces, axis=-1)]
    reduce_sum x49 -> x0, other arithmetic: 94.6 us -> none  [the longest x14 37.3 us: norm_backward(): jnp.sum(slope_in * normed, axis=0)]
    reduce_scatter x2, waiting for transfers between devices: 179 us -> 263 us  [the longest x1 211 us: body(): grad_s = lax.psum_scatter(grad_s, 'dp', scatter_dimension=0, tiled=True)]
  transfers between devices with their start and end apart: 26 -> 2, of which waited for: 9 -> 2; matrix products, arithmetic and copies ran while one was open for 49% -> 4% of each run, Pallas kernels for 0% -> 0%
where the time goes in v1:
time: 549 us
  waiting for transfers between devices  263 us (48%)
  Pallas kernels  226 us (41%)
  matrix products  31 us (6%)
  local copies, waits for them, and re-layouts  15 us (3%)
  between operations  14.2 us (3%)
    pallas_call x1, Pallas kernels, relay(): pl.pallas_call(functools.partial(relay_kernel, dims), out_shape=(shape((M...  226 us
    reduce_scatter x1, waiting for transfers between devices, body(): grad_s = lax.psum_scatter(grad_s, 'dp', scatter_dimension=0, tiled=True)  211 us
    reduce_scatter x1, waiting for transfers between devices, body(): grad_t = lax.psum_scatter(grad_t, 'dp', scatter_dimension=0, tiled=True)  51 us
    dot_general x2, matrix products, left_product(): lax.dot_general(former, latter, (((0,), (0,)), ((), ())), preferred_eleme...  31 us
  transfers between devices with their start and end apart: 2, of which 2 were waited for; matrix products, arithmetic and copies ran while one was open for 4% of the time, Pallas kernels for 0%

profile of v1, /device:TPU:0, one launch (start us, length us, event | category | flops | bytes accessed | tf_op | source)
XLA Modules:
  0.0 548.9 jit_solution(6425623084524553756)
XLA Ops:
  7.2 0.0 reduce-scatter.5.cloned.1.call-start
  7.2 1.3 copy.25
  8.5 1.3 copy.26
  9.8 1.1 pad.15.clone
  10.9 1.1 pad.16.clone
  12.0 226.1 %shard_map.152 = (bf16[4,224,512]{2,1,0:T(8,128)(2,1)}, bf16[4,224,512]{2,1,0:T(8,128)(2,1)}, bf16[4,224,512]{2,1,0:T(8,128)(2,1)}, bf16[4,224,1152]{2,1,0:T(8,1...) custom-call(bf16[4,224,512]{2,1,0:T(8,128)(2,1)} %bitcast.39, ...), custom_call_target="tpu_custom_call" | custom-call | tf_op jit(solution)/shard_map/pallas_call | solution.py:538
  238.1 2.5 pad_slice_fusion.9
  240.6 0.0 copy-start
  240.6 11.5 %convolution_bitcast_fusion.1 = f32[3456,512]{1,0:T(8,128)} fusion(bf16[4,4,7,7,1152]{4,3,2,1,0:T(8,128)(2,1)S(1)} %get-tuple-element.29, bf16[4,4,7,7,1152]{4,3,2,1,0:T(8,128)(2,1)} %bitcast.43, bf16[4,4,7,7,1152]{4,3,2,1,0:T(8,128)(2,1)S(1)} %get-tuple-element.28, bf16[4,4,7,8,512]{4,3,2,1,0:T(8,128)(2,1)} %bitcast.48), kind=kOutput, calls=%fused_computation.1 | convolution fusion | flops 2790789120 | bytes 13414400 | tf_op jit(solution)/shard_map/dot_general | solution.py:614
  252.1 0.0 reduce-scatter.5.cloned.1.call-update
  252.1 0.0 reduce-scatter.3.cloned.1.call-start
  252.2 0.0 copy-done
  252.2 0.2 fusion.6
  252.4 0.2 fusion.7
  252.6 0.2 fusion.8
  252.9 0.3 fusion.9
  253.1 0.1 constant_dynamic-update-slice_fusion
  253.2 0.3 fusion.10
  253.5 0.2 fusion.11
  253.7 0.2 fusion.12
  253.9 0.2 fusion.13
  254.2 19.5 %convolution_bitcast_fusion = f32[4608,1152]{1,0:T(8,128)} fusion(bf16[4,4,7,7,4608]{4,3,2,1,0:T(8,128)(2,1)S(1)} %fusion.13, bf16[4,4,7,8,1152]{4,3,2,1,0:T(8,128)(2,1)S(1)} %bitcast.47), kind=kOutput, calls=%fused_computation | convolution fusion | flops 8323596288 | bytes 30523392 | tf_op jit(solution)/shard_map/dot_general | solution.py:614
  273.7 0.0 reduce-scatter.3.cloned.1.call-update
  273.7 1.1 copy-done.1
  274.8 0.3 copy-done.2
  275.1 2.1 copy_bitcast_fusion
  277.2 51.0 %reduce-scatter.5.cloned.1.call-done = f32[432,512]{1,0:T(8,128)} async-done(((f32[3456,512]{1,0:T(8,128)}), f32[432,512]{1,0:T(8,128)}) %reduce-scatter.5.cloned.1.call-update) | async-done | bytes 884752 | tf_op jit(solution)/shard_map/reduce_scatter | solution.py:663
  328.2 211.5 %reduce-scatter.3.cloned.1.call-done = f32[576,1152]{1,0:T(8,128)} async-done(((f32[4608,1152]{1,0:T(8,128)}), f32[576,1152]{1,0:T(8,128)}) %reduce-scatter.3.cloned.1.call-update) | async-done | bytes 2654224 | tf_op jit(solution)/shard_map/reduce_scatter | solution.py:662
  539.7 0.6 copy.41
  540.3 0.6 copy.42
  540.9 0.6 copy.43
  541.5 0.6 copy.44
  (12 shorter events, 0.0 us)
Async XLA Ops:
  7.2 321.0 %reduce-scatter.5.cloned.1.call-start = ((), (), s32[]{:S(2)}) async-start(), calls=%async_computation.3 | async-start | bytes 7962624 | tf_op jit(solution)/shard_map/reduce_scatter | solution.py:663
  240.6 11.6 %copy-start = (bf16[4,224,512]{2,1,0:T(8,128)(2,1)S(1)}, bf16[4,224,512]{2,1,0:T(8,128)(2,1)}, u32[]{:S(2)}) copy-start(bf16[4,224,512]{2,1,0:T(8,128)(2,1)} %get-tuple-element.20) | copy-start | bytes 2752516
  252.1 287.5 %reduce-scatter.3.cloned.1.call-start = ((), (), s32[]{:S(2)}) async-start(), calls=%async_computation.2 | async-start | bytes 23887872 | tf_op jit(solution)/shard_map/reduce_scatter | solution.py:662
  252.2 2.0 copy-start.7
  273.6 1.2 copy-start.1
  273.6 1.5 copy-start.2
  273.6 266.1 %copy-start.4 = (f32[1,1152]{1,0:T(1,128)S(1)}, f32[1,1152]{1,0:T(1,128)}, u32[]{:S(2)}) copy-start(f32[1,1152]{1,0:T(1,128)} %get-tuple-element.44) | copy-start | bytes 13828
  273.6 266.7 %copy-start.3 = (f32[1,1152]{1,0:T(1,128)S(1)}, f32[1,1152]{1,0:T(1,128)}, u32[]{:S(2)}) copy-start(f32[1,1152]{1,0:T(1,128)} %get-tuple-element.45) | copy-start | bytes 13828
  273.6 267.2 %copy-start.6 = (f32[1,512]{1,0:T(1,128)S(1)}, f32[1,512]{1,0:T(1,128)}, u32[]{:S(2)}) copy-start(f32[1,512]{1,0:T(1,128)} %get-tuple-element.46) | copy-start | bytes 6148
  273.6 267.8 %copy-start.5 = (f32[1,512]{1,0:T(1,128)S(1)}, f32[1,512]{1,0:T(1,128)}, u32[]{:S(2)}) copy-start(f32[1,512]{1,0:T(1,128)} %get-tuple-element.47) | copy-start | bytes 6148
Sparse Core Ops, SparseCore 0:
  252.3 75.8 reduce-scatter.4
  331.1 208.5 reduce-scatter.2

commit v2 on v1

--- a/solution.py
+++ b/solution.py
@@ -86,6 +86,8 @@
     store_sem,
     pipe_send,
     pipe_recv,
+    twin_send,
+    twin_recv,
 ):
     cm, frames, height, width = dims
     rows = cm * frames * height * width
@@ -195,6 +197,23 @@
     def store(kind, src, dst, m):
         return pltpu.make_async_copy(src.at[m], dst.at[m], store_sem.at[kind, m])
 
+    def keep_operand(kind, src, dst, m):
+        return pltpu.make_async_copy(src.at[m], dst.at[0, m], store_sem.at[kind, m])
+
+    def twin_operand(kind, src, dst, m):
+        return pltpu.make_async_remote_copy(
+            src_ref=src.at[m],
+            dst_ref=dst.at[1, m],
+            send_sem=twin_send.at[kind - 2, m],
+            recv_sem=twin_recv.at[kind - 2, m],
+            device_id={"dp": me + 1 - 2 * lax.rem(me, 2)},
+            device_id_type=MESH,
+        )
+
+    def share_operand(kind, src, dst, m):
+        keep_operand(kind, src, dst, m).start()
+        twin_operand(kind, src, dst, m).start()
+
     def shift_space(x, dh, dw):
         if dw:
             x = pltpu.roll(x, (-dw) % rows, 0)
@@ -255,7 +274,7 @@
         def _():
             to_pipe(1, a_in, skip_in, m, 1).start()
 
-        store(2, a_in, o_in, m).start()
+        share_operand(2, a_in, o_in, m)
 
         def column(i, s):
             x = a_in[m, :, s].astype(f32)
@@ -294,7 +313,7 @@
                 cols[:, at] = shift_time(value, dt).astype(bf16)
 
         lane_chunks(m_ch, column)
-        store(3, hidden, o_hidden, m).start()
+        share_operand(3, hidden, o_hidden, m)
 
         @pl.when(m == 0)
         def _():
@@ -377,7 +396,7 @@
                 cols[:, at] = shift_time(value, -dt).astype(bf16)
 
         lane_chunks(d, column)
-        store(4, gr, o_gr, m).start()
+        share_operand(4, gr, o_gr, m)
         gq[...] = jnp.dot(cols[:, : 3 * d], w_t_back[...], preferred_element_type=f32)
 
         def sums(i, s):
@@ -412,7 +431,7 @@
                     cols[:, at] = shift_rows(y, -dh).astype(bf16)
 
         lane_chunks(m_ch, column)
-        store(5, gu, o_gu, m).start()
+        share_operand(5, gu, o_gu, m)
 
         @pl.when(even_inner)
         def _():
@@ -491,17 +510,16 @@
     lax.fori_loop(0, 2 * MB, step, 0)
 
     def finish(m, carry):
-        for kind, (src, dst) in enumerate(
-            (
-                (a_out, o_act),
-                (ig_out, o_grad),
-                (a_in, o_in),
-                (hidden, o_hidden),
-                (gr, o_gr),
-                (gu, o_gu),
-            )
+        store(0, a_out, o_act, m).wait()
+        store(1, ig_out, o_grad, m).wait()
+        for kind, src, dst in (
+            (2, a_in, o_in),
+            (3, hidden, o_hidden),
+            (4, gr, o_gr),
+            (5, gu, o_gu),
         ):
-            store(kind, src, dst, m).wait()
+            keep_operand(kind, src, dst, m).wait()
+            twin_operand(kind, src, dst, m).wait()
 
         @pl.when(jnp.logical_not(last))
         def _():
@@ -540,10 +558,10 @@
         out_shape=(
             shape((MB, rows, d), bf16),
             shape((MB, rows, d), bf16),
-            shape((MB, rows, d), bf16),
-            shape((MB, rows, m_ch), bf16),
-            shape((MB, rows, m_ch), bf16),
-            shape((MB, rows, d), bf16),
+            shape((2, MB, rows, d), bf16),
+            shape((2, MB, rows, m_ch), bf16),
+            shape((2, MB, rows, m_ch), bf16),
+            shape((2, MB, rows, d), bf16),
             shape((1, m_ch), f32),
             shape((1, m_ch), f32),
             shape((1, d), f32),
@@ -586,11 +604,304 @@
             dma((6, MB)),
             dma((4, MB)),
             dma((4, MB)),
+            dma((4, MB)),
+            dma((4, MB)),
         ],
         compiler_params=pltpu.CompilerParams(
             collective_id=0, has_side_effects=True, vmem_limit_bytes=62 * 2**20
         ),
     )(clips, boxes, w_s, w_t, g_s, b_s, g_t, b_t, cotangent)
+
+
+def send_order(n, z, q):
+    table = []
+    for here in range(n):
+        sign = 1 if here < n / 2 else -1
+        table.append(sorted(range(n), key=lambda to: (-abs(to - here), -sign * to)))
+    dest = 0
+    for here in range(n):
+        for at in range(n):
+            dest = dest + jnp.where((z == here) & (q == at), table[here][at], 0)
+    return dest
+
+
+def gradient_kernel(
+    dims,
+    a_hbm,
+    v_hbm,
+    gu_hbm,
+    gr_hbm,
+    o_s,
+    o_t,
+    a_raw,
+    v_raw,
+    a_pad,
+    v_pad,
+    gu,
+    gr,
+    edge,
+    window,
+    acc_s,
+    acc_t,
+    got_s,
+    got_t,
+    out_s,
+    out_t,
+    load_sem,
+    send_sem,
+    recv_sem,
+):
+    frames, height, width = dims
+    n_clips, rows, d = a_hbm.shape
+    m_ch = v_hbm.shape[2]
+    step = height * width
+    me = lax.axis_index("dp")
+    n = lax.axis_size("dp") // 2
+    z = lax.div(me, 2)
+    core = lax.rem(me, 2)
+    rows_s, rows_t = o_s.shape[0], o_t.shape[0]
+    piece = got_s.shape[3]
+    n_pieces = m_ch // piece
+    span = acc_s.shape[0]
+    lead = a_pad.shape[2] - rows - 8
+
+    load_gu = [
+        pltpu.make_async_copy(gu_hbm.at[i], gu.at[pl.ds(i * rows, rows)], load_sem.at[2, i])
+        for i in range(n_clips)
+    ]
+    load_gr = [
+        pltpu.make_async_copy(gr_hbm.at[i], gr.at[pl.ds(i * rows, rows)], load_sem.at[3, i])
+        for i in range(n_clips)
+    ]
+    for copy in load_gu + load_gr:
+        copy.start()
+
+    def load_a(i):
+        return pltpu.make_async_copy(a_hbm.at[i], a_raw.at[lax.rem(i, 2)], load_sem.at[0, i])
+
+    def load_v(i):
+        return pltpu.make_async_copy(v_hbm.at[i], v_raw.at[lax.rem(i, 2)], load_sem.at[1, i])
+
+    load_a(0).start()
+    load_v(0).start()
+
+    barrier = pltpu.get_barrier_semaphore()
+
+    @pl.when(z > 0)
+    def _():
+        pl.semaphore_signal(barrier, 1, device_id={"dp": me - 2}, device_id_type=MESH)
+
+    @pl.when(z < n - 1)
+    def _():
+        pl.semaphore_signal(barrier, 1, device_id={"dp": me + 2}, device_id_type=MESH)
+
+    h = lax.broadcasted_iota(jnp.int32, (frames, height, width, 128), 1)
+    for dh in (-1, 0, 1):
+        inside = (h + dh >= 0) & (h + dh < height)
+        edge[dh + 1] = jnp.where(inside, 1.0, 0.0).astype(f32).reshape(rows, 128)
+
+    def prepare(i, carry):
+        load_a(i).wait()
+        load_v(i).wait()
+
+        @pl.when(i + 1 < n_clips)
+        def _():
+            load_a(i + 1).start()
+            load_v(i + 1).start()
+
+        slot = lax.rem(i, 2)
+        for c in range(0, d, 128):
+            x = a_raw[slot, :, c : c + 128].astype(f32)
+            for dw in (-1, 0, 1):
+                y = pltpu.roll(x, (-dw) % rows, 0) if dw else x
+                a_pad[i, dw + 1, lead : lead + rows, c : c + 128] = y
+                a_pad[i, dw + 1, lead - 8 : lead, c : c + 128] = jnp.zeros((8, 128), f32)
+                a_pad[i, dw + 1, lead + rows :, c : c + 128] = jnp.zeros((8, 128), f32)
+        zero = jnp.zeros((step, 128), f32)
+        for c in range(0, m_ch, 128):
+            v_pad[i, :step, c : c + 128] = zero
+            v_pad[i, step : step + rows, c : c + 128] = v_raw[slot, :, c : c + 128].astype(f32)
+            v_pad[i, step + rows :, c : c + 128] = zero
+        return carry
+
+    lax.fori_loop(0, n_clips, prepare, 0)
+    for copy in load_gu + load_gr:
+        copy.wait()
+    pl.semaphore_wait(barrier, 2 - jnp.where(z == 0, 1, 0) - jnp.where(z == n - 1, 1, 0))
+
+    def transfer(src, dst, dest, p):
+        right = dest > z
+        slot = dest + jnp.where(right, 1, 0)
+        return pltpu.make_async_remote_copy(
+            src_ref=src,
+            dst_ref=dst(slot),
+            send_sem=send_sem.at[dest, p],
+            recv_sem=recv_sem.at[slot, p],
+            device_id={"dp": me + jnp.where(right, 2, -2)},
+            device_id_type=MESH,
+        )
+
+    def settle(dest, acc, start, size, got, out, final, p):
+        at = pl.ds(pl.multiple_of(start, 8), size)
+        from_left = (z > 0) & (dest >= z)
+        from_right = (z < n - 1) & (dest <= z)
+
+        @pl.when(from_left)
+        def _():
+            ref = got(dest + 1)
+            pltpu.make_async_copy(ref, ref, recv_sem.at[dest + 1, p]).wait()
+            acc[at, :] += ref[...].astype(f32)
+
+        @pl.when(from_right)
+        def _():
+            ref = got(dest)
+            pltpu.make_async_copy(ref, ref, recv_sem.at[dest, p]).wait()
+            acc[at, :] += ref[...].astype(f32)
+
+        @pl.when(dest == z)
+        def _():
+            final[...] = acc[at, :]
+
+        @pl.when(dest != z)
+        def _():
+            ref = out(dest)
+            ref[...] = acc[at, :].astype(bf16)
+            transfer(ref, got, dest, p).start()
+
+    def place(row0):
+        low = lax.div(row0, 128)
+        return low, row0 - low * 128
+
+    def job(q, carry):
+        dest = send_order(n, z, q)
+        owner = 2 * dest + core
+
+        low, start = place(owner * rows_s)
+
+        def fill_space(i, c):
+            for j in range(span // 128):
+                chunk = jnp.minimum(low + j, 9 * d // 128 - 1)
+                tap = lax.div(chunk, d // 128)
+                lane = chunk - tap * (d // 128)
+                dh = lax.div(tap, 3)
+                dw = tap - 3 * dh
+                x = a_pad[
+                    i,
+                    dw,
+                    pl.ds(pl.multiple_of(lead - 8 + 8 * dh, 8), rows),
+                    pl.ds(pl.multiple_of(lane * 128, 128), 128),
+                ]
+                window[pl.ds(pl.multiple_of(i * rows, 16), rows), j * 128 : (j + 1) * 128] = (
+                    x * edge[dh]
+                ).astype(bf16)
+            return c
+
+        lax.fori_loop(0, n_clips, fill_space, 0)
+
+        def space(p, c):
+            s = pl.ds(pl.multiple_of(p * piece, 128), piece)
+            acc_s[...] = lax.dot_general(
+                window[...], gu[:, s], (((0,), (0,)), ((), ())), preferred_element_type=f32
+            )
+            settle(
+                dest,
+                acc_s,
+                start,
+                rows_s,
+                lambda slot: got_s.at[slot, p],
+                lambda to: out_s.at[to, p],
+                o_s.at[:, s],
+                p,
+            )
+            return c
+
+        lax.fori_loop(0, n_pieces, space, 0)
+
+        low_t, start_t = place(owner * rows_t)
+
+        def fill_time(i, c):
+            for j in range(span // 128):
+                chunk = jnp.minimum(low_t + j, 3 * m_ch // 128 - 1)
+                tap = lax.div(chunk, m_ch // 128)
+                lane = chunk - tap * (m_ch // 128)
+                x = v_pad[
+                    i,
+                    pl.ds(pl.multiple_of(tap * step, 8), rows),
+                    pl.ds(pl.multiple_of(lane * 128, 128), 128),
+                ]
+                window[pl.ds(pl.multiple_of(i * rows, 16), rows), j * 128 : (j + 1) * 128] = (
+                    x.astype(bf16)
+                )
+            return c
+
+        lax.fori_loop(0, n_clips, fill_time, 0)
+        acc_t[...] = lax.dot_general(
+            window[...], gr[...], (((0,), (0,)), ((), ())), preferred_element_type=f32
+        )
+        settle(
+            dest,
+            acc_t,
+            start_t,
+            rows_t,
+            lambda slot: got_t.at[slot],
+            lambda to: out_t.at[to],
+            o_t,
+            n_pieces,
+        )
+        return carry
+
+    lax.fori_loop(0, n, job, 0)
+
+    def finish(q, carry):
+        dest = send_order(n, z, q)
+        for p in range(n_pieces):
+            transfer(out_s.at[dest, p], lambda slot: got_s.at[slot, p], dest, p).wait_send()
+        transfer(out_t.at[dest], lambda slot: got_t.at[slot], dest, n_pieces).wait_send()
+        return carry
+
+    lax.fori_loop(0, n - 1, finish, 0)
+
+
+def gradients(dims, n_dp, a, v, gu, gr):
+    n_clips, rows, d = a.shape
+    m_ch = v.shape[2]
+    frames, height, width = dims
+    step = height * width
+    rows_s, rows_t = 9 * d // n_dp, 3 * m_ch // n_dp
+    n = n_dp // 2
+    piece = 384
+    n_pieces = m_ch // piece
+    span = 640
+    shape = jax.ShapeDtypeStruct
+    dma = pltpu.SemaphoreType.DMA
+    return pl.pallas_call(
+        functools.partial(gradient_kernel, dims),
+        out_shape=(shape((rows_s, m_ch), f32), shape((rows_t, d), f32)),
+        in_specs=[pl.BlockSpec(memory_space=pl.ANY)] * 4,
+        out_specs=[pl.BlockSpec(memory_space=pltpu.VMEM)] * 2,
+        scratch_shapes=[
+            pltpu.VMEM((2, rows, d), bf16),
+            pltpu.VMEM((2, rows, m_ch), bf16),
+            pltpu.VMEM((n_clips, 3, rows + 16, d), f32),
+            pltpu.VMEM((n_clips, rows + 2 * step, m_ch), f32),
+            pltpu.VMEM((n_clips * rows, m_ch), bf16),
+            pltpu.VMEM((n_clips * rows, d), bf16),
+            pltpu.VMEM((3, rows, 128), f32),
+            pltpu.VMEM((n_clips * rows, span), bf16),
+            pltpu.VMEM((span, piece), f32),
+            pltpu.VMEM((span, d), f32),
+            pltpu.VMEM((n + 1, n_pieces, rows_s, piece), bf16),
+            pltpu.VMEM((n + 1, rows_t, d), bf16),
+            pltpu.VMEM((n, n_pieces, rows_s, piece), bf16),
+            pltpu.VMEM((n, rows_t, d), bf16),
+            dma((4, n_clips)),
+            dma((n, n_pieces + 1)),
+            dma((n + 1, n_pieces + 1)),
+        ],
+        compiler_params=pltpu.CompilerParams(
+            collective_id=1, has_side_effects=True, vmem_limit_bytes=62 * 2**20
+        ),
+    )(a, v, gu, gr)
 
 
 def spatial_columns(activity):
@@ -654,13 +965,23 @@
     def frames_of(x):
         return x.reshape(n_clips, frames, height, width, x.shape[-1])[:, :, :, :breadth]
 
-    cells = n_clips * frames * height * breadth
-    cols = spatial_columns(frames_of(a_in)).reshape(cells, -1)
-    grad_s = left_product(cols, frames_of(gu).reshape(cells, -1))
-    stacked = temporal_columns(frames_of(hidden)).reshape(cells, -1)
-    grad_t = left_product(stacked, frames_of(gr).reshape(cells, -1))
-    grad_s = lax.psum_scatter(grad_s, "dp", scatter_dimension=0, tiled=True)
-    grad_t = lax.psum_scatter(grad_t, "dp", scatter_dimension=0, tiled=True)
+    n_dp = lax.axis_size("dp")
+    rows_s, rows_t = 9 * d // n_dp, 3 * m_ch // n_dp
+    if rows_s % 64 == 0 and rows_t % 16 == 0 and rows_s <= 576 and rows_t <= 528 and n_dp <= 8:
+        clip_rows = frames * height * width
+        grad_s, grad_t = gradients(
+            (frames, height, width),
+            n_dp,
+            *[x.reshape(2 * n_clips, clip_rows, x.shape[-1]) for x in (a_in, hidden, gu, gr)],
+        )
+    else:
+        cells = n_clips * frames * height * breadth
+        cols = spatial_columns(frames_of(a_in[0])).reshape(cells, -1)
+        grad_s = left_product(cols, frames_of(gu[0]).reshape(cells, -1))
+        stacked = temporal_columns(frames_of(hidden[0])).reshape(cells, -1)
+        grad_t = left_product(stacked, frames_of(gr[0]).reshape(cells, -1))
+        grad_s = lax.psum_scatter(grad_s, "dp", scatter_dimension=0, tiled=True)
+        grad_t = lax.psum_scatter(grad_t, "dp", scatter_dimension=0, tiled=True)
     return (
         frames_of(act)[None],
         frames_of(grad)[None],

time: 549 us -> 378 us (0.69)
  waiting for transfers between devices: 263 us -> 0 us
  Pallas kernels: 226 us -> 363 us
  matrix products: 31 us -> 0 us
  between operations: 14.2 us -> 0.71 us
    reduce_scatter x2 -> x0, waiting for transfers between devices: 263 us -> none  [the longest x1 211 us: body(): grad_s = lax.psum_scatter(grad_s, 'dp', scatter_dimension=0, tiled=True)]
    pallas_call x0 -> x1, Pallas kernels: none -> 136 us  [gradients(): pl.pallas_call(functools.partial(gradient_kernel, dims), out_shape=(shape...]
    dot_general x2 -> x0, matrix products: 31 us -> none  [left_product(): lax.dot_general(former, latter, (((0,), (0,)), ((), ())), preferred_eleme...]
  transfers between devices with their start and end apart: 2 -> 0, of which waited for: 2 -> 0; matrix products, arithmetic and copies ran while one was open for 4% -> 0% of each run, Pallas kernels for 0% -> 0%
where the time goes in v2:
time: 378 us
  Pallas kernels  363 us (96%)
  local copies, waits for them, and re-layouts  14.1 us (4%)
    pallas_call x1, Pallas kernels, relay(): pl.pallas_call(functools.partial(relay_kernel, dims), out_shape=(shape((M...  227 us
    pallas_call x1, Pallas kernels, gradients(): pl.pallas_call(functools.partial(gradient_kernel, dims), out_shape=(shape...  136 us
    unnamed x20, local copies, waits for them, and re-layouts  8.32 us

profile of v2, /device:TPU:0, one launch (start us, length us, event | category | flops | bytes accessed | tf_op | source)
XLA Modules:
  0.0 377.7 jit_solution(8612490605443832280)
XLA Ops:
  0.6 0.0 copy-start.1
  0.6 1.4 copy.23
  2.0 1.1 pad.7.clone
  3.1 0.0 copy-done.1
  3.1 0.2 copy.24
  3.3 1.1 pad.8.clone
  4.4 226.9 %shard_map.152 = (bf16[4,224,512]{2,1,0:T(8,128)(2,1)}, bf16[4,224,512]{2,1,0:T(8,128)(2,1)}, bf16[2,4,224,512]{3,2,1,0:T(8,128)(2,1)}, bf16[2,4,224,1152]{3,2,1...) custom-call(bf16[4,224,512]{2,1,0:T(8,128)(2,1)} %bitcast.21, ...), custom_call_target="tpu_custom_call" | custom-call | tf_op jit(solution)/shard_map/pallas_call | solution.py:556
  231.3 3.5 copy_bitcast_fusion
  234.8 136.1 %shard_map.153 = (f32[576,1152]{1,0:T(8,128)}, f32[432,512]{1,0:T(8,128)}) custom-call(bf16[8,224,512]{2,1,0:T(8,128)(2,1)} %bitcast.25, bf16[8,224,1152]{2,1,0:T(8,128)(2,1)} %bitcast.19, bf16[8,224,1152]{2,1,0:T(8,128)(2,1)} %bitcast.20, bf16[8,224,512]{2,1,0:T(8,128)(2,1)} %bitcast.26), custom_call_target="tpu_custom_call" | custom-call | tf_op jit(solution)/shard_map/pallas_call | solution.py:877
  370.9 0.0 copy-start
  370.9 0.0 copy-start.3
  370.9 0.0 copy-start.2
  370.9 0.0 copy-start.5
  370.9 0.0 copy-start.4
  370.9 3.5 copy.33
  374.4 0.0 copy-done
  374.4 0.9 copy.34
  375.4 0.0 copy-done.3
  375.4 0.6 copy.35
  375.9 0.0 copy-done.2
  376.0 0.6 copy.36
  376.5 0.0 copy-done.5
  376.5 0.6 copy.37
  377.1 0.0 copy-done.4
  377.1 0.6 copy.38
Async XLA Ops:
  0.6 2.5 copy-start.1
  370.9 3.5 copy-start
  370.9 4.5 %copy-start.3 = (f32[1,1152]{1,0:T(1,128)S(1)}, f32[1,1152]{1,0:T(1,128)}, u32[]{:S(2)}) copy-start(f32[1,1152]{1,0:T(1,128)} %get-tuple-element.46) | copy-start | bytes 13828
  370.9 5.0 %copy-start.2 = (f32[1,1152]{1,0:T(1,128)S(1)}, f32[1,1152]{1,0:T(1,128)}, u32[]{:S(2)}) copy-start(f32[1,1152]{1,0:T(1,128)} %get-tuple-element.47) | copy-start | bytes 13828
  370.9 5.6 %copy-start.5 = (f32[1,512]{1,0:T(1,128)S(1)}, f32[1,512]{1,0:T(1,128)}, u32[]{:S(2)}) copy-start(f32[1,512]{1,0:T(1,128)} %get-tuple-element.48) | copy-start | bytes 6148
  370.9 6.2 %copy-start.4 = (f32[1,512]{1,0:T(1,128)S(1)}, f32[1,512]{1,0:T(1,128)}, u32[]{:S(2)}) copy-start(f32[1,512]{1,0:T(1,128)} %get-tuple-element.49) | copy-start | bytes 6148

commit v3 on v2

--- a/solution.py
+++ b/solution.py
@@ -103,10 +103,13 @@
     even_inner = jnp.logical_and(jnp.logical_not(odd), jnp.logical_not(last))
     skipping = odd.astype(f32)
 
-    load_ws = pltpu.make_async_copy(w_s_hbm, w_s, w_sem.at[0])
-    load_wt = pltpu.make_async_copy(w_t_hbm, w_t, w_sem.at[1])
-    load_ws.start()
-    load_wt.start()
+    def load_ws(part, tap):
+        half = d // 2
+        src = w_s_hbm.at[pl.ds(tap * d + part * half, half)]
+        dst = w_s.at[pl.ds((part * 9 + tap) * half, half)]
+        return pltpu.make_async_copy(src, dst, w_sem.at[part * 9 + tap])
+
+    load_wt = pltpu.make_async_copy(w_t_hbm, w_t, w_sem.at[18])
 
     def load_clip(m):
         return pltpu.make_async_copy(clips.at[m], a_in.at[m], load_sem.at[m])
@@ -118,6 +121,11 @@
     def _():
         for m in range(MB):
             load_clip(m).start()
+
+    for part in range(2):
+        for tap in range(9):
+            load_ws(part, tap).start()
+    load_wt.start()
 
     @pl.when(last)
     def _():
@@ -194,6 +202,19 @@
             device_id_type=MESH,
         )
 
+    half = d // 2
+
+    def half_to_pipe(kind, part, src, dst, m, step):
+        s = pl.ds(part * half, half)
+        return pltpu.make_async_remote_copy(
+            src_ref=src.at[m, :, s],
+            dst_ref=dst.at[m, :, s],
+            send_sem=pipe_send.at[kind + part, m],
+            recv_sem=pipe_recv.at[kind + part, m],
+            device_id={"pipe": section + step},
+            device_id_type=MESH,
+        )
+
     def store(kind, src, dst, m):
         return pltpu.make_async_copy(src.at[m], dst.at[m], store_sem.at[kind, m])
 
@@ -266,35 +287,46 @@
         def _():
             load_clip(m).wait()
 
-        @pl.when(jnp.logical_not(first))
-        def _():
-            to_pipe(0, a_out, a_in, m, 1).wait_recv()
+        for part in range(2):
+
+            @pl.when(jnp.logical_not(first))
+            def _():
+                half_to_pipe(2, part, a_out, a_in, m, 1).wait_recv()
+
+            def column(i, s):
+                s = pl.ds(pl.multiple_of(part * half + i * 128, 128), 128)
+                x = a_in[m, :, s].astype(f32)
+                for dw in (-1, 0, 1):
+                    y = shift_space(x, 0, dw)
+                    for dh in (-1, 0, 1):
+                        tap = (dh + 1) * 3 + dw + 1
+                        at = part * 9 * half + tap * half + i * 128
+                        cols[:, pl.ds(pl.multiple_of(at, 128), 128)] = shift_rows(y, dh).astype(
+                            bf16
+                        )
+
+            lane_chunks(half, column)
+
+            @pl.when((m == 0) & first)
+            def _():
+                for tap in range(9):
+                    load_ws(part, tap).wait()
+
+            k = slice(part * 9 * half, (part + 1) * 9 * half)
+            value = jnp.dot(cols[:, k], w_s[k, :], preferred_element_type=f32)
+            if part == 0:
+                uh[m] = value
+            else:
+                uh[m] += value
 
         @pl.when(even_inner)
         def _():
-            to_pipe(1, a_in, skip_in, m, 1).start()
-
-        share_operand(2, a_in, o_in, m)
-
-        def column(i, s):
-            x = a_in[m, :, s].astype(f32)
-            for dw in (-1, 0, 1):
-                y = shift_space(x, 0, dw)
-                for dh in (-1, 0, 1):
-                    tap = (dh + 1) * 3 + dw + 1
-                    at = pl.ds(pl.multiple_of(tap * d + i * 128, 128), 128)
-                    cols[:, at] = shift_rows(y, dh).astype(bf16)
-
-        lane_chunks(d, column)
-
-        @pl.when(m == 0)
-        def _():
-            load_ws.wait()
-
-        uh[m] = jnp.dot(cols[:, : 9 * d], w_s[...], preferred_element_type=f32)
+            to_pipe(0, a_in, skip_in, m, 1).start()
+
         x_s[m, me, :, 2 * m_ch :] = cnt[m]
         lane_chunks(m_ch, lambda i, s: local_sums(m, uh[m, :, s], x_s, i, m_ch))
         share(0, x_s, m)
+        share_operand(2, a_in, o_in, m)
 
     def forward_temporal(m):
         shared(0, x_s, m)
@@ -315,7 +347,7 @@
         lane_chunks(m_ch, column)
         share_operand(3, hidden, o_hidden, m)
 
-        @pl.when(m == 0)
+        @pl.when((m == 0) & first)
         def _():
             load_wt.wait()
 
@@ -332,7 +364,7 @@
 
         @pl.when(odd)
         def _():
-            to_pipe(1, a_in, skip_in, m, 1).wait_recv()
+            to_pipe(0, a_in, skip_in, m, 1).wait_recv()
 
         def column(i, s):
             n, mean, rstd = merged(m, x_t, i, d)
@@ -345,7 +377,8 @@
 
         @pl.when(jnp.logical_not(last))
         def _():
-            to_pipe(0, a_out, a_in, m, 1).start()
+            for part in range(2):
+                half_to_pipe(2, part, a_out, a_in, m, 1).start()
 
         store(0, a_out, o_act, m).start()
 
@@ -356,12 +389,13 @@
 
         @pl.when(jnp.logical_not(last))
         def _():
-            to_pipe(2, ig_out, ga_in, m, -1).wait_recv()
+            for part in range(2):
+                half_to_pipe(4, part, ig_out, ga_in, m, -1).wait_recv()
 
         def column(i, s):
             normed = rh[m, :, s]
             slope = ga_in[m, :, s].astype(f32) * keep[m] * silu_slope(preact(m, s, normed))
-            gp[m, :, s] = slope
+            gp[lax.rem(m, 2), :, s] = slope
             gs_out[m, :, s] = slope.astype(bf16)
             x_bt[m, me, :, s] = jnp.sum(slope, axis=0, keepdims=True)
             at = pl.ds(pl.multiple_of(d + i * 128, 128), 128)
@@ -372,7 +406,7 @@
 
         @pl.when(odd)
         def _():
-            to_pipe(3, gs_out, gs_in, m, -1).start()
+            to_pipe(1, gs_out, gs_in, m, -1).start()
 
     def totals(buf, m, s, i, channels):
         at = pl.ds(pl.multiple_of(channels + i * 128, 128), 128)
@@ -387,7 +421,7 @@
             o_shift_t[:, s] += shift_sum
             o_gain_t[:, s] += gain_sum
             scale = g_t[:, s] * fact_t[m, :, s]
-            value = keep[m] * scale * (gp[m, :, s] - (shift_sum + rh[m, :, s] * gain_sum) / n)
+            value = keep[m] * scale * (gp[lax.rem(m, 2), :, s] - (shift_sum + rh[m, :, s] * gain_sum) / n)
             value = value.astype(bf16)
             gr[m, :, s] = value
             value = value.astype(f32)
@@ -397,12 +431,12 @@
 
         lane_chunks(d, column)
         share_operand(4, gr, o_gr, m)
-        gq[...] = jnp.dot(cols[:, : 3 * d], w_t_back[...], preferred_element_type=f32)
+        gq[lax.rem(m, 2)] = jnp.dot(cols[:, : 3 * d], w_t_back[...], preferred_element_type=f32)
 
         def sums(i, s):
             normed = uh[m, :, s]
-            slope = keep[m] * gq[:, s] * silu_slope(g_s[:, s] * normed + b_s[:, s])
-            gq[:, s] = slope
+            slope = keep[m] * gq[lax.rem(m, 2), :, s] * silu_slope(g_s[:, s] * normed + b_s[:, s])
+            gq[lax.rem(m, 2), :, s] = slope
             x_bs[m, me, :, s] = jnp.sum(slope, axis=0, keepdims=True)
             at = pl.ds(pl.multiple_of(m_ch + i * 128, 128), 128)
             x_bs[m, me, :, at] = jnp.sum(slope * normed, axis=0, keepdims=True)
@@ -419,7 +453,7 @@
             o_shift_s[:, s] += shift_sum
             o_gain_s[:, s] += gain_sum
             scale = g_s[:, s] * fact_s[m, :, s]
-            value = keep[m] * scale * (gq[:, s] - (shift_sum + uh[m, :, s] * gain_sum) / n)
+            value = keep[m] * scale * (gq[lax.rem(m, 2), :, s] - (shift_sum + uh[m, :, s] * gain_sum) / n)
             value = value.astype(bf16)
             gu[m, :, s] = value
             value = value.astype(f32)
@@ -435,26 +469,33 @@
 
         @pl.when(even_inner)
         def _():
-            to_pipe(3, gs_out, gs_in, m, -1).wait_recv()
+            to_pipe(1, gs_out, gs_in, m, -1).wait_recv()
 
         with_skip = even_inner.astype(f32)
-        half = d // 2
         for part in range(2):
             s = slice(part * half, (part + 1) * half)
             value = jnp.dot(cols[...], w_s_back[:, s], preferred_element_type=f32)
             ig_out[m, :, s] = (value + with_skip * gs_in[m, :, s].astype(f32)).astype(bf16)
 
+            @pl.when(jnp.logical_not(first))
+            def _():
+                half_to_pipe(4, part, ig_out, ga_in, m, -1).start()
+
+        store(1, ig_out, o_grad, m).start()
+
+    def turn_weights():
         @pl.when(jnp.logical_not(first))
         def _():
-            to_pipe(2, ig_out, ga_in, m, -1).start()
-
-        store(1, ig_out, o_grad, m).start()
-
-    def turn_weights():
+            for part in range(2):
+                for tap in range(9):
+                    load_ws(part, tap).wait()
+            load_wt.wait()
+
         def spatial(tap, carry):
-            src = pl.ds(pl.multiple_of(tap * d, 128), d)
             dst = pl.ds(pl.multiple_of(tap * m_ch, 128), m_ch)
-            w_s_back[dst, :] = w_s[src, :].T
+            for part in range(2):
+                src = pl.ds(pl.multiple_of((part * 9 + tap) * half, 128), half)
+                w_s_back[dst, part * half : (part + 1) * half] = w_s[src, :].T
             return carry
 
         lax.fori_loop(0, 9, spatial, 0)
@@ -467,47 +508,37 @@
 
         lax.fori_loop(0, 3, temporal, 0)
 
-    wait_back = jnp.where(last, 1, MB)
+    pairs = MB // 2
+    wait_back = jnp.where(last, 1, pairs)
 
     def step(s, carry):
-        mf = s
-        mb = s - wait_back
-        do_f = mf < MB
-        do_b = jnp.logical_and(mb >= 0, mb < MB)
-        mf = jnp.minimum(mf, MB - 1)
-        mb = jnp.clip(mb, 0, MB - 1)
-
-        @pl.when(do_f)
-        def _():
-            forward_spatial(mf)
-
-        @pl.when(s == wait_back)
+        do_f = s < pairs
+        do_b = jnp.logical_and(s >= wait_back, s < wait_back + pairs)
+        mf = 2 * jnp.minimum(s, pairs - 1)
+        mb = 2 * jnp.clip(s - wait_back, 0, pairs - 1)
+
+        @pl.when(s == jnp.where(first, wait_back, 0))
         def _():
             turn_weights()
 
-        @pl.when(do_b)
-        def _():
-            backward_in(mb)
-
-        @pl.when(do_f)
-        def _():
-            forward_temporal(mf)
-
-        @pl.when(do_b)
-        def _():
-            backward_temporal(mb)
-
-        @pl.when(do_f)
-        def _():
-            forward_out(mf)
-
-        @pl.when(do_b)
-        def _():
-            backward_spatial(mb)
-
+        def both(when, phase, m):
+            @pl.when(when)
+            def _():
+                def one(j, c):
+                    phase(m + j)
+                    return c
+
+                lax.fori_loop(0, 2, one, 0)
+
+        both(do_b, backward_in, mb)
+        both(do_f, forward_spatial, mf)
+        both(do_b, backward_temporal, mb)
+        both(do_f, forward_temporal, mf)
+        both(do_b, backward_spatial, mb)
+        both(do_f, forward_out, mf)
         return carry
 
-    lax.fori_loop(0, 2 * MB, step, 0)
+    lax.fori_loop(0, 2 * pairs, step, 0)
 
     def finish(m, carry):
         store(0, a_out, o_act, m).wait()
@@ -523,19 +554,21 @@
 
         @pl.when(jnp.logical_not(last))
         def _():
-            to_pipe(0, a_out, a_in, m, 1).wait_send()
+            for part in range(2):
+                half_to_pipe(2, part, a_out, a_in, m, 1).wait_send()
 
         @pl.when(even_inner)
         def _():
-            to_pipe(1, a_in, skip_in, m, 1).wait_send()
+            to_pipe(0, a_in, skip_in, m, 1).wait_send()
 
         @pl.when(jnp.logical_not(first))
         def _():
-            to_pipe(2, ig_out, ga_in, m, -1).wait_send()
+            for part in range(2):
+                half_to_pipe(4, part, ig_out, ga_in, m, -1).wait_send()
 
         @pl.when(odd)
         def _():
-            to_pipe(3, gs_out, gs_in, m, -1).wait_send()
+            to_pipe(1, gs_out, gs_in, m, -1).wait_send()
 
         return carry
 
@@ -587,8 +620,8 @@
             wide,
             pltpu.VMEM((MB, rows, m_ch), f32),
             pltpu.VMEM((MB, rows, d), f32),
-            pltpu.VMEM((MB, rows, d), f32),
-            pltpu.VMEM((rows, m_ch), f32),
+            pltpu.VMEM((2, rows, d), f32),
+            pltpu.VMEM((2, rows, m_ch), f32),
             pltpu.VMEM((MB, rows, 128), f32),
             pltpu.VMEM((MB, 1, m_ch), f32),
             pltpu.VMEM((MB, 1, d), f32),
@@ -599,11 +632,11 @@
             pltpu.VMEM((MB, n_dp, 1, 2 * m_ch), f32),
             dma((4, MB)),
             dma((4, MB)),
-            dma((2,)),
+            dma((19,)),
             dma((MB,)),
             dma((6, MB)),
-            dma((4, MB)),
-            dma((4, MB)),
+            dma((6, MB)),
+            dma((6, MB)),
             dma((4, MB)),
             dma((4, MB)),
         ],
@@ -633,13 +666,10 @@
     gr_hbm,
     o_s,
     o_t,
-    a_raw,
-    v_raw,
-    a_pad,
-    v_pad,
+    a,
+    v,
     gu,
     gr,
-    edge,
     window,
     acc_s,
     acc_t,
@@ -654,7 +684,6 @@
     frames, height, width = dims
     n_clips, rows, d = a_hbm.shape
     m_ch = v_hbm.shape[2]
-    step = height * width
     me = lax.axis_index("dp")
     n = lax.axis_size("dp") // 2
     z = lax.div(me, 2)
@@ -663,27 +692,6 @@
     piece = got_s.shape[3]
     n_pieces = m_ch // piece
     span = acc_s.shape[0]
-    lead = a_pad.shape[2] - rows - 8
-
-    load_gu = [
-        pltpu.make_async_copy(gu_hbm.at[i], gu.at[pl.ds(i * rows, rows)], load_sem.at[2, i])
-        for i in range(n_clips)
-    ]
-    load_gr = [
-        pltpu.make_async_copy(gr_hbm.at[i], gr.at[pl.ds(i * rows, rows)], load_sem.at[3, i])
-        for i in range(n_clips)
-    ]
-    for copy in load_gu + load_gr:
-        copy.start()
-
-    def load_a(i):
-        return pltpu.make_async_copy(a_hbm.at[i], a_raw.at[lax.rem(i, 2)], load_sem.at[0, i])
-
-    def load_v(i):
-        return pltpu.make_async_copy(v_hbm.at[i], v_raw.at[lax.rem(i, 2)], load_sem.at[1, i])
-
-    load_a(0).start()
-    load_v(0).start()
 
     barrier = pltpu.get_barrier_semaphore()
 
@@ -695,39 +703,25 @@
     def _():
         pl.semaphore_signal(barrier, 1, device_id={"dp": me + 2}, device_id_type=MESH)
 
-    h = lax.broadcasted_iota(jnp.int32, (frames, height, width, 128), 1)
-    for dh in (-1, 0, 1):
-        inside = (h + dh >= 0) & (h + dh < height)
-        edge[dh + 1] = jnp.where(inside, 1.0, 0.0).astype(f32).reshape(rows, 128)
-
-    def prepare(i, carry):
-        load_a(i).wait()
-        load_v(i).wait()
-
-        @pl.when(i + 1 < n_clips)
-        def _():
-            load_a(i + 1).start()
-            load_v(i + 1).start()
-
-        slot = lax.rem(i, 2)
-        for c in range(0, d, 128):
-            x = a_raw[slot, :, c : c + 128].astype(f32)
-            for dw in (-1, 0, 1):
-                y = pltpu.roll(x, (-dw) % rows, 0) if dw else x
-                a_pad[i, dw + 1, lead : lead + rows, c : c + 128] = y
-                a_pad[i, dw + 1, lead - 8 : lead, c : c + 128] = jnp.zeros((8, 128), f32)
-                a_pad[i, dw + 1, lead + rows :, c : c + 128] = jnp.zeros((8, 128), f32)
-        zero = jnp.zeros((step, 128), f32)
-        for c in range(0, m_ch, 128):
-            v_pad[i, :step, c : c + 128] = zero
-            v_pad[i, step : step + rows, c : c + 128] = v_raw[slot, :, c : c + 128].astype(f32)
-            v_pad[i, step + rows :, c : c + 128] = zero
-        return carry
-
-    lax.fori_loop(0, n_clips, prepare, 0)
-    for copy in load_gu + load_gr:
-        copy.wait()
+    loads = [
+        pltpu.make_async_copy(src, dst, load_sem.at[i])
+        for i, (src, dst) in enumerate(((a_hbm, a), (gu_hbm, gu), (v_hbm, v), (gr_hbm, gr)))
+    ]
+    for copy in loads:
+        copy.start()
     pl.semaphore_wait(barrier, 2 - jnp.where(z == 0, 1, 0) - jnp.where(z == n - 1, 1, 0))
+    loads[0].wait()
+
+    def moved(x, before, after, dt, step):
+        if not dt:
+            return x
+        y = x.reshape(before, after, 128)
+        zero = jnp.zeros((before, step, 128), f32)
+        if dt > 0:
+            y = jnp.concatenate([y[:, step:], zero], axis=1)
+        else:
+            y = jnp.concatenate([zero, y[:, :-step]], axis=1)
+        return y.reshape(rows, 128)
 
     def transfer(src, dst, dest, p):
         right = dest > z
@@ -779,29 +773,42 @@
         low, start = place(owner * rows_s)
 
         def fill_space(i, c):
+            to = pl.ds(pl.multiple_of(i * rows, 16), rows)
             for j in range(span // 128):
                 chunk = jnp.minimum(low + j, 9 * d // 128 - 1)
                 tap = lax.div(chunk, d // 128)
-                lane = chunk - tap * (d // 128)
-                dh = lax.div(tap, 3)
-                dw = tap - 3 * dh
-                x = a_pad[
-                    i,
-                    dw,
-                    pl.ds(pl.multiple_of(lead - 8 + 8 * dh, 8), rows),
-                    pl.ds(pl.multiple_of(lane * 128, 128), 128),
-                ]
-                window[pl.ds(pl.multiple_of(i * rows, 16), rows), j * 128 : (j + 1) * 128] = (
-                    x * edge[dh]
-                ).astype(bf16)
+                lane = pl.ds(pl.multiple_of((chunk - tap * (d // 128)) * 128, 128), 128)
+
+                def fill(dh, dw):
+                    x = a[i, :, lane].astype(f32)
+                    if dw:
+                        x = pltpu.roll(x, (-dw) % rows, 0)
+                    x = moved(x, frames, height * width, dh, width)
+                    window[to, j * 128 : (j + 1) * 128] = x.astype(bf16)
+
+                lax.switch(
+                    tap,
+                    [
+                        functools.partial(fill, dh, dw)
+                        for dh in (-1, 0, 1)
+                        for dw in (-1, 0, 1)
+                    ],
+                )
             return c
 
         lax.fori_loop(0, n_clips, fill_space, 0)
+
+        @pl.when(q == 0)
+        def _():
+            loads[1].wait()
+
 
         def space(p, c):
             s = pl.ds(pl.multiple_of(p * piece, 128), piece)
             acc_s[...] = lax.dot_general(
-                window[...], gu[:, s], (((0,), (0,)), ((), ())), preferred_element_type=f32
+                window[...],
+                gu[:, :, s].reshape(n_clips * rows, piece),
+                (((0,), (0,)), ((), ())), preferred_element_type=f32
             )
             settle(
                 dest,
@@ -820,23 +827,30 @@
         low_t, start_t = place(owner * rows_t)
 
         def fill_time(i, c):
+            to = pl.ds(pl.multiple_of(i * rows, 16), rows)
             for j in range(span // 128):
                 chunk = jnp.minimum(low_t + j, 3 * m_ch // 128 - 1)
                 tap = lax.div(chunk, m_ch // 128)
-                lane = chunk - tap * (m_ch // 128)
-                x = v_pad[
-                    i,
-                    pl.ds(pl.multiple_of(tap * step, 8), rows),
-                    pl.ds(pl.multiple_of(lane * 128, 128), 128),
-                ]
-                window[pl.ds(pl.multiple_of(i * rows, 16), rows), j * 128 : (j + 1) * 128] = (
-                    x.astype(bf16)
-                )
+                lane = pl.ds(pl.multiple_of((chunk - tap * (m_ch // 128)) * 128, 128), 128)
+
+                def fill(dt):
+                    x = v[i, :, lane].astype(f32)
+                    x = moved(x, 1, rows, dt, height * width)
+                    window[to, j * 128 : (j + 1) * 128] = x.astype(bf16)
+
+                lax.switch(tap, [functools.partial(fill, dt) for dt in (-1, 0, 1)])
             return c
+
+        @pl.when(q == 0)
+        def _():
+            loads[2].wait()
+            loads[3].wait()
 
         lax.fori_loop(0, n_clips, fill_time, 0)
         acc_t[...] = lax.dot_general(
-            window[...], gr[...], (((0,), (0,)), ((), ())), preferred_element_type=f32
+            window[...],
+            gr[...].reshape(n_clips * rows, d),
+            (((0,), (0,)), ((), ())), preferred_element_type=f32
         )
         settle(
             dest,
@@ -865,8 +879,6 @@
 def gradients(dims, n_dp, a, v, gu, gr):
     n_clips, rows, d = a.shape
     m_ch = v.shape[2]
-    frames, height, width = dims
-    step = height * width
     rows_s, rows_t = 9 * d // n_dp, 3 * m_ch // n_dp
     n = n_dp // 2
     piece = 384
@@ -880,13 +892,10 @@
         in_specs=[pl.BlockSpec(memory_space=pl.ANY)] * 4,
         out_specs=[pl.BlockSpec(memory_space=pltpu.VMEM)] * 2,
         scratch_shapes=[
-            pltpu.VMEM((2, rows, d), bf16),
-            pltpu.VMEM((2, rows, m_ch), bf16),
-            pltpu.VMEM((n_clips, 3, rows + 16, d), f32),
-            pltpu.VMEM((n_clips, rows + 2 * step, m_ch), f32),
-            pltpu.VMEM((n_clips * rows, m_ch), bf16),
-            pltpu.VMEM((n_clips * rows, d), bf16),
-            pltpu.VMEM((3, rows, 128), f32),
+            pltpu.VMEM(a.shape, bf16),
+            pltpu.VMEM(v.shape, bf16),
+            pltpu.VMEM(gu.shape, bf16),
+            pltpu.VMEM(gr.shape, bf16),
             pltpu.VMEM((n_clips * rows, span), bf16),
             pltpu.VMEM((span, piece), f32),
             pltpu.VMEM((span, d), f32),
@@ -894,12 +903,12 @@
             pltpu.VMEM((n + 1, rows_t, d), bf16),
             pltpu.VMEM((n, n_pieces, rows_s, piece), bf16),
             pltpu.VMEM((n, rows_t, d), bf16),
-            dma((4, n_clips)),
+            dma((4,)),
             dma((n, n_pieces + 1)),
             dma((n + 1, n_pieces + 1)),
         ],
         compiler_params=pltpu.CompilerParams(
-            collective_id=1, has_side_effects=True, vmem_limit_bytes=62 * 2**20
+            collective_id=1, has_side_effects=True, vmem_limit_bytes=40 * 2**20
         ),
     )(a, v, gu, gr)
 

time: 378 us -> 360 us (0.952)
  Pallas kernels: 363 us -> 343 us
    pallas_call x1, Pallas kernels: 136 us -> 126 us  [gradients(): pl.pallas_call(functools.partial(gradient_kernel, dims), out_shape=(shape...]
    pallas_call x1, Pallas kernels: 227 us -> 217 us  [relay(): pl.pallas_call(functools.partial(relay_kernel, dims), out_shape=(shape((M...]
    unnamed x20 -> x24, local copies, waits for them, and re-layouts: 8.32 us -> 10 us
where the time goes in v3:
time: 360 us
  Pallas kernels  343 us (95%)
  local copies, waits for them, and re-layouts  15.9 us (4%)
    pallas_call x1, Pallas kernels, relay(): pl.pallas_call(functools.partial(relay_kernel, dims), out_shape=(shape((M...  217 us
    pallas_call x1, Pallas kernels, gradients(): pl.pallas_call(functools.partial(gradient_kernel, dims), out_shape=(shape...  126 us
    unnamed x24, local copies, waits for them, and re-layouts  10 us

profile of v3, /device:TPU:0, one launch (start us, length us, event | category | flops | bytes accessed | tf_op | source)
XLA Modules:
  0.0 359.6 jit_solution(11731537596397853358)
XLA Ops:
  0.6 0.0 copy-start.3
  0.6 1.4 copy.23
  2.0 1.1 pad.7.clone
  3.1 0.0 copy-done.3
  3.1 0.2 copy.24
  3.3 1.1 pad.8.clone
  4.4 217.1 %shard_map.152 = (bf16[4,224,512]{2,1,0:T(8,128)(2,1)}, bf16[4,224,512]{2,1,0:T(8,128)(2,1)}, bf16[2,4,224,512]{3,2,1,0:T(8,128)(2,1)}, bf16[2,4,224,1152]{3,2,1...) custom-call(bf16[4,224,512]{2,1,0:T(8,128)(2,1)} %bitcast.25, ...), custom_call_target="tpu_custom_call" | custom-call | tf_op jit(solution)/shard_map/pallas_call | solution.py:589
  221.5 0.0 copy-start.1
  221.5 3.7 %copy_bitcast_fusion = (bf16[1,4,4,7,7,512]{5,2,4,3,1,0:T(4,128)(2,1)}, bf16[1,4,4,7,7,512]{5,2,4,3,1,0:T(4,128)(2,1)}) fusion(bf16[4,4,7,7,512]{4,3,2,1,0:T(8,128)(2,1)} %bitcast.29, bf16[4,4,7,7,512]{4,3,2,1,0:T(8,128)(2,1)} %bitcast.28), kind=kLoop, calls=%fused_computation | loop fusion | bytes 3211264 | tf_op jit(solution)/shard_map/broadcast_in_dim | solution.py:996
  225.2 0.0 copy-done.1
  225.2 0.0 copy-start
  225.2 2.2 copy-done
  227.4 0.0 copy-start.2
  227.4 1.5 copy-done.2
  228.9 125.9 %shard_map.153 = (f32[576,1152]{1,0:T(8,128)S(1)}, f32[432,512]{1,0:T(8,128)S(1)}) custom-call(bf16[8,224,512]{2,1,0:T(8,128)(2,1)S(1)} %bitcast.20, bf16[8,224,1152]{2,1,0:T(8,128)(2,1)S(1)} %bitcast.18, bf16[8,224,1152]{2,1,0:T(8,128)(2,1)} %bitcast.24, bf16[8,224,512]{2,1,0:T(8,128)(2,1)S(1)} %bitcast.21), custom_call_target="tpu_custom_call" | custom-call | tf_op jit(solution)/shard_map/pallas_call | solution.py:889
  354.8 0.0 copy-start.5
  354.8 0.0 copy-start.4
  354.8 0.0 copy-start.7
  354.8 0.0 copy-start.6
  354.8 1.5 copy.33
  356.3 0.9 copy.34
  357.2 0.0 copy-done.5
  357.2 0.6 copy.35
  357.8 0.0 copy-done.4
  357.8 0.6 copy.36
  358.4 0.0 copy-done.7
  358.4 0.6 copy.37
  359.0 0.0 copy-done.6
  359.0 0.6 copy.38
Async XLA Ops:
  0.6 2.5 copy-start.3
  221.5 3.7 %copy-start.1 = (bf16[2,4,224,512]{3,2,1,0:T(8,128)(2,1)S(1)}, bf16[2,4,224,512]{3,2,1,0:T(8,128)(2,1)}, u32[]{:S(2)}) copy-start(bf16[2,4,224,512]{3,2,1,0:T(8,128)(2,1)} %get-tuple-element.22) | copy-start | bytes 5505028
  225.2 2.2 copy-start
  227.4 1.5 copy-start.2
  354.8 2.5 copy-start.5
  354.8 3.0 copy-start.4
  354.8 3.6 %copy-start.7 = (f32[1,512]{1,0:T(1,128)S(1)}, f32[1,512]{1,0:T(1,128)}, u32[]{:S(2)}) copy-start(f32[1,512]{1,0:T(1,128)} %get-tuple-element.48) | copy-start | bytes 6148
  354.8 4.2 %copy-start.6 = (f32[1,512]{1,0:T(1,128)S(1)}, f32[1,512]{1,0:T(1,128)}, u32[]{:S(2)}) copy-start(f32[1,512]{1,0:T(1,128)} %get-tuple-element.49) | copy-start | bytes 6148

commit v4 on v3

--- a/solution.py
+++ b/solution.py
@@ -60,6 +60,8 @@
     a_in,
     skip_in,
     a_out,
+    r_in,
+    r_out,
     ga_in,
     gs_in,
     gs_out,
@@ -68,17 +70,23 @@
     gr,
     gu,
     uh,
-    rh,
-    gp,
+    r_sum,
     gq,
     keep,
     fact_s,
     fact_t,
+    off_t,
+    fact_p,
+    off_p,
     cnt,
+    scale_out,
+    scale_in,
     x_s,
     x_t,
+    x_p,
     x_bt,
     x_bs,
+    x_bp,
     x_send,
     x_recv,
     w_sem,
@@ -101,7 +109,9 @@
     last = section == n_pipe - 1
     odd = lax.rem(section, 2) == 1
     even_inner = jnp.logical_and(jnp.logical_not(odd), jnp.logical_not(last))
-    skipping = odd.astype(f32)
+    early = section < 2
+    skip_own = odd.astype(f32)
+    skip_prev = jnp.logical_not(jnp.logical_or(odd, first)).astype(f32)
 
     def load_ws(part, tap):
         half = d // 2
@@ -117,11 +127,21 @@
     def load_cot(m):
         return pltpu.make_async_copy(cotangent.at[m], ga_in.at[m], load_sem.at[m])
 
+    def load_skip(m):
+        return pltpu.make_async_copy(clips.at[m], skip_in.at[m], load_sem.at[m])
+
+    local_skip = jnp.logical_not(jnp.logical_or(first, last))
+
     @pl.when(first)
     def _():
         for m in range(MB):
             load_clip(m).start()
 
+    @pl.when(local_skip)
+    def _():
+        for m in range(MB):
+            load_skip(m).start()
+
     for part in range(2):
         for tap in range(9):
             load_ws(part, tap).start()
@@ -132,8 +152,12 @@
         for m in range(MB):
             load_cot(m).start()
 
-    for ref in (o_gain_s, o_shift_s, o_gain_t, o_shift_t, skip_in, gs_in):
+    for ref in (o_gain_s, o_shift_s, o_gain_t, o_shift_t, gs_in, scale_in):
         ref[...] = jnp.zeros_like(ref)
+
+    @pl.when(first)
+    def _():
+        skip_in[...] = jnp.zeros_like(skip_in)
 
     barrier = pltpu.get_barrier_semaphore()
 
@@ -145,13 +169,34 @@
 
     lax.fori_loop(1, n_dp, greet, 0)
 
+    def greet_pipe(step):
+        def greet_one(j, carry):
+            pl.semaphore_signal(
+                barrier,
+                1,
+                device_id={"pipe": section + step, "dp": j},
+                device_id_type=MESH,
+            )
+            return carry
+
+        lax.fori_loop(0, n_dp, greet_one, 0)
+
     @pl.when(jnp.logical_not(first))
     def _():
-        pl.semaphore_signal(barrier, 1, device_id={"pipe": section - 1}, device_id_type=MESH)
+        greet_pipe(-1)
 
     @pl.when(jnp.logical_not(last))
     def _():
-        pl.semaphore_signal(barrier, 1, device_id={"pipe": section + 1}, device_id_type=MESH)
+        greet_pipe(1)
+
+    pl.semaphore_signal(
+        barrier,
+        1,
+        device_id={"pipe": section + jnp.where(early, 2, -2)},
+        device_id_type=MESH,
+    )
+    scale_out[0] = g_t[...]
+    scale_out[1] = b_t[...]
 
     def make_keep(m, carry):
         n_rows = frames * height * width
@@ -171,7 +216,22 @@
         return carry
 
     lax.fori_loop(0, MB, make_keep, 0)
-    pl.semaphore_wait(barrier, n_dp + 1 - jnp.where(first, 1, 0) - jnp.where(last, 1, 0))
+    sides = 3 - jnp.where(first, 1, 0) - jnp.where(last, 1, 0)
+    pl.semaphore_wait(barrier, sides * n_dp)
+
+    def send_scale():
+        return pltpu.make_async_remote_copy(
+            src_ref=scale_out,
+            dst_ref=scale_in,
+            send_sem=w_sem.at[19],
+            recv_sem=w_sem.at[20],
+            device_id={"pipe": section + 1},
+            device_id_type=MESH,
+        )
+
+    @pl.when(jnp.logical_not(last))
+    def _():
+        send_scale().start()
 
     def share(kind, buf, m):
         def send(j, carry):
@@ -192,6 +252,28 @@
         pltpu.make_async_copy(others, others, x_send.at[kind, m]).wait()
         pltpu.make_async_copy(others, others, x_recv.at[kind, m]).wait()
 
+    def cross(kind, src, dst, m, step):
+        def send(j, carry):
+            pltpu.make_async_remote_copy(
+                src_ref=src,
+                dst_ref=dst.at[m, me],
+                send_sem=x_send.at[kind, m],
+                recv_sem=x_recv.at[kind, m],
+                device_id={"pipe": section + step, "dp": lax.rem(me + j, n_dp)},
+                device_id_type=MESH,
+            ).start()
+            return carry
+
+        lax.fori_loop(0, n_dp, send, 0)
+
+    def crossed(kind, buf, m):
+        slots = buf.at[m]
+        pltpu.make_async_copy(slots, slots, x_recv.at[kind, m]).wait()
+
+    def cross_sent(kind, buf, m):
+        slots = buf.at[m]
+        pltpu.make_async_copy(slots, slots, x_send.at[kind, m]).wait()
+
     def to_pipe(kind, src, dst, m, step):
         return pltpu.make_async_remote_copy(
             src_ref=src.at[m],
@@ -271,6 +353,7 @@
         spread = jnp.sum(dev * dev, axis=0, keepdims=True)
         buf[m, me, :, pl.ds(pl.multiple_of(c * 128, 128), 128)] = total
         buf[m, me, :, pl.ds(pl.multiple_of(channels + c * 128, 128), 128)] = spread
+        return dev
 
     def merged(m, buf, c, channels):
         counts = buf[m, :, :, 2 * channels :]
@@ -282,16 +365,56 @@
         var = jnp.sum(spreads + counts * off * off, axis=0) / n
         return n, mean, lax.rsqrt(var + eps_norm)
 
+    def lanes_of(part, i):
+        return pl.ds(pl.multiple_of(part * half + i * 128, 128), 128)
+
+    def normed_prev(m, s):
+        return (r_in[m, :, s].astype(f32) + off_p[m, :, s]) * fact_p[m, :, s]
+
+    def preact_prev(m, s, normed):
+        return scale_in[0, :, s] * normed + scale_in[1, :, s]
+
+    def skipped_prev(m, s, value):
+        return value + skip_prev * skip_in[m, :, s].astype(f32)
+
+    def activate(m, part, i, s):
+        s = lanes_of(part, i)
+        n, mean, rstd = merged(m, x_p, part * (half // 128) + i, d)
+        off_p[m, :, s] = x_p[m, me, :, s] / x_p[m, me, :, 2 * d :] - mean
+        fact_p[m, :, s] = rstd
+        value = preact_prev(m, s, normed_prev(m, s))
+
+        @pl.when(section == 2)
+        def _():
+            a_in[m, :, s] = (keep[m] * silu(skipped_prev(m, s, value))).astype(bf16)
+
+        @pl.when(section != 2)
+        def _():
+            a_in[m, :, s] = (keep[m] * silu(value)).astype(bf16)
+
     def forward_spatial(m):
         @pl.when(first)
         def _():
             load_clip(m).wait()
 
+        @pl.when(jnp.logical_not(first))
+        def _():
+            @pl.when(m == 0)
+            def _():
+                send_scale().wait_recv()
+
+            @pl.when(local_skip)
+            def _():
+                load_skip(m).wait()
+
+            crossed(4, x_p, m)
+
         for part in range(2):
 
             @pl.when(jnp.logical_not(first))
             def _():
-                half_to_pipe(2, part, a_out, a_in, m, 1).wait_recv()
+                half_to_pipe(2, part, r_out, r_in, m, 1).wait_recv()
+                lane_chunks(half, functools.partial(activate, m, part))
 
             def column(i, s):
                 s = pl.ds(pl.multiple_of(part * half + i * 128, 128), 128)
@@ -313,18 +436,19 @@
                     load_ws(part, tap).wait()
 
             k = slice(part * 9 * half, (part + 1) * 9 * half)
-            value = jnp.dot(cols[:, k], w_s[k, :], preferred_element_type=f32)
-            if part == 0:
-                uh[m] = value
-            else:
-                uh[m] += value
-
-        @pl.when(even_inner)
-        def _():
-            to_pipe(0, a_in, skip_in, m, 1).start()
+            for s in (slice(0, 512), slice(512, m_ch)):
+                value = jnp.dot(cols[:, k], w_s[k, s], preferred_element_type=f32)
+                if part == 0:
+                    uh[m, :, s] = value
+                else:
+                    uh[m, :, s] += value
 
         x_s[m, me, :, 2 * m_ch :] = cnt[m]
-        lane_chunks(m_ch, lambda i, s: local_sums(m, uh[m, :, s], x_s, i, m_ch))
+
+        def sums(i, s):
+            local_sums(m, uh[m, :, s], x_s, i, m_ch)
+
+        lane_chunks(m_ch, sums)
         share(0, x_s, m)
         share_operand(2, a_in, o_in, m)
 
@@ -351,77 +475,97 @@
         def _():
             load_wt.wait()
 
-        rh[m] = jnp.dot(cols[:, : 3 * m_ch], w_t[...], preferred_element_type=f32)
+        r_sum[...] = jnp.dot(cols[:, : 3 * m_ch], w_t[...], preferred_element_type=f32)
         x_t[m, me, :, 2 * d :] = cnt[m]
-        lane_chunks(d, lambda i, s: local_sums(m, rh[m, :, s], x_t, i, d))
+
+        def centre(i, s):
+            r_out[m, :, s] = local_sums(m, r_sum[:, s], x_t, i, d).astype(bf16)
+
+        lane_chunks(d, centre)
+
+        @pl.when(jnp.logical_not(last))
+        def _():
+            cross(4, x_t.at[m, me], x_p, m, 1)
+            for part in range(2):
+                half_to_pipe(2, part, r_out, r_in, m, 1).start()
+
         share(1, x_t, m)
 
-    def preact(m, s, normed):
-        return g_t[:, s] * normed + b_t[:, s] + skipping * skip_in[m, :, s].astype(f32)
+    def normed_own(m, s):
+        return (r_out[m, :, s].astype(f32) + off_t[m, :, s]) * fact_t[m, :, s]
+
+    def preact_own(m, s, normed):
+        return g_t[:, s] * normed + b_t[:, s] + skip_own * skip_in[m, :, s].astype(f32)
 
     def forward_out(m):
+        @pl.when(last)
+        def _():
+            to_pipe(0, a_out, skip_in, m, 2).wait_recv()
+
         shared(1, x_t, m)
-
-        @pl.when(odd)
-        def _():
-            to_pipe(0, a_in, skip_in, m, 1).wait_recv()
 
         def column(i, s):
             n, mean, rstd = merged(m, x_t, i, d)
+            off_t[m, :, s] = x_t[m, me, :, s] / cnt[m] - mean
             fact_t[m, :, s] = rstd
-            normed = (rh[m, :, s] - mean) * rstd
-            rh[m, :, s] = normed
-            a_out[m, :, s] = (keep[m] * silu(preact(m, s, normed))).astype(bf16)
+            value = keep[m] * silu(preact_own(m, s, normed_own(m, s)))
+            a_out[m, :, s] = value.astype(bf16)
 
         lane_chunks(d, column)
-
-        @pl.when(jnp.logical_not(last))
-        def _():
-            for part in range(2):
-                half_to_pipe(2, part, a_out, a_in, m, 1).start()
-
         store(0, a_out, o_act, m).start()
 
+        @pl.when(section == 1)
+        def _():
+            to_pipe(0, a_out, skip_in, m, 2).start()
+
+    def slope_sums(row, value, normed, i, s):
+        row[:, s] = jnp.sum(value, axis=0, keepdims=True)
+        at = pl.ds(pl.multiple_of(d + i * 128, 128), 128)
+        row[:, at] = jnp.sum(value * normed, axis=0, keepdims=True)
+
+    def own_slope(m, s, normed):
+        return ga_in[m, :, s].astype(f32) * keep[m] * silu_slope(preact_own(m, s, normed))
+
     def backward_in(m):
-        @pl.when(last)
-        def _():
-            load_cot(m).wait()
-
-        @pl.when(jnp.logical_not(last))
-        def _():
-            for part in range(2):
-                half_to_pipe(4, part, ig_out, ga_in, m, -1).wait_recv()
+        load_cot(m).wait()
 
         def column(i, s):
-            normed = rh[m, :, s]
-            slope = ga_in[m, :, s].astype(f32) * keep[m] * silu_slope(preact(m, s, normed))
-            gp[lax.rem(m, 2), :, s] = slope
-            gs_out[m, :, s] = slope.astype(bf16)
-            x_bt[m, me, :, s] = jnp.sum(slope, axis=0, keepdims=True)
-            at = pl.ds(pl.multiple_of(d + i * 128, 128), 128)
-            x_bt[m, me, :, at] = jnp.sum(slope * normed, axis=0, keepdims=True)
+            normed = normed_own(m, s)
+            slope_sums(x_bt.at[m, me], own_slope(m, s, normed), normed, i, s)
 
         lane_chunks(d, column)
         share(2, x_bt, m)
-
-        @pl.when(odd)
-        def _():
-            to_pipe(1, gs_out, gs_in, m, -1).start()
 
     def totals(buf, m, s, i, channels):
         at = pl.ds(pl.multiple_of(channels + i * 128, 128), 128)
         return jnp.sum(buf[m, :, :, s], axis=0), jnp.sum(buf[m, :, :, at], axis=0)
 
     def backward_temporal(m):
-        shared(2, x_bt, m)
+        @pl.when(last)
+        def _():
+            shared(2, x_bt, m)
+
+        @pl.when(jnp.logical_not(last))
+        def _():
+            crossed(2, x_bt, m)
+            for part in range(2):
+                half_to_pipe(4, part, ig_out, ga_in, m, -1).wait_recv()
+
         n = jnp.sum(x_t[m, :, :, 2 * d :], axis=0)
 
         def column(i, s):
             shift_sum, gain_sum = totals(x_bt, m, s, i, d)
             o_shift_t[:, s] += shift_sum
             o_gain_t[:, s] += gain_sum
+            normed = normed_own(m, s)
+            slope = own_slope(m, s, normed)
+
+            @pl.when(last)
+            def _():
+                gs_out[m, :, s] = slope.astype(bf16)
+
             scale = g_t[:, s] * fact_t[m, :, s]
-            value = keep[m] * scale * (gp[lax.rem(m, 2), :, s] - (shift_sum + rh[m, :, s] * gain_sum) / n)
+            value = keep[m] * scale * (slope - (shift_sum + normed * gain_sum) / n)
             value = value.astype(bf16)
             gr[m, :, s] = value
             value = value.astype(f32)
@@ -431,6 +575,7 @@
 
         lane_chunks(d, column)
         share_operand(4, gr, o_gr, m)
+
         gq[lax.rem(m, 2)] = jnp.dot(cols[:, : 3 * d], w_t_back[...], preferred_element_type=f32)
 
         def sums(i, s):
@@ -479,9 +624,29 @@
 
             @pl.when(jnp.logical_not(first))
             def _():
-                half_to_pipe(4, part, ig_out, ga_in, m, -1).start()
+                def sums(i, s):
+                    s = lanes_of(part, i)
+                    normed = normed_prev(m, s)
+                    slope = silu_slope(skipped_prev(m, s, preact_prev(m, s, normed)))
+                    slope = ig_out[m, :, s].astype(f32) * keep[m] * slope
+
+                    @pl.when(section == 2)
+                    def _():
+                        gs_out[m, :, s] = slope.astype(bf16)
+
+                    slope_sums(x_bp.at[m, 0], slope, normed, part * (half // 128) + i, s)
+
+                if part == 0:
+                    half_to_pipe(4, part, ig_out, ga_in, m, -1).start()
+                lane_chunks(half, sums)
+                if part == 1:
+                    cross(2, x_bp.at[m, 0], x_bt, m, -1)
+                    half_to_pipe(4, part, ig_out, ga_in, m, -1).start()
 
         store(1, ig_out, o_grad, m).start()
+
+    def send_skip_grad(m):
+        to_pipe(1, gs_out, gs_in, m, jnp.where(last, -1, -2)).start()
 
     def turn_weights():
         @pl.when(jnp.logical_not(first))
@@ -530,12 +695,17 @@
 
                 lax.fori_loop(0, 2, one, 0)
 
-        both(do_b, backward_in, mb)
+        inner = jnp.logical_not(last)
+        done_f = jnp.logical_and(s > 0, s <= pairs)
+        md = 2 * jnp.clip(s - 1, 0, pairs - 1)
+        both(jnp.logical_and(done_f, last), forward_out, md)
+        both(jnp.logical_and(do_b, last), backward_in, mb)
         both(do_f, forward_spatial, mf)
+        both(jnp.logical_and(done_f, inner), forward_out, md)
         both(do_b, backward_temporal, mb)
         both(do_f, forward_temporal, mf)
         both(do_b, backward_spatial, mb)
-        both(do_f, forward_out, mf)
+        both(jnp.logical_and(do_b, jnp.logical_not(early)), send_skip_grad, mb)
         return carry
 
     lax.fori_loop(0, 2 * pairs, step, 0)
@@ -554,25 +724,32 @@
 
         @pl.when(jnp.logical_not(last))
         def _():
+            cross_sent(4, x_p, m)
             for part in range(2):
-                half_to_pipe(2, part, a_out, a_in, m, 1).wait_send()
-
-        @pl.when(even_inner)
-        def _():
-            to_pipe(0, a_in, skip_in, m, 1).wait_send()
+                half_to_pipe(2, part, r_out, r_in, m, 1).wait_send()
+
+
+        @pl.when(section == 1)
+        def _():
+            to_pipe(0, a_out, skip_in, m, 2).wait_send()
 
         @pl.when(jnp.logical_not(first))
         def _():
+            cross_sent(2, x_bt, m)
             for part in range(2):
                 half_to_pipe(4, part, ig_out, ga_in, m, -1).wait_send()
 
-        @pl.when(odd)
+        @pl.when(jnp.logical_not(early))
         def _():
             to_pipe(1, gs_out, gs_in, m, -1).wait_send()
 
         return carry
 
     lax.fori_loop(0, MB, finish, 0)
+
+    @pl.when(jnp.logical_not(last))
+    def _():
+        send_scale().wait_send()
 
 
 def relay(dims, n_dp, clips, boxes, w_s, w_t, g_s, b_s, g_t, b_t, cotangent):
@@ -615,24 +792,32 @@
             narrow,
             narrow,
             narrow,
+            narrow,
+            narrow,
             wide,
             narrow,
             wide,
             pltpu.VMEM((MB, rows, m_ch), f32),
-            pltpu.VMEM((MB, rows, d), f32),
-            pltpu.VMEM((2, rows, d), f32),
+            pltpu.VMEM((rows, d), f32),
             pltpu.VMEM((2, rows, m_ch), f32),
             pltpu.VMEM((MB, rows, 128), f32),
             pltpu.VMEM((MB, 1, m_ch), f32),
             pltpu.VMEM((MB, 1, d), f32),
+            pltpu.VMEM((MB, 1, d), f32),
+            pltpu.VMEM((MB, 1, d), f32),
+            pltpu.VMEM((MB, 1, d), f32),
             pltpu.VMEM((MB, 1, 128), f32),
+            pltpu.VMEM((2, 1, d), f32),
+            pltpu.VMEM((2, 1, d), f32),
             pltpu.VMEM((MB, n_dp, 1, 2 * m_ch + 128), f32),
+            pltpu.VMEM((MB, n_dp, 1, 2 * d + 128), f32),
             pltpu.VMEM((MB, n_dp, 1, 2 * d + 128), f32),
             pltpu.VMEM((MB, n_dp, 1, 2 * d), f32),
             pltpu.VMEM((MB, n_dp, 1, 2 * m_ch), f32),
-            dma((4, MB)),
-            dma((4, MB)),
-            dma((19,)),
+            pltpu.VMEM((MB, 1, 1, 2 * d), f32),
+            dma((5, MB)),
+            dma((5, MB)),
+            dma((21,)),
             dma((MB,)),
             dma((6, MB)),
             dma((6, MB)),
@@ -709,7 +894,6 @@
     ]
     for copy in loads:
         copy.start()
-    pl.semaphore_wait(barrier, 2 - jnp.where(z == 0, 1, 0) - jnp.where(z == n - 1, 1, 0))
     loads[0].wait()
 
     def moved(x, before, after, dt, step):
@@ -801,6 +985,8 @@
         @pl.when(q == 0)
         def _():
             loads[1].wait()
+            sides = 2 - jnp.where(z == 0, 1, 0) - jnp.where(z == n - 1, 1, 0)
+            pl.semaphore_wait(barrier, sides)
 
 
         def space(p, c):

time: 360 us -> 348 us (0.967)
  Pallas kernels: 343 us -> 332 us
    pallas_call x1, Pallas kernels: 217 us -> 207 us  [relay(): pl.pallas_call(functools.partial(relay_kernel, dims), out_shape=(shape((M...]
where the time goes in v4:
time: 348 us
  Pallas kernels  332 us (95%)
  local copies, waits for them, and re-layouts  15.9 us (5%)
    pallas_call x1, Pallas kernels, relay(): pl.pallas_call(functools.partial(relay_kernel, dims), out_shape=(shape((M...  207 us
    pallas_call x1, Pallas kernels, gradients(): pl.pallas_call(functools.partial(gradient_kernel, dims), out_shape=(shape...  125 us
    unnamed x24, local copies, waits for them, and re-layouts  10 us

profile of v4, /device:TPU:0, one launch (start us, length us, event | category | flops | bytes accessed | tf_op | source)
XLA Modules:
  0.0 348.1 jit_solution(813995233642933862)
XLA Ops:
  0.6 0.0 copy-start.3
  0.6 1.4 copy.23
  2.0 1.1 pad.7.clone
  3.1 0.0 copy-done.3
  3.1 0.2 copy.24
  3.3 1.1 pad.8.clone
  4.4 206.8 %shard_map.152 = (bf16[4,224,512]{2,1,0:T(8,128)(2,1)}, bf16[4,224,512]{2,1,0:T(8,128)(2,1)}, bf16[2,4,224,512]{3,2,1,0:T(8,128)(2,1)}, bf16[2,4,224,1152]{3,2,1...) custom-call(bf16[4,224,512]{2,1,0:T(8,128)(2,1)} %bitcast.25, ...), custom_call_target="tpu_custom_call" | custom-call | tf_op jit(solution)/shard_map/pallas_call | solution.py:766
  211.3 0.0 copy-start.1
  211.3 3.7 %copy_bitcast_fusion = (bf16[1,4,4,7,7,512]{5,2,4,3,1,0:T(4,128)(2,1)}, bf16[1,4,4,7,7,512]{5,2,4,3,1,0:T(4,128)(2,1)}) fusion(bf16[4,4,7,7,512]{4,3,2,1,0:T(8,128)(2,1)} %bitcast.29, bf16[4,4,7,7,512]{4,3,2,1,0:T(8,128)(2,1)} %bitcast.28), kind=kLoop, calls=%fused_computation | loop fusion | bytes 3211264 | tf_op jit(solution)/shard_map/broadcast_in_dim | solution.py:1182
  214.9 0.0 copy-done.1
  214.9 0.0 copy-start
  214.9 2.2 copy-done
  217.1 0.0 copy-start.2
  217.1 1.5 copy-done.2
  218.6 124.7 %shard_map.153 = (f32[576,1152]{1,0:T(8,128)S(1)}, f32[432,512]{1,0:T(8,128)S(1)}) custom-call(bf16[8,224,512]{2,1,0:T(8,128)(2,1)S(1)} %bitcast.20, bf16[8,224,1152]{2,1,0:T(8,128)(2,1)S(1)} %bitcast.18, bf16[8,224,1152]{2,1,0:T(8,128)(2,1)} %bitcast.24, bf16[8,224,512]{2,1,0:T(8,128)(2,1)S(1)} %bitcast.21), custom_call_target="tpu_custom_call" | custom-call | tf_op jit(solution)/shard_map/pallas_call | solution.py:1075
  343.3 0.0 copy-start.5
  343.3 0.0 copy-start.4
  343.3 0.0 copy-start.7
  343.3 0.0 copy-start.6
  343.4 1.5 copy.33
  344.9 0.9 copy.34
  345.8 0.0 copy-done.5
  345.8 0.6 copy.35
  346.4 0.0 copy-done.4
  346.4 0.6 copy.36
  347.0 0.0 copy-done.7
  347.0 0.6 copy.37
  347.5 0.0 copy-done.6
  347.6 0.6 copy.38
Async XLA Ops:
  0.6 2.5 copy-start.3
  211.3 3.7 %copy-start.1 = (bf16[2,4,224,512]{3,2,1,0:T(8,128)(2,1)S(1)}, bf16[2,4,224,512]{3,2,1,0:T(8,128)(2,1)}, u32[]{:S(2)}) copy-start(bf16[2,4,224,512]{3,2,1,0:T(8,128)(2,1)} %get-tuple-element.22) | copy-start | bytes 5505028
  214.9 2.2 copy-start
  217.1 1.5 copy-start.2
  343.3 2.5 copy-start.5
  343.3 3.0 copy-start.4
  343.3 3.6 %copy-start.7 = (f32[1,512]{1,0:T(1,128)S(1)}, f32[1,512]{1,0:T(1,128)}, u32[]{:S(2)}) copy-start(f32[1,512]{1,0:T(1,128)} %get-tuple-element.48) | copy-start | bytes 6148
  343.3 4.2 %copy-start.6 = (f32[1,512]{1,0:T(1,128)S(1)}, f32[1,512]{1,0:T(1,128)}, u32[]{:S(2)}) copy-start(f32[1,512]{1,0:T(1,128)} %get-tuple-element.49) | copy-start | bytes 6148

commit v5 on v4

--- a/solution.py
+++ b/solution.py
@@ -96,6 +96,7 @@
     pipe_recv,
     twin_send,
     twin_recv,
+    hub_sem,
 ):
     cm, frames, height, width = dims
     rows = cm * frames * height * width
@@ -297,6 +298,38 @@
             device_id_type=MESH,
         )
 
+    hubs = o_in.shape[0] > 2
+    z = lax.div(me, 2)
+    outer = jnp.logical_or(z == 0, z == n_dp // 2 - 1)
+
+    def to_hub(m):
+        return pltpu.make_async_remote_copy(
+            src_ref=a_in.at[m],
+            dst_ref=o_in.at[2, m],
+            send_sem=hub_sem.at[0, m],
+            recv_sem=hub_sem.at[1, m],
+            device_id={"dp": me + jnp.where(z == 0, 2, -2)},
+            device_id_type=MESH,
+        )
+
+    def inputs_to_hub():
+        @pl.when(outer)
+        def _():
+            for m in range(MB):
+                to_hub(m).start()
+
+    def gu_to_hub(part):
+        m = min(part, 1)
+        s = (pl.ds(0, m_ch), pl.ds(0, 640), pl.ds(640, m_ch - 640))[part]
+        return pltpu.make_async_remote_copy(
+            src_ref=gu.at[m, :, s],
+            dst_ref=o_gu.at[2, m, :, s],
+            send_sem=hub_sem.at[2, part],
+            recv_sem=hub_sem.at[3, part],
+            device_id={"dp": me + jnp.where(z == 0, 2, -2)},
+            device_id_type=MESH,
+        )
+
     def store(kind, src, dst, m):
         return pltpu.make_async_copy(src.at[m], dst.at[m], store_sem.at[kind, m])
 
@@ -611,6 +644,13 @@
 
         lane_chunks(m_ch, column)
         share_operand(5, gu, o_gu, m)
+        if hubs:
+            for part in range(2):
+
+                @pl.when(outer & first & (m == part))
+                def _():
+                    gu_to_hub(part).start()
+
 
         @pl.when(even_inner)
         def _():
@@ -703,9 +743,26 @@
         both(do_f, forward_spatial, mf)
         both(jnp.logical_and(done_f, inner), forward_out, md)
         both(do_b, backward_temporal, mb)
+        if hubs:
+
+            @pl.when(outer & (s == wait_back + 1) & first)
+            def _():
+                gu_to_hub(2).start()
+
         both(do_f, forward_temporal, mf)
         both(do_b, backward_spatial, mb)
         both(jnp.logical_and(do_b, jnp.logical_not(early)), send_skip_grad, mb)
+        if hubs:
+
+            @pl.when(s == jnp.where(last, wait_back + 1, pairs - 1))
+            def _():
+                inputs_to_hub()
+
+            @pl.when(outer & (s == wait_back + 1) & jnp.logical_not(first))
+            def _():
+                for part in range(3):
+                    gu_to_hub(part).start()
+
         return carry
 
     lax.fori_loop(0, 2 * pairs, step, 0)
@@ -746,13 +803,27 @@
         return carry
 
     lax.fori_loop(0, MB, finish, 0)
+    if hubs:
+        for m in range(MB):
+
+            @pl.when(outer)
+            def _():
+                to_hub(m).wait_send()
+                if m < 3:
+                    gu_to_hub(m).wait_send()
+
+            @pl.when(jnp.logical_not(outer))
+            def _():
+                to_hub(m).wait_recv()
+                if m < 3:
+                    gu_to_hub(m).wait_recv()
 
     @pl.when(jnp.logical_not(last))
     def _():
         send_scale().wait_send()
 
 
-def relay(dims, n_dp, clips, boxes, w_s, w_t, g_s, b_s, g_t, b_t, cotangent):
+def relay(dims, n_dp, hubs, clips, boxes, w_s, w_t, g_s, b_s, g_t, b_t, cotangent):
     cm, frames, height, width = dims
     rows = cm * frames * height * width
     d, m_ch = w_t.shape[1], w_s.shape[1]
@@ -768,9 +839,9 @@
         out_shape=(
             shape((MB, rows, d), bf16),
             shape((MB, rows, d), bf16),
-            shape((2, MB, rows, d), bf16),
+            shape((3 if hubs else 2, MB, rows, d), bf16),
             shape((2, MB, rows, m_ch), bf16),
-            shape((2, MB, rows, m_ch), bf16),
+            shape((3 if hubs else 2, MB, rows, m_ch), bf16),
             shape((2, MB, rows, d), bf16),
             shape((1, m_ch), f32),
             shape((1, m_ch), f32),
@@ -824,6 +895,7 @@
             dma((6, MB)),
             dma((4, MB)),
             dma((4, MB)),
+            dma((4, MB)),
         ],
         compiler_params=pltpu.CompilerParams(
             collective_id=0, has_side_effects=True, vmem_limit_bytes=62 * 2**20
@@ -834,13 +906,19 @@
 def send_order(n, z, q):
     table = []
     for here in range(n):
-        sign = 1 if here < n / 2 else -1
-        table.append(sorted(range(n), key=lambda to: (-abs(to - here), -sign * to)))
+        up = sorted(range(here + 1, n), reverse=True)
+        down = list(range(here))
+        table.append((up + down if here < n / 2 else down + up) + [here])
     dest = 0
     for here in range(n):
         for at in range(n):
             dest = dest + jnp.where((z == here) & (q == at), table[here][at], 0)
     return dest
+
+
+FIRST = 128
+PIECE = 256
+SPAN = 640
 
 
 def gradient_kernel(
@@ -856,6 +934,7 @@
     gu,
     gr,
     window,
+    window_t,
     acc_s,
     acc_t,
     got_s,
@@ -863,38 +942,100 @@
     out_s,
     out_t,
     load_sem,
-    send_sem,
-    recv_sem,
+    a_sem,
+    gu_send,
+    gu_recv,
+    fwd_send,
+    fwd_recv,
+    s_send,
+    s_recv,
+    t_send,
+    t_recv,
 ):
     frames, height, width = dims
-    n_clips, rows, d = a_hbm.shape
+    nc, rows, d = a_hbm.shape[0] // 3, a_hbm.shape[1], a_hbm.shape[2]
     m_ch = v_hbm.shape[2]
     me = lax.axis_index("dp")
     n = lax.axis_size("dp") // 2
     z = lax.div(me, 2)
     core = lax.rem(me, 2)
+    twin = me + 1 - 2 * core
+    inner = jnp.logical_and(z > 0, z < n - 1)
+    outer = jnp.logical_not(inner)
+    step = jnp.where(z < n / 2, 2, -2)
     rows_s, rows_t = o_s.shape[0], o_t.shape[0]
-    piece = got_s.shape[3]
-    n_pieces = m_ch // piece
-    span = acc_s.shape[0]
+    n_pieces = 1 + (m_ch - FIRST) // PIECE
 
     barrier = pltpu.get_barrier_semaphore()
+
+    def greet(device):
+        pl.semaphore_signal(barrier, 1, device_id={"dp": device}, device_id_type=MESH)
+
+    greet(twin)
 
     @pl.when(z > 0)
     def _():
-        pl.semaphore_signal(barrier, 1, device_id={"dp": me - 2}, device_id_type=MESH)
+        greet(me - 2)
 
     @pl.when(z < n - 1)
     def _():
-        pl.semaphore_signal(barrier, 1, device_id={"dp": me + 2}, device_id_type=MESH)
-
-    loads = [
-        pltpu.make_async_copy(src, dst, load_sem.at[i])
-        for i, (src, dst) in enumerate(((a_hbm, a), (gu_hbm, gu), (v_hbm, v), (gr_hbm, gr)))
-    ]
-    for copy in loads:
-        copy.start()
-    loads[0].wait()
+        greet(me + 2)
+
+    load_a = pltpu.make_async_copy(a_hbm, a.at[pl.ds(0, 3 * nc)], load_sem.at[0])
+    ready = 2 * nc + nc // 2
+    load_gu = pltpu.make_async_copy(
+        gu_hbm.at[pl.ds(0, ready)], gu.at[pl.ds(0, ready)], load_sem.at[1]
+    )
+    load_v = pltpu.make_async_copy(v_hbm, v, load_sem.at[2])
+    load_gr = pltpu.make_async_copy(gr_hbm, gr, load_sem.at[3])
+
+    @pl.when(inner)
+    def _():
+        load_a.start()
+        load_gu.start()
+
+    load_v.start()
+    load_gr.start()
+    pl.semaphore_wait(barrier, 3 - jnp.where(z == 0, 1, 0) - jnp.where(z == n - 1, 1, 0))
+
+    def columns(p):
+        if isinstance(p, int) and p == 0:
+            return pl.ds(0, FIRST)
+        return pl.ds(pl.multiple_of(FIRST + (p - 1) * PIECE, 128), PIECE)
+
+    def remote(src, dst, send, recv, device):
+        return pltpu.make_async_remote_copy(
+            src_ref=src,
+            dst_ref=dst,
+            send_sem=send,
+            recv_sem=recv,
+            device_id={"dp": device},
+            device_id_type=MESH,
+        )
+
+    def gu_to_hub(p):
+        s = columns(p)
+        return remote(
+            gu_hbm.at[pl.ds(nc // 2, nc // 2), :, s],
+            gu.at[pl.ds(ready, nc // 2), :, s],
+            gu_send.at[p],
+            gu_recv.at[p],
+            me + step,
+        )
+
+    def gu_to_twin(p):
+        s = columns(p)
+        return remote(
+            gu.at[pl.ds(2 * nc, nc), :, s],
+            gu.at[pl.ds(3 * nc, nc), :, s],
+            fwd_send.at[p],
+            fwd_recv.at[p],
+            twin,
+        )
+
+    a_to_twin = remote(
+        a.at[pl.ds(2 * nc, nc)], a.at[pl.ds(3 * nc, nc)], a_sem.at[0], a_sem.at[1], twin
+    )
 
     def moved(x, before, after, dt, step):
         if not dt:
@@ -907,58 +1048,87 @@
             y = jnp.concatenate([zero, y[:, :-step]], axis=1)
         return y.reshape(rows, 128)
 
-    def transfer(src, dst, dest, p):
-        right = dest > z
-        slot = dest + jnp.where(right, 1, 0)
-        return pltpu.make_async_remote_copy(
-            src_ref=src,
-            dst_ref=dst(slot),
-            send_sem=send_sem.at[dest, p],
-            recv_sem=recv_sem.at[slot, p],
-            device_id={"dp": me + jnp.where(right, 2, -2)},
-            device_id_type=MESH,
-        )
-
-    def settle(dest, acc, start, size, got, out, final, p):
-        at = pl.ds(pl.multiple_of(start, 8), size)
-        from_left = (z > 0) & (dest >= z)
-        from_right = (z < n - 1) & (dest <= z)
-
-        @pl.when(from_left)
-        def _():
-            ref = got(dest + 1)
-            pltpu.make_async_copy(ref, ref, recv_sem.at[dest + 1, p]).wait()
-            acc[at, :] += ref[...].astype(f32)
-
-        @pl.when(from_right)
-        def _():
-            ref = got(dest)
-            pltpu.make_async_copy(ref, ref, recv_sem.at[dest, p]).wait()
-            acc[at, :] += ref[...].astype(f32)
-
-        @pl.when(dest == z)
-        def _():
-            final[...] = acc[at, :]
-
-        @pl.when(dest != z)
-        def _():
-            ref = out(dest)
-            ref[...] = acc[at, :].astype(bf16)
-            transfer(ref, got, dest, p).start()
-
     def place(row0):
         low = lax.div(row0, 128)
         return low, row0 - low * 128
 
-    def job(q, carry):
+    def time_job(q):
         dest = send_order(n, z, q)
-        owner = 2 * dest + core
-
-        low, start = place(owner * rows_s)
+        low, start = place((2 * dest + core) * rows_t)
+
+        def fill_time(i, c):
+            to = pl.ds(pl.multiple_of(i * rows, 16), rows)
+            for j in range(SPAN // 128):
+                chunk = jnp.minimum(low + j, 3 * m_ch // 128 - 1)
+                tap = lax.div(chunk, m_ch // 128)
+                lane = pl.ds(pl.multiple_of((chunk - tap * (m_ch // 128)) * 128, 128), 128)
+
+                def fill(dt):
+                    x = v[i, :, lane].astype(f32)
+                    x = moved(x, 1, rows, dt, height * width)
+                    window_t[to, j * 128 : (j + 1) * 128] = x.astype(bf16)
+
+                lax.switch(tap, [functools.partial(fill, dt) for dt in (-1, 0, 1)])
+            return c
+
+        lax.fori_loop(0, 2 * nc, fill_time, 0)
+        acc_t[...] = lax.dot_general(
+            window_t[...],
+            gr[...].reshape(2 * nc * rows, d),
+            (((0,), (0,)), ((), ())),
+            preferred_element_type=f32,
+        )
+        at = pl.ds(pl.multiple_of(start, 8), rows_t)
+
+        def add(slot):
+            pltpu.make_async_copy(got_t.at[slot], got_t.at[slot], t_recv.at[slot]).wait()
+            acc_t[at, :] += got_t[slot].astype(f32)
+
+        @pl.when((z > 0) & (dest >= z))
+        def _():
+            add(dest + 1)
+
+        @pl.when((z < n - 1) & (dest <= z))
+        def _():
+            add(dest)
+
+        @pl.when(dest == z)
+        def _():
+            o_t[...] = acc_t[at, :]
+
+        @pl.when(dest != z)
+        def _():
+            out_t[dest] = acc_t[at, :].astype(bf16)
+            time_send(dest).start()
+
+    def time_send(dest):
+        right = dest > z
+        slot = dest + jnp.where(right, 1, 0)
+        return remote(
+            out_t.at[dest],
+            got_t.at[slot],
+            t_send.at[dest],
+            t_recv.at[slot],
+            me + jnp.where(right, 2, -2),
+        )
+
+    def hub_dest(k):
+        near = z < n / 2
+        far_out = jnp.where(near, n - 1, 0)
+        own_out = n - 1 - far_out
+        return jnp.where(
+            k == 0, far_out, jnp.where(k == 1, n - 1 - z, jnp.where(k == 2, own_out, z))
+        )
+
+    def space_place(k):
+        return place((2 * hub_dest(k) + core) * rows_s)
+
+    def fill_window(k, first, count):
+        low, start = space_place(k)
 
         def fill_space(i, c):
             to = pl.ds(pl.multiple_of(i * rows, 16), rows)
-            for j in range(span // 128):
+            for j in range(SPAN // 128):
                 chunk = jnp.minimum(low + j, 9 * d // 128 - 1)
                 tap = lax.div(chunk, d // 128)
                 lane = pl.ds(pl.multiple_of((chunk - tap * (d // 128)) * 128, 128), 128)
@@ -968,7 +1138,7 @@
                     if dw:
                         x = pltpu.roll(x, (-dw) % rows, 0)
                     x = moved(x, frames, height * width, dh, width)
-                    window[to, j * 128 : (j + 1) * 128] = x.astype(bf16)
+                    window[k, to, j * 128 : (j + 1) * 128] = x.astype(bf16)
 
                 lax.switch(
                     tap,
@@ -980,96 +1150,167 @@
                 )
             return c
 
-        lax.fori_loop(0, n_clips, fill_space, 0)
-
-        @pl.when(q == 0)
-        def _():
-            loads[1].wait()
-            sides = 2 - jnp.where(z == 0, 1, 0) - jnp.where(z == n - 1, 1, 0)
-            pl.semaphore_wait(barrier, sides)
-
-
-        def space(p, c):
-            s = pl.ds(pl.multiple_of(p * piece, 128), piece)
-            acc_s[...] = lax.dot_general(
-                window[...],
-                gu[:, :, s].reshape(n_clips * rows, piece),
-                (((0,), (0,)), ((), ())), preferred_element_type=f32
-            )
-            settle(
-                dest,
-                acc_s,
-                start,
-                rows_s,
-                lambda slot: got_s.at[slot, p],
-                lambda to: out_s.at[to, p],
-                o_s.at[:, s],
-                p,
-            )
-            return c
-
-        lax.fori_loop(0, n_pieces, space, 0)
-
-        low_t, start_t = place(owner * rows_t)
-
-        def fill_time(i, c):
-            to = pl.ds(pl.multiple_of(i * rows, 16), rows)
-            for j in range(span // 128):
-                chunk = jnp.minimum(low_t + j, 3 * m_ch // 128 - 1)
-                tap = lax.div(chunk, m_ch // 128)
-                lane = pl.ds(pl.multiple_of((chunk - tap * (m_ch // 128)) * 128, 128), 128)
-
-                def fill(dt):
-                    x = v[i, :, lane].astype(f32)
-                    x = moved(x, 1, rows, dt, height * width)
-                    window[to, j * 128 : (j + 1) * 128] = x.astype(bf16)
-
-                lax.switch(tap, [functools.partial(fill, dt) for dt in (-1, 0, 1)])
-            return c
-
-        @pl.when(q == 0)
-        def _():
-            loads[2].wait()
-            loads[3].wait()
-
-        lax.fori_loop(0, n_clips, fill_time, 0)
-        acc_t[...] = lax.dot_general(
-            window[...],
-            gr[...].reshape(n_clips * rows, d),
-            (((0,), (0,)), ((), ())), preferred_element_type=f32
-        )
-        settle(
-            dest,
-            acc_t,
-            start_t,
-            rows_t,
-            lambda slot: got_t.at[slot],
-            lambda to: out_t.at[to],
-            o_t,
-            n_pieces,
-        )
+        lax.fori_loop(first, first + count, fill_space, 0)
+
+    def space_send(k, p):
+        s = columns(p)
+        return remote(
+            out_s.at[k, :, s],
+            got_s.at[jnp.where(k == 1, 1, 0), :, s],
+            s_send.at[k, p],
+            s_recv.at[jnp.where(k == 1, 1, 0), p],
+            me + jnp.where(k == 2, -step, step),
+        )
+
+    def space_job(k, p):
+        s = columns(p)
+        size = FIRST if isinstance(p, int) else PIECE
+        low, start = space_place(k)
+        at = pl.ds(pl.multiple_of(start, 8), rows_s)
+        acc_s[:, :size] = lax.dot_general(
+            window[k],
+            gu[:, :, s].reshape(4 * nc * rows, size),
+            (((0,), (0,)), ((), ())),
+            preferred_element_type=f32,
+        )
+
+        @pl.when(k >= 2)
+        def _():
+            got = got_s.at[k - 2, :, s]
+            pltpu.make_async_copy(got, got, s_recv.at[k - 2, p]).wait()
+            acc_s[at, :size] += got[...].astype(f32)
+
+        @pl.when(k == 3)
+        def _():
+            o_s[:, s] = acc_s[at, :size]
+
+        @pl.when(k < 3)
+        def _():
+            out_s[k, :, s] = acc_s[at, :size].astype(bf16)
+            space_send(k, p).start()
+
+    def take_gu(p):
+        gu_to_hub(p).wait_recv()
+        gu_to_twin(p).start()
+        gu_to_twin(p).wait_recv()
+
+    @pl.when(inner)
+    def _():
+        load_a.wait()
+        a_to_twin.start()
+
+        fill_window(0, 0, 3 * nc)
+        a_to_twin.wait_recv()
+        fill_window(0, 3 * nc, nc)
+        load_gu.wait()
+
+        def pair(first, p):
+            def one(k, c):
+                space_job(k, p)
+                return c
+
+            lax.fori_loop(first, first + 2, one, 0)
+
+        def first_round(k, carry):
+            @pl.when(k == 0)
+            def _():
+                take_gu(0)
+
+            @pl.when(k > 0)
+            def _():
+                fill_window(k, 0, 4 * nc)
+
+            @pl.when(k < 2)
+            def _():
+                space_job(k, 0)
+
+            return carry
+
+        lax.fori_loop(0, 4, first_round, 0)
+        load_v.wait()
+        load_gr.wait()
+
+        def later_round(p, carry):
+            take_gu(p)
+            pair(0, p)
+
+            @pl.when(p < 3)
+            def _():
+                time_job(p - 1)
+
+            @pl.when(p == 1)
+            def _():
+                pair(2, 0)
+
+            @pl.when(p > 1)
+            def _():
+                pair(2, p - 1)
+
+            @pl.when(p == 3)
+            def _():
+                time_job(2)
+
+            return carry
+
+        lax.fori_loop(1, n_pieces, later_round, 0)
+        pair(2, jnp.int32(n_pieces - 1))
+        time_job(3)
+        a_to_twin.wait_send()
+        gu_to_twin(0).wait_send()
+
+        def sent(p, carry):
+            gu_to_twin(p).wait_send()
+            for k in range(3):
+                space_send(k, p).wait_send()
+            return carry
+
+        for k in range(3):
+            space_send(k, 0).wait_send()
+        lax.fori_loop(1, n_pieces, sent, 0)
+
+    @pl.when(outer)
+    def _():
+        gu_to_hub(0).start()
+        gu_to_hub(1).start()
+        load_v.wait()
+        load_gr.wait()
+
+        def round_out(q, carry):
+            time_job(q)
+
+            @pl.when(q == 0)
+            def _():
+                gu_to_hub(2).start()
+
+            @pl.when(q == 1)
+            def _():
+                for p in range(3, n_pieces):
+                    gu_to_hub(p).start()
+
+            return carry
+
+        lax.fori_loop(0, n, round_out, 0)
+
+        for p in range(n_pieces):
+            s = columns(p)
+            got = got_s.at[0, :, s]
+            pltpu.make_async_copy(got, got, s_recv.at[0, p]).wait()
+            o_s[:, s] = got[...].astype(f32)
+            gu_to_hub(p).wait_send()
+
+    def finish(q, carry):
+        time_send(send_order(n, z, q)).wait_send()
         return carry
 
-    lax.fori_loop(0, n, job, 0)
-
-    def finish(q, carry):
-        dest = send_order(n, z, q)
-        for p in range(n_pieces):
-            transfer(out_s.at[dest, p], lambda slot: got_s.at[slot, p], dest, p).wait_send()
-        transfer(out_t.at[dest], lambda slot: got_t.at[slot], dest, n_pieces).wait_send()
-        return carry
-
     lax.fori_loop(0, n - 1, finish, 0)
 
 
 def gradients(dims, n_dp, a, v, gu, gr):
-    n_clips, rows, d = a.shape
+    nc, rows, d = a.shape[0] // 3, a.shape[1], a.shape[2]
     m_ch = v.shape[2]
     rows_s, rows_t = 9 * d // n_dp, 3 * m_ch // n_dp
     n = n_dp // 2
-    piece = 384
-    n_pieces = m_ch // piece
-    span = 640
+    n_pieces = 1 + (m_ch - FIRST) // PIECE
     shape = jax.ShapeDtypeStruct
     dma = pltpu.SemaphoreType.DMA
     return pl.pallas_call(
@@ -1078,23 +1319,31 @@
         in_specs=[pl.BlockSpec(memory_space=pl.ANY)] * 4,
         out_specs=[pl.BlockSpec(memory_space=pltpu.VMEM)] * 2,
         scratch_shapes=[
-            pltpu.VMEM(a.shape, bf16),
+            pltpu.VMEM((4 * nc, rows, d), bf16),
             pltpu.VMEM(v.shape, bf16),
-            pltpu.VMEM(gu.shape, bf16),
+            pltpu.VMEM((4 * nc, rows, m_ch), bf16),
             pltpu.VMEM(gr.shape, bf16),
-            pltpu.VMEM((n_clips * rows, span), bf16),
-            pltpu.VMEM((span, piece), f32),
-            pltpu.VMEM((span, d), f32),
-            pltpu.VMEM((n + 1, n_pieces, rows_s, piece), bf16),
+            pltpu.VMEM((4, 4 * nc * rows, SPAN), bf16),
+            pltpu.VMEM((2 * nc * rows, SPAN), bf16),
+            pltpu.VMEM((SPAN, PIECE), f32),
+            pltpu.VMEM((SPAN, d), f32),
+            pltpu.VMEM((2, rows_s, m_ch), bf16),
             pltpu.VMEM((n + 1, rows_t, d), bf16),
-            pltpu.VMEM((n, n_pieces, rows_s, piece), bf16),
+            pltpu.VMEM((3, rows_s, m_ch), bf16),
             pltpu.VMEM((n, rows_t, d), bf16),
             dma((4,)),
-            dma((n, n_pieces + 1)),
-            dma((n + 1, n_pieces + 1)),
+            dma((2,)),
+            dma((n_pieces,)),
+            dma((n_pieces,)),
+            dma((n_pieces,)),
+            dma((n_pieces,)),
+            dma((3, n_pieces)),
+            dma((2, n_pieces)),
+            dma((n,)),
+            dma((n + 1,)),
         ],
         compiler_params=pltpu.CompilerParams(
-            collective_id=1, has_side_effects=True, vmem_limit_bytes=40 * 2**20
+            collective_id=1, has_side_effects=True, vmem_limit_bytes=62 * 2**20
         ),
     )(a, v, gu, gr)
 
@@ -1143,9 +1392,12 @@
         x = jnp.pad(x, ((0, 0), (0, 0), (0, 0), (0, width - breadth), (0, 0)))
         return x.reshape(MB, rows, d)
 
+    n_dp = lax.axis_size("dp")
+    hubs = n_dp == 8 and 9 * d // n_dp == 576 and 3 * m_ch // n_dp == 432 and d % 128 == 0
     act, grad, a_in, hidden, gu, gr, gain_s, shift_s, gain_t, shift_t = relay(
         (cm, frames, height, width),
-        lax.axis_size("dp"),
+        n_dp,
+        hubs,
         padded(clips),
         boxes,
         spatial_w[0],
@@ -1160,14 +1412,12 @@
     def frames_of(x):
         return x.reshape(n_clips, frames, height, width, x.shape[-1])[:, :, :, :breadth]
 
-    n_dp = lax.axis_size("dp")
-    rows_s, rows_t = 9 * d // n_dp, 3 * m_ch // n_dp
-    if rows_s % 64 == 0 and rows_t % 16 == 0 and rows_s <= 576 and rows_t <= 528 and n_dp <= 8:
+    if hubs:
         clip_rows = frames * height * width
         grad_s, grad_t = gradients(
             (frames, height, width),
             n_dp,
-            *[x.reshape(2 * n_clips, clip_rows, x.shape[-1]) for x in (a_in, hidden, gu, gr)],
+            *[x.reshape(-1, clip_rows, x.shape[-1]) for x in (a_in, hidden, gu, gr)],
         )
     else:
         cells = n_clips * frames * height * breadth

time: 348 us -> 328 us (0.943); the launches traced: 348 us -> 324 us
  Pallas kernels: 332 us -> 310 us
    pallas_call x1, Pallas kernels: 125 us -> 102 us  [gradients(): pl.pallas_call(functools.partial(gradient_kernel, dims), out_shape=(shape...]
    unnamed x24 -> x20, local copies, waits for them, and re-layouts: 10 us -> 8.32 us
where the time goes in v5:
time: 328 us; the launch traced here: 324 us
  Pallas kernels  310 us (95%)
  local copies, waits for them, and re-layouts  14.1 us (4%)
    pallas_call x1, Pallas kernels, relay(): pl.pallas_call(functools.partial(relay_kernel, dims), out_shape=(shape((M...  208 us
    pallas_call x1, Pallas kernels, gradients(): pl.pallas_call(functools.partial(gradient_kernel, dims), out_shape=(shape...  102 us
    unnamed x20, local copies, waits for them, and re-layouts  8.32 us

profile of v5, /device:TPU:0, one launch (start us, length us, event | category | flops | bytes accessed | tf_op | source)
XLA Modules:
  0.0 324.4 jit_solution(5328013710754091759)
XLA Ops:
  0.6 0.0 copy-start.1
  0.6 1.4 copy.23
  2.0 1.1 pad.7.clone
  3.1 0.0 copy-done.1
  3.1 0.2 copy.24
  3.3 1.1 pad.8.clone
  4.4 207.6 %shard_map.152 = (bf16[4,224,512]{2,1,0:T(8,128)(2,1)}, bf16[4,224,512]{2,1,0:T(8,128)(2,1)}, bf16[3,4,224,512]{3,2,1,0:T(8,128)(2,1)}, bf16[2,4,224,1152]{3,2,1...) custom-call(bf16[4,224,512]{2,1,0:T(8,128)(2,1)} %bitcast.21, ...), custom_call_target="tpu_custom_call" | custom-call | tf_op jit(solution)/shard_map/pallas_call | solution.py:837
  212.0 3.5 %copy_bitcast_fusion = (bf16[1,4,4,7,7,512]{5,2,4,3,1,0:T(4,128)(2,1)}, bf16[1,4,4,7,7,512]{5,2,4,3,1,0:T(4,128)(2,1)}) fusion(bf16[4,4,7,7,512]{4,3,2,1,0:T(8,128)(2,1)} %bitcast.28, bf16[4,4,7,7,512]{4,3,2,1,0:T(8,128)(2,1)} %bitcast.27), kind=kLoop, calls=%fused_computation | loop fusion | bytes 3211264 | tf_op jit(solution)/shard_map/broadcast_in_dim | solution.py:1432
  215.5 102.0 %shard_map.153 = (f32[576,1152]{1,0:T(8,128)}, f32[432,512]{1,0:T(8,128)}) custom-call(bf16[12,224,512]{2,1,0:T(8,128)(2,1)} %bitcast.24, bf16[8,224,1152]{2,1,0:T(8,128)(2,1)} %bitcast.20, bf16[12,224,1152]{2,1,0:T(8,128)(2,1)} %bitcast.19, bf16[8,224,512]{2,1,0:T(8,128)(2,1)} %bitcast.26), custom_call_target="tpu_custom_call" | custom-call | tf_op jit(solution)/shard_map/pallas_call | solution.py:1316
  317.5 0.0 copy-start
  317.6 0.0 copy-start.3
  317.6 0.0 copy-start.2
  317.6 0.0 copy-start.5
  317.6 0.0 copy-start.4
  317.6 3.5 %copy.33 = f32[1,576,1152]{2,1,0:T(8,128)} copy(f32[1,576,1152]{2,1,0:T(8,128)} %bitcast.25) | data formatting | bytes 5308416
  321.1 0.0 copy-done
  321.1 0.9 copy.34
  322.0 0.0 copy-done.3
  322.0 0.6 copy.35
  322.6 0.0 copy-done.2
  322.6 0.6 copy.36
  323.2 0.0 copy-done.5
  323.2 0.6 copy.37
  323.8 0.0 copy-done.4
  323.8 0.6 copy.38
Async XLA Ops:
  0.6 2.5 copy-start.1
  317.5 3.5 %copy-start = (f32[432,512]{1,0:T(8,128)S(1)}, f32[432,512]{1,0:T(8,128)}, u32[]{:S(2)}) copy-start(f32[432,512]{1,0:T(8,128)} %get-tuple-element.27) | copy-start | bytes 2654212
  317.6 4.5 %copy-start.3 = (f32[1,1152]{1,0:T(1,128)S(1)}, f32[1,1152]{1,0:T(1,128)}, u32[]{:S(2)}) copy-start(f32[1,1152]{1,0:T(1,128)} %get-tuple-element.46) | copy-start | bytes 13828
  317.6 5.0 %copy-start.2 = (f32[1,1152]{1,0:T(1,128)S(1)}, f32[1,1152]{1,0:T(1,128)}, u32[]{:S(2)}) copy-start(f32[1,1152]{1,0:T(1,128)} %get-tuple-element.47) | copy-start | bytes 13828
  317.6 5.6 %copy-start.5 = (f32[1,512]{1,0:T(1,128)S(1)}, f32[1,512]{1,0:T(1,128)}, u32[]{:S(2)}) copy-start(f32[1,512]{1,0:T(1,128)} %get-tuple-element.48) | copy-start | bytes 6148
  317.6 6.2 %copy-start.4 = (f32[1,512]{1,0:T(1,128)S(1)}, f32[1,512]{1,0:T(1,128)}, u32[]{:S(2)}) copy-start(f32[1,512]{1,0:T(1,128)} %get-tuple-element.49) | copy-start | bytes 6148

commit v6 on v5

--- a/solution.py
+++ b/solution.py
@@ -916,9 +916,34 @@
     return dest
 
 
-FIRST = 128
-PIECE = 256
+PIECE = 384
 SPAN = 640
+
+HUB_JOBS = (
+    (0, 0, -1),
+    (0, 1, 0),
+    (1, 0, -1),
+    (2, 0, -1),
+    (0, 2, 1),
+    (2, 1, -1),
+    (1, 1, -1),
+    (1, 2, -1),
+    (3, 0, 2),
+    (2, 2, 3),
+    (3, 1, -1),
+    (3, 2, -1),
+)
+
+
+def of_job(j, column):
+    return sum(jnp.where(j == i, job[column], 0) for i, job in enumerate(HUB_JOBS))
+
+
+def is_one_of(j, members):
+    found = j < 0
+    for i in members:
+        found = found | (j == i)
+    return found
 
 
 def gradient_kernel(
@@ -964,7 +989,7 @@
     outer = jnp.logical_not(inner)
     step = jnp.where(z < n / 2, 2, -2)
     rows_s, rows_t = o_s.shape[0], o_t.shape[0]
-    n_pieces = 1 + (m_ch - FIRST) // PIECE
+    n_pieces = m_ch // PIECE
 
     barrier = pltpu.get_barrier_semaphore()
 
@@ -999,9 +1024,7 @@
     pl.semaphore_wait(barrier, 3 - jnp.where(z == 0, 1, 0) - jnp.where(z == n - 1, 1, 0))
 
     def columns(p):
-        if isinstance(p, int) and p == 0:
-            return pl.ds(0, FIRST)
-        return pl.ds(pl.multiple_of(FIRST + (p - 1) * PIECE, 128), PIECE)
+        return pl.ds(pl.multiple_of(p * PIECE, 128), PIECE)
 
     def remote(src, dst, send, recv, device):
         return pltpu.make_async_remote_copy(
@@ -1164,12 +1187,11 @@
 
     def space_job(k, p):
         s = columns(p)
-        size = FIRST if isinstance(p, int) else PIECE
         low, start = space_place(k)
         at = pl.ds(pl.multiple_of(start, 8), rows_s)
-        acc_s[:, :size] = lax.dot_general(
+        acc_s[...] = lax.dot_general(
             window[k],
-            gu[:, :, s].reshape(4 * nc * rows, size),
+            gu[:, :, s].reshape(4 * nc * rows, PIECE),
             (((0,), (0,)), ((), ())),
             preferred_element_type=f32,
         )
@@ -1178,15 +1200,15 @@
         def _():
             got = got_s.at[k - 2, :, s]
             pltpu.make_async_copy(got, got, s_recv.at[k - 2, p]).wait()
-            acc_s[at, :size] += got[...].astype(f32)
+            acc_s[at, :] += got[...].astype(f32)
 
         @pl.when(k == 3)
         def _():
-            o_s[:, s] = acc_s[at, :size]
+            o_s[:, s] = acc_s[at, :]
 
         @pl.when(k < 3)
         def _():
-            out_s[k, :, s] = acc_s[at, :size].astype(bf16)
+            out_s[k, :, s] = acc_s[at, :].astype(bf16)
             space_send(k, p).start()
 
     def take_gu(p):
@@ -1199,64 +1221,42 @@
         load_a.wait()
         a_to_twin.start()
 
-        fill_window(0, 0, 3 * nc)
         a_to_twin.wait_recv()
-        fill_window(0, 3 * nc, nc)
-        load_gu.wait()
-
-        def pair(first, p):
-            def one(k, c):
-                space_job(k, p)
-                return c
-
-            lax.fori_loop(first, first + 2, one, 0)
-
-        def first_round(k, carry):
-            @pl.when(k == 0)
-            def _():
-                take_gu(0)
-
-            @pl.when(k > 0)
+
+        new_k = [i for i, job in enumerate(HUB_JOBS) if job[0] not in [x[0] for x in HUB_JOBS[:i]]]
+        new_p = [i for i, job in enumerate(HUB_JOBS) if job[1] not in [x[1] for x in HUB_JOBS[:i]]]
+        timed = [i for i, job in enumerate(HUB_JOBS) if job[2] >= 0]
+
+        def hub_job(j, carry):
+            k, p = of_job(j, 0), of_job(j, 1)
+
+            @pl.when(is_one_of(j, new_k))
             def _():
                 fill_window(k, 0, 4 * nc)
 
-            @pl.when(k < 2)
-            def _():
-                space_job(k, 0)
+            @pl.when(j == 0)
+            def _():
+                load_gu.wait()
+
+            @pl.when(is_one_of(j, new_p))
+            def _():
+                take_gu(p)
+
+            space_job(k, p)
+
+            @pl.when(j == timed[0])
+            def _():
+                load_v.wait()
+                load_gr.wait()
+
+            @pl.when(is_one_of(j, timed))
+            def _():
+                time_job(of_job(j, 2))
 
             return carry
 
-        lax.fori_loop(0, 4, first_round, 0)
-        load_v.wait()
-        load_gr.wait()
-
-        def later_round(p, carry):
-            take_gu(p)
-            pair(0, p)
-
-            @pl.when(p < 3)
-            def _():
-                time_job(p - 1)
-
-            @pl.when(p == 1)
-            def _():
-                pair(2, 0)
-
-            @pl.when(p > 1)
-            def _():
-                pair(2, p - 1)
-
-            @pl.when(p == 3)
-            def _():
-                time_job(2)
-
-            return carry
-
-        lax.fori_loop(1, n_pieces, later_round, 0)
-        pair(2, jnp.int32(n_pieces - 1))
-        time_job(3)
+        lax.fori_loop(0, len(HUB_JOBS), hub_job, 0)
         a_to_twin.wait_send()
-        gu_to_twin(0).wait_send()
 
         def sent(p, carry):
             gu_to_twin(p).wait_send()
@@ -1264,9 +1264,7 @@
                 space_send(k, p).wait_send()
             return carry
 
-        for k in range(3):
-            space_send(k, 0).wait_send()
-        lax.fori_loop(1, n_pieces, sent, 0)
+        lax.fori_loop(0, n_pieces, sent, 0)
 
     @pl.when(outer)
     def _():
@@ -1280,11 +1278,7 @@
 
             @pl.when(q == 0)
             def _():
-                gu_to_hub(2).start()
-
-            @pl.when(q == 1)
-            def _():
-                for p in range(3, n_pieces):
+                for p in range(2, n_pieces):
                     gu_to_hub(p).start()
 
             return carry
@@ -1310,7 +1304,7 @@
     m_ch = v.shape[2]
     rows_s, rows_t = 9 * d // n_dp, 3 * m_ch // n_dp
     n = n_dp // 2
-    n_pieces = 1 + (m_ch - FIRST) // PIECE
+    n_pieces = m_ch // PIECE
     shape = jax.ShapeDtypeStruct
     dma = pltpu.SemaphoreType.DMA
     return pl.pallas_call(

time: 328 us -> 319 us (0.973)
  the two profiles are of different devices: /device:TPU:0 before, /device:TPU:11 now
where the time goes in v6:
time: 319 us
  Pallas kernels  304 us (95%)
  local copies, waits for them, and re-layouts  14.1 us (4%)
    pallas_call x1, Pallas kernels, relay(): pl.pallas_call(functools.partial(relay_kernel, dims), out_shape=(shape((M...  207 us
    pallas_call x1, Pallas kernels, gradients(): pl.pallas_call(functools.partial(gradient_kernel, dims), out_shape=(shape...  97.2 us
    unnamed x20, local copies, waits for them, and re-layouts  8.32 us

profile of v6, /device:TPU:11, one launch (start us, length us, event | category | flops | bytes accessed | tf_op | source)
XLA Modules:
  0.0 319.1 jit_solution(710543611405975553)
XLA Ops:
  0.6 0.0 copy-start.1
  0.6 1.4 copy.23
  2.0 1.1 pad.7.clone
  3.1 0.0 copy-done.1
  3.1 0.2 copy.24
  3.3 1.1 pad.8.clone
  4.4 207.1 %shard_map.152 = (bf16[4,224,512]{2,1,0:T(8,128)(2,1)}, bf16[4,224,512]{2,1,0:T(8,128)(2,1)}, bf16[3,4,224,512]{3,2,1,0:T(8,128)(2,1)}, bf16[2,4,224,1152]{3,2,1...) custom-call(bf16[4,224,512]{2,1,0:T(8,128)(2,1)} %bitcast.21, ...), custom_call_target="tpu_custom_call" | custom-call | tf_op jit(solution)/shard_map/pallas_call | solution.py:837
  211.6 3.5 %copy_bitcast_fusion = (bf16[1,4,4,7,7,512]{5,2,4,3,1,0:T(4,128)(2,1)}, bf16[1,4,4,7,7,512]{5,2,4,3,1,0:T(4,128)(2,1)}) fusion(bf16[4,4,7,7,512]{4,3,2,1,0:T(8,128)(2,1)} %bitcast.28, bf16[4,4,7,7,512]{4,3,2,1,0:T(8,128)(2,1)} %bitcast.27), kind=kLoop, calls=%fused_computation | loop fusion | bytes 3211264 | tf_op jit(solution)/shard_map/broadcast_in_dim | solution.py:1426
  215.1 97.2 %shard_map.153 = (f32[576,1152]{1,0:T(8,128)}, f32[432,512]{1,0:T(8,128)}) custom-call(bf16[12,224,512]{2,1,0:T(8,128)(2,1)} %bitcast.24, bf16[8,224,1152]{2,1,0:T(8,128)(2,1)} %bitcast.20, bf16[12,224,1152]{2,1,0:T(8,128)(2,1)} %bitcast.19, bf16[8,224,512]{2,1,0:T(8,128)(2,1)} %bitcast.26), custom_call_target="tpu_custom_call" | custom-call | tf_op jit(solution)/shard_map/pallas_call | solution.py:1310
  312.2 0.0 copy-start
  312.3 0.0 copy-start.3
  312.3 0.0 copy-start.2
  312.3 0.0 copy-start.5
  312.3 0.0 copy-start.4
  312.3 3.5 %copy.33 = f32[1,576,1152]{2,1,0:T(8,128)} copy(f32[1,576,1152]{2,1,0:T(8,128)} %bitcast.25) | data formatting | bytes 5308416
  315.8 0.0 copy-done
  315.8 0.9 copy.34
  316.7 0.0 copy-done.3
  316.7 0.6 copy.35
  317.3 0.0 copy-done.2
  317.3 0.6 copy.36
  317.9 0.0 copy-done.5
  317.9 0.6 copy.37
  318.5 0.0 copy-done.4
  318.5 0.6 copy.38
Async XLA Ops:
  0.6 2.5 copy-start.1
  312.2 3.5 %copy-start = (f32[432,512]{1,0:T(8,128)S(1)}, f32[432,512]{1,0:T(8,128)}, u32[]{:S(2)}) copy-start(f32[432,512]{1,0:T(8,128)} %get-tuple-element.27) | copy-start | bytes 2654212
  312.3 4.5 %copy-start.3 = (f32[1,1152]{1,0:T(1,128)S(1)}, f32[1,1152]{1,0:T(1,128)}, u32[]{:S(2)}) copy-start(f32[1,1152]{1,0:T(1,128)} %get-tuple-element.46) | copy-start | bytes 13828
  312.3 5.0 %copy-start.2 = (f32[1,1152]{1,0:T(1,128)S(1)}, f32[1,1152]{1,0:T(1,128)}, u32[]{:S(2)}) copy-start(f32[1,1152]{1,0:T(1,128)} %get-tuple-element.47) | copy-start | bytes 13828
  312.3 5.6 %copy-start.5 = (f32[1,512]{1,0:T(1,128)S(1)}, f32[1,512]{1,0:T(1,128)}, u32[]{:S(2)}) copy-start(f32[1,512]{1,0:T(1,128)} %get-tuple-element.48) | copy-start | bytes 6148
  312.3 6.2 %copy-start.4 = (f32[1,512]{1,0:T(1,128)S(1)}, f32[1,512]{1,0:T(1,128)}, u32[]{:S(2)}) copy-start(f32[1,512]{1,0:T(1,128)} %get-tuple-element.49) | copy-start | bytes 6148

commit v7 on v6

--- a/solution.py
+++ b/solution.py
@@ -217,23 +217,6 @@
         return carry
 
     lax.fori_loop(0, MB, make_keep, 0)
-    sides = 3 - jnp.where(first, 1, 0) - jnp.where(last, 1, 0)
-    pl.semaphore_wait(barrier, sides * n_dp)
-
-    def send_scale():
-        return pltpu.make_async_remote_copy(
-            src_ref=scale_out,
-            dst_ref=scale_in,
-            send_sem=w_sem.at[19],
-            recv_sem=w_sem.at[20],
-            device_id={"pipe": section + 1},
-            device_id_type=MESH,
-        )
-
-    @pl.when(jnp.logical_not(last))
-    def _():
-        send_scale().start()
-
     def share(kind, buf, m):
         def send(j, carry):
             pltpu.make_async_remote_copy(
@@ -319,8 +302,8 @@
                 to_hub(m).start()
 
     def gu_to_hub(part):
-        m = min(part, 1)
-        s = (pl.ds(0, m_ch), pl.ds(0, 640), pl.ds(640, m_ch - 640))[part]
+        m = max(part - 1, 0)
+        s = (pl.ds(0, 640), pl.ds(640, m_ch - 640), pl.ds(0, PIECE))[min(part, 2)]
         return pltpu.make_async_remote_copy(
             src_ref=gu.at[m, :, s],
             dst_ref=o_gu.at[2, m, :, s],
@@ -425,32 +408,17 @@
         def _():
             a_in[m, :, s] = (keep[m] * silu(value)).astype(bf16)
 
-    def forward_spatial(m):
-        @pl.when(first)
-        def _():
-            load_clip(m).wait()
-
-        @pl.when(jnp.logical_not(first))
-        def _():
-            @pl.when(m == 0)
-            def _():
-                send_scale().wait_recv()
-
-            @pl.when(local_skip)
-            def _():
-                load_skip(m).wait()
-
-            crossed(4, x_p, m)
-
+    def spatial_conv(m, begins):
         for part in range(2):
-
-            @pl.when(jnp.logical_not(first))
-            def _():
-                half_to_pipe(2, part, r_out, r_in, m, 1).wait_recv()
-                lane_chunks(half, functools.partial(activate, m, part))
+            if not begins:
+
+                @pl.when(jnp.logical_not(first))
+                def _():
+                    half_to_pipe(2, part, r_out, r_in, m, 1).wait_recv()
+                    lane_chunks(half, functools.partial(activate, m, part))
 
             def column(i, s):
-                s = pl.ds(pl.multiple_of(part * half + i * 128, 128), 128)
+                s = lanes_of(part, i)
                 x = a_in[m, :, s].astype(f32)
                 for dw in (-1, 0, 1):
                     y = shift_space(x, 0, dw)
@@ -462,9 +430,7 @@
                         )
 
             lane_chunks(half, column)
-
-            @pl.when((m == 0) & first)
-            def _():
+            if begins:
                 for tap in range(9):
                     load_ws(part, tap).wait()
 
@@ -475,6 +441,49 @@
                     uh[m, :, s] = value
                 else:
                     uh[m, :, s] += value
+
+    @pl.when(first)
+    def _():
+        load_clip(0).wait()
+        spatial_conv(0, True)
+
+    sides = 3 - jnp.where(first, 1, 0) - jnp.where(last, 1, 0)
+    pl.semaphore_wait(barrier, sides * n_dp)
+
+    def send_scale():
+        return pltpu.make_async_remote_copy(
+            src_ref=scale_out,
+            dst_ref=scale_in,
+            send_sem=w_sem.at[19],
+            recv_sem=w_sem.at[20],
+            device_id={"pipe": section + 1},
+            device_id_type=MESH,
+        )
+
+    @pl.when(jnp.logical_not(last))
+    def _():
+        send_scale().start()
+
+    def forward_spatial(m):
+        @pl.when(first & (m > 0))
+        def _():
+            load_clip(m).wait()
+
+        @pl.when(jnp.logical_not(first))
+        def _():
+            @pl.when(m == 0)
+            def _():
+                send_scale().wait_recv()
+
+            @pl.when(local_skip)
+            def _():
+                load_skip(m).wait()
+
+            crossed(4, x_p, m)
+
+        @pl.when(jnp.logical_not(first & (m == 0)))
+        def _():
+            spatial_conv(m, False)
 
         x_s[m, me, :, 2 * m_ch :] = cnt[m]
 
@@ -645,9 +654,9 @@
         lane_chunks(m_ch, column)
         share_operand(5, gu, o_gu, m)
         if hubs:
-            for part in range(2):
-
-                @pl.when(outer & first & (m == part))
+            for part, when in ((0, 0), (1, 0), (3, 2)):
+
+                @pl.when(outer & first & (m == when))
                 def _():
                     gu_to_hub(part).start()
 
@@ -735,32 +744,56 @@
 
                 lax.fori_loop(0, 2, one, 0)
 
+        def some(begin, end, m):
+            def spatial(j, c):
+                backward_spatial(m + j)
+                return c
+
+            def skip(j, c):
+                send_skip_grad(m + j)
+                return c
+
+            lax.fori_loop(begin, end, spatial, 0)
+
+            @pl.when(jnp.logical_not(early))
+            def _():
+                lax.fori_loop(begin, end, skip, 0)
+
         inner = jnp.logical_not(last)
         done_f = jnp.logical_and(s > 0, s <= pairs)
         md = 2 * jnp.clip(s - 1, 0, pairs - 1)
         both(jnp.logical_and(done_f, last), forward_out, md)
         both(jnp.logical_and(do_b, last), backward_in, mb)
+        some(1, jnp.where(last & do_b & (s > wait_back), 2, 1), mb - 2)
         both(do_f, forward_spatial, mf)
         both(jnp.logical_and(done_f, inner), forward_out, md)
         both(do_b, backward_temporal, mb)
         if hubs:
 
-            @pl.when(outer & (s == wait_back + 1) & first)
+            @pl.when(outer & first & (s == wait_back + 1))
             def _():
                 gu_to_hub(2).start()
 
         both(do_f, forward_temporal, mf)
-        both(do_b, backward_spatial, mb)
-        both(jnp.logical_and(do_b, jnp.logical_not(early)), send_skip_grad, mb)
+        ends = s == wait_back + pairs - 1
+        some(0, jnp.where(do_b, jnp.where(last & jnp.logical_not(ends), 1, 2), 0), mb)
         if hubs:
 
             @pl.when(s == jnp.where(last, wait_back + 1, pairs - 1))
             def _():
                 inputs_to_hub()
 
-            @pl.when(outer & (s == wait_back + 1) & jnp.logical_not(first))
-            def _():
-                for part in range(3):
+            @pl.when(outer & (section == 1) & (s == wait_back))
+            def _():
+                gu_to_hub(0).start()
+
+            @pl.when(outer & (section > 1) & (s == wait_back + 1))
+            def _():
+                gu_to_hub(0).start()
+
+            @pl.when(outer & jnp.logical_not(first) & (s == wait_back + 1))
+            def _():
+                for part in range(1, MB):
                     gu_to_hub(part).start()
 
         return carry
@@ -804,19 +837,21 @@
 
     lax.fori_loop(0, MB, finish, 0)
     if hubs:
-        for m in range(MB):
-
-            @pl.when(outer)
-            def _():
+
+
+        @pl.when(outer)
+        def _():
+            for m in range(MB):
                 to_hub(m).wait_send()
-                if m < 3:
-                    gu_to_hub(m).wait_send()
-
-            @pl.when(jnp.logical_not(outer))
-            def _():
+            for part in range(MB):
+                gu_to_hub(part).wait_send()
+
+        @pl.when(jnp.logical_not(outer))
+        def _():
+            for m in range(MB):
                 to_hub(m).wait_recv()
-                if m < 3:
-                    gu_to_hub(m).wait_recv()
+            for part in range(MB):
+                gu_to_hub(part).wait_recv()
 
     @pl.when(jnp.logical_not(last))
     def _():
@@ -1007,10 +1042,13 @@
         greet(me + 2)
 
     load_a = pltpu.make_async_copy(a_hbm, a.at[pl.ds(0, 3 * nc)], load_sem.at[0])
-    ready = 2 * nc + nc // 2
+    full = 2 * nc + nc // MB
     load_gu = pltpu.make_async_copy(
-        gu_hbm.at[pl.ds(0, ready)], gu.at[pl.ds(0, ready)], load_sem.at[1]
+        gu_hbm.at[pl.ds(0, full)], gu.at[pl.ds(0, full)], load_sem.at[1]
     )
+    late = 3 * nc - nc // MB
+    early = (pl.ds(full, late - full), slice(None), pl.ds(0, PIECE))
+    load_early = pltpu.make_async_copy(gu_hbm.at[early], gu.at[early], load_sem.at[4])
     load_v = pltpu.make_async_copy(v_hbm, v, load_sem.at[2])
     load_gr = pltpu.make_async_copy(gr_hbm, gr, load_sem.at[3])
 
@@ -1018,6 +1056,7 @@
     def _():
         load_a.start()
         load_gu.start()
+        load_early.start()
 
     load_v.start()
     load_gr.start()
@@ -1039,10 +1078,20 @@
     def gu_to_hub(p):
         s = columns(p)
         return remote(
-            gu_hbm.at[pl.ds(nc // 2, nc // 2), :, s],
-            gu.at[pl.ds(ready, nc // 2), :, s],
+            gu_hbm.at[pl.ds(nc // MB, nc - nc // MB), :, s],
+            gu.at[pl.ds(full, nc - nc // MB), :, s],
             gu_send.at[p],
             gu_recv.at[p],
+            me + step,
+        )
+
+    def first_to_hub():
+        s = pl.ds(0, PIECE)
+        return remote(
+            gu_hbm.at[pl.ds(late - 2 * nc, nc // MB), :, s],
+            gu.at[pl.ds(late, nc // MB), :, s],
+            gu_send.at[0],
+            gu_recv.at[0],
             me + step,
         )
 
@@ -1212,7 +1261,14 @@
             space_send(k, p).start()
 
     def take_gu(p):
-        gu_to_hub(p).wait_recv()
+        @pl.when(p == 0)
+        def _():
+            first_to_hub().wait_recv()
+
+        @pl.when(p > 0)
+        def _():
+            gu_to_hub(p).wait_recv()
+
         gu_to_twin(p).start()
         gu_to_twin(p).wait_recv()
 
@@ -1237,6 +1293,7 @@
             @pl.when(j == 0)
             def _():
                 load_gu.wait()
+                load_early.wait()
 
             @pl.when(is_one_of(j, new_p))
             def _():
@@ -1268,7 +1325,7 @@
 
     @pl.when(outer)
     def _():
-        gu_to_hub(0).start()
+        first_to_hub().start()
         gu_to_hub(1).start()
         load_v.wait()
         load_gr.wait()
@@ -1290,7 +1347,7 @@
             got = got_s.at[0, :, s]
             pltpu.make_async_copy(got, got, s_recv.at[0, p]).wait()
             o_s[:, s] = got[...].astype(f32)
-            gu_to_hub(p).wait_send()
+            (gu_to_hub(p) if p else first_to_hub()).wait_send()
 
     def finish(q, carry):
         time_send(send_order(n, z, q)).wait_send()
@@ -1325,7 +1382,7 @@
             pltpu.VMEM((n + 1, rows_t, d), bf16),
             pltpu.VMEM((3, rows_s, m_ch), bf16),
             pltpu.VMEM((n, rows_t, d), bf16),
-            dma((4,)),
+            dma((5,)),
             dma((2,)),
             dma((n_pieces,)),
             dma((n_pieces,)),

time: 319 us -> 314 us (0.984)
  the two profiles are of different devices: /device:TPU:11 before, /device:TPU:0 now
where the time goes in v7:
time: 314 us; the launch traced here: 312 us
  Pallas kernels  297 us (95%)
  local copies, waits for them, and re-layouts  14.1 us (4%)
    pallas_call x1, Pallas kernels, relay(): pl.pallas_call(functools.partial(relay_kernel, dims), out_shape=(shape((M...  208 us
    pallas_call x1, Pallas kernels, gradients(): pl.pallas_call(functools.partial(gradient_kernel, dims), out_shape=(shape...  88.7 us
    unnamed x20, local copies, waits for them, and re-layouts  8.32 us

profile of v7, /device:TPU:0, one launch (start us, length us, event | category | flops | bytes accessed | tf_op | source)
XLA Modules:
  0.0 311.6 jit_solution(7571989623750934588)
XLA Ops:
  0.6 0.0 copy-start.1
  0.6 1.4 copy.23
  2.0 1.1 pad.7.clone
  3.1 0.0 copy-done.1
  3.1 0.2 copy.24
  3.3 1.1 pad.8.clone
  4.4 208.1 %shard_map.152 = (bf16[4,224,512]{2,1,0:T(8,128)(2,1)}, bf16[4,224,512]{2,1,0:T(8,128)(2,1)}, bf16[3,4,224,512]{3,2,1,0:T(8,128)(2,1)}, bf16[2,4,224,1152]{3,2,1...) custom-call(bf16[4,224,512]{2,1,0:T(8,128)(2,1)} %bitcast.21, ...), custom_call_target="tpu_custom_call" | custom-call | tf_op jit(solution)/shard_map/pallas_call | solution.py:872
  212.6 3.5 %copy_bitcast_fusion = (bf16[1,4,4,7,7,512]{5,2,4,3,1,0:T(4,128)(2,1)}, bf16[1,4,4,7,7,512]{5,2,4,3,1,0:T(4,128)(2,1)}) fusion(bf16[4,4,7,7,512]{4,3,2,1,0:T(8,128)(2,1)} %bitcast.28, bf16[4,4,7,7,512]{4,3,2,1,0:T(8,128)(2,1)} %bitcast.27), kind=kLoop, calls=%fused_computation | loop fusion | bytes 3211264 | tf_op jit(solution)/shard_map/broadcast_in_dim | solution.py:1483
  216.1 88.7 %shard_map.153 = (f32[576,1152]{1,0:T(8,128)}, f32[432,512]{1,0:T(8,128)}) custom-call(bf16[12,224,512]{2,1,0:T(8,128)(2,1)} %bitcast.24, bf16[8,224,1152]{2,1,0:T(8,128)(2,1)} %bitcast.20, bf16[12,224,1152]{2,1,0:T(8,128)(2,1)} %bitcast.19, bf16[8,224,512]{2,1,0:T(8,128)(2,1)} %bitcast.26), custom_call_target="tpu_custom_call" | custom-call | tf_op jit(solution)/shard_map/pallas_call | solution.py:1367
  304.8 0.0 copy-start
  304.8 0.0 copy-start.3
  304.8 0.0 copy-start.2
  304.8 0.0 copy-start.5
  304.9 0.0 copy-start.4
  304.9 3.5 %copy.33 = f32[1,576,1152]{2,1,0:T(8,128)} copy(f32[1,576,1152]{2,1,0:T(8,128)} %bitcast.25) | data formatting | bytes 5308416
  308.4 0.0 copy-done
  308.4 0.9 copy.34
  309.3 0.0 copy-done.3
  309.3 0.6 copy.35
  309.9 0.0 copy-done.2
  309.9 0.6 copy.36
  310.5 0.0 copy-done.5
  310.5 0.6 copy.37
  311.0 0.0 copy-done.4
  311.0 0.6 copy.38
Async XLA Ops:
  0.6 2.5 copy-start.1
  304.8 3.5 %copy-start = (f32[432,512]{1,0:T(8,128)S(1)}, f32[432,512]{1,0:T(8,128)}, u32[]{:S(2)}) copy-start(f32[432,512]{1,0:T(8,128)} %get-tuple-element.27) | copy-start | bytes 2654212
  304.8 4.5 %copy-start.3 = (f32[1,1152]{1,0:T(1,128)S(1)}, f32[1,1152]{1,0:T(1,128)}, u32[]{:S(2)}) copy-start(f32[1,1152]{1,0:T(1,128)} %get-tuple-element.46) | copy-start | bytes 13828
  304.8 5.0 %copy-start.2 = (f32[1,1152]{1,0:T(1,128)S(1)}, f32[1,1152]{1,0:T(1,128)}, u32[]{:S(2)}) copy-start(f32[1,1152]{1,0:T(1,128)} %get-tuple-element.47) | copy-start | bytes 13828
  304.8 5.6 %copy-start.5 = (f32[1,512]{1,0:T(1,128)S(1)}, f32[1,512]{1,0:T(1,128)}, u32[]{:S(2)}) copy-start(f32[1,512]{1,0:T(1,128)} %get-tuple-element.48) | copy-start | bytes 6148
  304.9 6.2 %copy-start.4 = (f32[1,512]{1,0:T(1,128)S(1)}, f32[1,512]{1,0:T(1,128)}, u32[]{:S(2)}) copy-start(f32[1,512]{1,0:T(1,128)} %get-tuple-element.49) | copy-start | bytes 6148

commit v8 on v7

--- a/solution.py
+++ b/solution.py
@@ -57,6 +57,9 @@
     w_s_back,
     w_t_back,
     cols,
+    raw,
+    raw_act,
+    raw_grad,
     a_in,
     skip_in,
     a_out,
@@ -99,6 +102,7 @@
     hub_sem,
 ):
     cm, frames, height, width = dims
+    breadth = clips.shape[2]
     rows = cm * frames * height * width
     d = a_in.shape[2]
     m_ch = hidden.shape[2]
@@ -122,26 +126,46 @@
 
     load_wt = pltpu.make_async_copy(w_t_hbm, w_t, w_sem.at[18])
 
-    def load_clip(m):
-        return pltpu.make_async_copy(clips.at[m], a_in.at[m], load_sem.at[m])
-
-    def load_cot(m):
-        return pltpu.make_async_copy(cotangent.at[m], ga_in.at[m], load_sem.at[m])
-
-    def load_skip(m):
-        return pltpu.make_async_copy(clips.at[m], skip_in.at[m], load_sem.at[m])
+    def load_raw(src, m):
+        at = pl.ds(m * cm, cm)
+        return pltpu.make_async_copy(src.at[at], raw.at[at], load_sem.at[m])
+
+    def unpack(m, dst):
+        pad = jnp.zeros((width - breadth, 128), f32)
+
+        def column(i, s):
+            pieces = []
+            for c in range(cm):
+                x = raw[m * cm + c, :, :, :, s].astype(f32)
+                x = jnp.transpose(x.reshape(height * breadth, frames, 128), (1, 0, 2))
+                for t in range(frames):
+                    for h in range(height):
+                        pieces += [x[t, h * breadth : (h + 1) * breadth], pad]
+            dst[m, :, s] = jnp.concatenate(pieces, axis=0).astype(bf16)
+
+        lane_chunks(d, column)
+
+    def pack(m, src, dst):
+        def column(i, s):
+            x = src[m, :, s].astype(f32).reshape(cm * frames * height, width, 128)
+            x = x[:, :breadth].reshape(cm, frames, height * breadth, 128)
+            for c in range(cm):
+                y = jnp.transpose(x[c], (1, 0, 2)).reshape(height, breadth, frames, 128)
+                dst[m * cm + c, :, :, :, s] = y.astype(bf16)
+
+        lane_chunks(d, column)
 
     local_skip = jnp.logical_not(jnp.logical_or(first, last))
 
     @pl.when(first)
     def _():
         for m in range(MB):
-            load_clip(m).start()
+            load_raw(clips, m).start()
 
     @pl.when(local_skip)
     def _():
         for m in range(MB):
-            load_skip(m).start()
+            load_raw(clips, m).start()
 
     for part in range(2):
         for tap in range(9):
@@ -151,7 +175,7 @@
     @pl.when(last)
     def _():
         for m in range(MB):
-            load_cot(m).start()
+            load_raw(cotangent, m).start()
 
     for ref in (o_gain_s, o_shift_s, o_gain_t, o_shift_t, gs_in, scale_in):
         ref[...] = jnp.zeros_like(ref)
@@ -314,7 +338,8 @@
         )
 
     def store(kind, src, dst, m):
-        return pltpu.make_async_copy(src.at[m], dst.at[m], store_sem.at[kind, m])
+        at = pl.ds(m * cm, cm)
+        return pltpu.make_async_copy(src.at[at], dst.at[at], store_sem.at[kind, m])
 
     def keep_operand(kind, src, dst, m):
         return pltpu.make_async_copy(src.at[m], dst.at[0, m], store_sem.at[kind, m])
@@ -444,7 +469,8 @@
 
     @pl.when(first)
     def _():
-        load_clip(0).wait()
+        load_raw(clips, 0).wait()
+        unpack(0, a_in)
         spatial_conv(0, True)
 
     sides = 3 - jnp.where(first, 1, 0) - jnp.where(last, 1, 0)
@@ -464,20 +490,29 @@
     def _():
         send_scale().start()
 
+    @pl.when(local_skip)
+    def _():
+        for m in range(MB):
+            load_raw(clips, m).wait()
+        lax.fori_loop(0, MB, lambda m, c: (unpack(m, skip_in), c)[1], 0)
+
+    @pl.when(last)
+    def _():
+        for m in range(MB):
+            load_raw(cotangent, m).wait()
+        lax.fori_loop(0, MB, lambda m, c: (unpack(m, ga_in), c)[1], 0)
+
     def forward_spatial(m):
         @pl.when(first & (m > 0))
         def _():
-            load_clip(m).wait()
+            load_raw(clips, m).wait()
+            unpack(m, a_in)
 
         @pl.when(jnp.logical_not(first))
         def _():
             @pl.when(m == 0)
             def _():
                 send_scale().wait_recv()
-
-            @pl.when(local_skip)
-            def _():
-                load_skip(m).wait()
 
             crossed(4, x_p, m)
 
@@ -554,7 +589,8 @@
             a_out[m, :, s] = value.astype(bf16)
 
         lane_chunks(d, column)
-        store(0, a_out, o_act, m).start()
+        pack(m, a_out, raw_act)
+        store(0, raw_act, o_act, m).start()
 
         @pl.when(section == 1)
         def _():
@@ -569,8 +605,6 @@
         return ga_in[m, :, s].astype(f32) * keep[m] * silu_slope(preact_own(m, s, normed))
 
     def backward_in(m):
-        load_cot(m).wait()
-
         def column(i, s):
             normed = normed_own(m, s)
             slope_sums(x_bt.at[m, me], own_slope(m, s, normed), normed, i, s)
@@ -692,7 +726,8 @@
                     cross(2, x_bp.at[m, 0], x_bt, m, -1)
                     half_to_pipe(4, part, ig_out, ga_in, m, -1).start()
 
-        store(1, ig_out, o_grad, m).start()
+        pack(m, ig_out, raw_grad)
+        store(1, raw_grad, o_grad, m).start()
 
     def send_skip_grad(m):
         to_pipe(1, gs_out, gs_in, m, jnp.where(last, -1, -2)).start()
@@ -801,8 +836,8 @@
     lax.fori_loop(0, 2 * pairs, step, 0)
 
     def finish(m, carry):
-        store(0, a_out, o_act, m).wait()
-        store(1, ig_out, o_grad, m).wait()
+        store(0, raw_act, o_act, m).wait()
+        store(1, raw_grad, o_grad, m).wait()
         for kind, src, dst in (
             (2, a_in, o_in),
             (3, hidden, o_hidden),
@@ -872,8 +907,8 @@
     return pl.pallas_call(
         functools.partial(relay_kernel, dims),
         out_shape=(
-            shape((MB, rows, d), bf16),
-            shape((MB, rows, d), bf16),
+            shape(clips.shape, bf16),
+            shape(clips.shape, bf16),
             shape((3 if hubs else 2, MB, rows, d), bf16),
             shape((2, MB, rows, m_ch), bf16),
             shape((3 if hubs else 2, MB, rows, m_ch), bf16),
@@ -891,6 +926,9 @@
             pltpu.VMEM((9 * m_ch, d), bf16),
             pltpu.VMEM((3 * d, m_ch), bf16),
             pltpu.VMEM((rows, 9 * m_ch), bf16),
+            pltpu.VMEM(clips.shape, bf16),
+            pltpu.VMEM(clips.shape, bf16),
+            pltpu.VMEM(clips.shape, bf16),
             narrow,
             narrow,
             narrow,
@@ -1439,9 +1477,8 @@
     rows = cm * frames * height * width
     m_ch = spatial_w.shape[2]
 
-    def padded(x):
-        x = jnp.pad(x, ((0, 0), (0, 0), (0, 0), (0, width - breadth), (0, 0)))
-        return x.reshape(MB, rows, d)
+    def frames_inside(x):
+        return x.transpose(0, 2, 3, 1, 4)
 
     n_dp = lax.axis_size("dp")
     hubs = n_dp == 8 and 9 * d // n_dp == 576 and 3 * m_ch // n_dp == 432 and d % 128 == 0
@@ -1449,7 +1486,7 @@
         (cm, frames, height, width),
         n_dp,
         hubs,
-        padded(clips),
+        frames_inside(clips),
         boxes,
         spatial_w[0],
         temporal_w[0],
@@ -1457,7 +1494,7 @@
         spatial_shift,
         temporal_gain,
         temporal_shift,
-        padded(cotangent),
+        frames_inside(cotangent),
     )
 
     def frames_of(x):
@@ -1479,8 +1516,8 @@
         grad_s = lax.psum_scatter(grad_s, "dp", scatter_dimension=0, tiled=True)
         grad_t = lax.psum_scatter(grad_t, "dp", scatter_dimension=0, tiled=True)
     return (
-        frames_of(act)[None],
-        frames_of(grad)[None],
+        act.transpose(0, 3, 1, 2, 4)[None],
+        grad.transpose(0, 3, 1, 2, 4)[None],
         grad_s[None],
         grad_t[None],
         gain_s,

time: 314 us -> 309 us (0.984)
  local copies, waits for them, and re-layouts: 14.1 us -> 7.09 us
    broadcast_in_dim x1 -> x0, local copies, waits for them, and re-layouts: 3.53 us -> none  [body(): frames_of(grad)[None]]
    unnamed x20 -> x24, local copies, waits for them, and re-layouts: 8.32 us -> 7.09 us
where the time goes in v8:
time: 309 us; the launch traced here: 307 us
  Pallas kernels  299 us (97%)
  local copies, waits for them, and re-layouts  7.09 us (2%)
    pallas_call x1, Pallas kernels, relay(): pl.pallas_call(functools.partial(relay_kernel, dims), out_shape=(shape(cl...  210 us
    pallas_call x1, Pallas kernels, gradients(): pl.pallas_call(functools.partial(gradient_kernel, dims), out_shape=(shape...  88.8 us
    unnamed x24, local copies, waits for them, and re-layouts  7.09 us

profile of v8, /device:TPU:0, one launch (start us, length us, event | category | flops | bytes accessed | tf_op | source)
XLA Modules:
  0.0 306.9 jit_solution(2523195529392333207)
XLA Ops:
  0.6 210.3 %shard_map.152 = (bf16[4,7,7,4,512]{4,3,2,1,0:T(4,128)(2,1)}, bf16[4,7,7,4,512]{4,3,2,1,0:T(4,128)(2,1)}, bf16[3,4,224,512]{3,2,1,0:T(8,128)(2,1)}, bf16[2,4,224...) custom-call(bf16[4,7,7,4,512]{4,3,2,1,0:T(4,128)(2,1)} %bitcast.26, ...), custom_call_target="tpu_custom_call" | custom-call | tf_op jit(solution)/shard_map/pallas_call | solution.py:907
  211.0 0.0 copy-start.3
  211.0 0.0 copy-start.2
  211.0 88.8 %shard_map.153 = (f32[576,1152]{1,0:T(8,128)}, f32[432,512]{1,0:T(8,128)}) custom-call(bf16[12,224,512]{2,1,0:T(8,128)(2,1)} %bitcast.20, bf16[8,224,1152]{2,1,0:T(8,128)(2,1)} %bitcast.18, bf16[12,224,1152]{2,1,0:T(8,128)(2,1)} %bitcast.17, bf16[8,224,512]{2,1,0:T(8,128)(2,1)} %bitcast.22), custom_call_target="tpu_custom_call" | custom-call | tf_op jit(solution)/shard_map/pallas_call | solution.py:1405
  299.8 0.0 copy-start
  299.8 0.0 copy-done.3
  299.8 0.9 copy.25
  300.7 0.0 copy-done.2
  300.7 0.0 copy-start.1
  300.7 0.9 copy.26
  301.6 0.5 copy-done
  302.1 0.0 copy-start.5
  302.1 0.0 copy-start.4
  302.1 0.0 copy-start.7
  302.1 0.0 copy-start.6
  302.1 1.5 copy.27
  303.6 0.0 copy-done.1
  303.6 0.9 copy.28
  304.5 0.0 copy-done.5
  304.5 0.6 copy.29
  305.1 0.0 copy-done.4
  305.1 0.6 copy.30
  305.7 0.0 copy-done.7
  305.7 0.6 copy.31
  306.3 0.0 copy-done.6
  306.3 0.6 copy.32
Async XLA Ops:
  211.0 88.8 %copy-start.3 = (bf16[4,7,7,4,512]{4,3,2,1,0:T(4,128)(2,1)S(1)}, bf16[4,7,7,4,512]{4,3,2,1,0:T(4,128)(2,1)}, u32[]{:S(2)}) copy-start(bf16[4,7,7,4,512]{4,3,2,1,0:T(4,128)(2,1)} %get-tuple-element.20) | copy-start | bytes 2408452
  211.0 89.7 %copy-start.2 = (bf16[4,7,7,4,512]{4,3,2,1,0:T(4,128)(2,1)S(1)}, bf16[4,7,7,4,512]{4,3,2,1,0:T(4,128)(2,1)}, u32[]{:S(2)}) copy-start(bf16[4,7,7,4,512]{4,3,2,1,0:T(4,128)(2,1)} %get-tuple-element.21) | copy-start | bytes 2408452
  299.8 2.3 copy-start
  300.7 2.9 copy-start.1
  302.1 2.4 copy-start.5
  302.1 3.0 copy-start.4
  302.1 3.6 %copy-start.7 = (f32[1,512]{1,0:T(1,128)S(1)}, f32[1,512]{1,0:T(1,128)}, u32[]{:S(2)}) copy-start(f32[1,512]{1,0:T(1,128)} %get-tuple-element.46) | copy-start | bytes 6148
  302.1 4.2 %copy-start.6 = (f32[1,512]{1,0:T(1,128)S(1)}, f32[1,512]{1,0:T(1,128)}, u32[]{:S(2)}) copy-start(f32[1,512]{1,0:T(1,128)} %get-tuple-element.47) | copy-start | bytes 6148

commit v9 on v8

--- a/solution.py
+++ b/solution.py
@@ -28,7 +28,7 @@
         body(i, pl.ds(pl.multiple_of(i * 128, 128), 128))
         return carry
 
-    lax.fori_loop(0, width // 128, step, 0)
+    lax.fori_loop(0, width // 128, step, 0, unroll=True)
 
 
 def relay_kernel(

time: 309 us -> 296 us (0.958)
  Pallas kernels: 299 us -> 286 us
    pallas_call x1, Pallas kernels: 210 us -> 197 us  [relay(): pl.pallas_call(functools.partial(relay_kernel, dims), out_shape=(shape(cl...]
where the time goes in v9:
time: 296 us; the launch traced here: 294 us
  Pallas kernels  286 us (97%)
  local copies, waits for them, and re-layouts  7.09 us (2%)
    pallas_call x1, Pallas kernels, relay(): pl.pallas_call(functools.partial(relay_kernel, dims), out_shape=(shape(cl...  197 us
    pallas_call x1, Pallas kernels, gradients(): pl.pallas_call(functools.partial(gradient_kernel, dims), out_shape=(shape...  88.8 us
    unnamed x24, local copies, waits for them, and re-layouts  7.09 us

profile of v9, /device:TPU:0, one launch (start us, length us, event | category | flops | bytes accessed | tf_op | source)
XLA Modules:
  0.0 293.6 jit_solution(15161824370350001259)
XLA Ops:
  0.6 197.0 %shard_map.152 = (bf16[4,7,7,4,512]{4,3,2,1,0:T(4,128)(2,1)}, bf16[4,7,7,4,512]{4,3,2,1,0:T(4,128)(2,1)}, bf16[3,4,224,512]{3,2,1,0:T(8,128)(2,1)}, bf16[2,4,224...) custom-call(bf16[4,7,7,4,512]{4,3,2,1,0:T(4,128)(2,1)} %bitcast.26, ...), custom_call_target="tpu_custom_call" | custom-call | tf_op jit(solution)/shard_map/pallas_call | solution.py:907
  197.6 0.0 copy-start.3
  197.6 0.0 copy-start.2
  197.6 88.8 %shard_map.153 = (f32[576,1152]{1,0:T(8,128)}, f32[432,512]{1,0:T(8,128)}) custom-call(bf16[12,224,512]{2,1,0:T(8,128)(2,1)} %bitcast.20, bf16[8,224,1152]{2,1,0:T(8,128)(2,1)} %bitcast.18, bf16[12,224,1152]{2,1,0:T(8,128)(2,1)} %bitcast.17, bf16[8,224,512]{2,1,0:T(8,128)(2,1)} %bitcast.22), custom_call_target="tpu_custom_call" | custom-call | tf_op jit(solution)/shard_map/pallas_call | solution.py:1405
  286.4 0.0 copy-start
  286.4 0.0 copy-done.3
  286.5 0.9 copy.25
  287.3 0.0 copy-done.2
  287.3 0.0 copy-start.1
  287.4 0.9 copy.26
  288.2 0.5 copy-done
  288.8 0.0 copy-start.5
  288.8 0.0 copy-start.4
  288.8 0.0 copy-start.7
  288.8 0.0 copy-start.6
  288.8 1.5 copy.27
  290.3 0.0 copy-done.1
  290.3 0.9 copy.28
  291.2 0.0 copy-done.5
  291.2 0.6 copy.29
  291.8 0.0 copy-done.4
  291.8 0.6 copy.30
  292.4 0.0 copy-done.7
  292.4 0.6 copy.31
  293.0 0.0 copy-done.6
  293.0 0.6 copy.32
Async XLA Ops:
  197.6 88.8 %copy-start.3 = (bf16[4,7,7,4,512]{4,3,2,1,0:T(4,128)(2,1)S(1)}, bf16[4,7,7,4,512]{4,3,2,1,0:T(4,128)(2,1)}, u32[]{:S(2)}) copy-start(bf16[4,7,7,4,512]{4,3,2,1,0:T(4,128)(2,1)} %get-tuple-element.20) | copy-start | bytes 2408452
  197.6 89.7 %copy-start.2 = (bf16[4,7,7,4,512]{4,3,2,1,0:T(4,128)(2,1)S(1)}, bf16[4,7,7,4,512]{4,3,2,1,0:T(4,128)(2,1)}, u32[]{:S(2)}) copy-start(bf16[4,7,7,4,512]{4,3,2,1,0:T(4,128)(2,1)} %get-tuple-element.21) | copy-start | bytes 2408452
  286.4 2.3 copy-start
  287.3 2.9 %copy-start.1 = (f32[432,512]{1,0:T(8,128)S(1)}, f32[432,512]{1,0:T(8,128)}, u32[]{:S(2)}) copy-start(f32[432,512]{1,0:T(8,128)} %get-tuple-element.27) | copy-start | bytes 2654212
  288.8 2.4 copy-start.5
  288.8 3.0 %copy-start.4 = (f32[1,1152]{1,0:T(1,128)S(1)}, f32[1,1152]{1,0:T(1,128)}, u32[]{:S(2)}) copy-start(f32[1,1152]{1,0:T(1,128)} %get-tuple-element.45) | copy-start | bytes 13828
  288.8 3.6 %copy-start.7 = (f32[1,512]{1,0:T(1,128)S(1)}, f32[1,512]{1,0:T(1,128)}, u32[]{:S(2)}) copy-start(f32[1,512]{1,0:T(1,128)} %get-tuple-element.46) | copy-start | bytes 6148
  288.8 4.2 %copy-start.6 = (f32[1,512]{1,0:T(1,128)S(1)}, f32[1,512]{1,0:T(1,128)}, u32[]{:S(2)}) copy-start(f32[1,512]{1,0:T(1,128)} %get-tuple-element.47) | copy-start | bytes 6148

commit v10 on v9

--- a/solution.py
+++ b/solution.py
@@ -253,7 +253,7 @@
             ).start()
             return carry
 
-        lax.fori_loop(1, n_dp, send, 0)
+        lax.fori_loop(1, n_dp, send, 0, unroll=n_dp <= 8)
 
     def shared(kind, buf, m):
         others = buf.at[m, pl.ds(0, n_dp - 1)]
@@ -272,7 +272,7 @@
             ).start()
             return carry
 
-        lax.fori_loop(0, n_dp, send, 0)
+        lax.fori_loop(0, n_dp, send, 0, unroll=n_dp <= 8)
 
     def crossed(kind, buf, m):
         slots = buf.at[m]
@@ -418,20 +418,15 @@
     def skipped_prev(m, s, value):
         return value + skip_prev * skip_in[m, :, s].astype(f32)
 
-    def activate(m, part, i, s):
+    def activate(m, part, skipped, i, s):
         s = lanes_of(part, i)
         n, mean, rstd = merged(m, x_p, part * (half // 128) + i, d)
         off_p[m, :, s] = x_p[m, me, :, s] / x_p[m, me, :, 2 * d :] - mean
         fact_p[m, :, s] = rstd
         value = preact_prev(m, s, normed_prev(m, s))
-
-        @pl.when(section == 2)
-        def _():
-            a_in[m, :, s] = (keep[m] * silu(skipped_prev(m, s, value))).astype(bf16)
-
-        @pl.when(section != 2)
-        def _():
-            a_in[m, :, s] = (keep[m] * silu(value)).astype(bf16)
+        if skipped:
+            value = skipped_prev(m, s, value)
+        a_in[m, :, s] = (keep[m] * silu(value)).astype(bf16)
 
     def spatial_conv(m, begins):
         for part in range(2):
@@ -440,7 +435,14 @@
                 @pl.when(jnp.logical_not(first))
                 def _():
                     half_to_pipe(2, part, r_out, r_in, m, 1).wait_recv()
-                    lane_chunks(half, functools.partial(activate, m, part))
+
+                @pl.when(section == 2)
+                def _():
+                    lane_chunks(half, functools.partial(activate, m, part, True))
+
+                @pl.when(odd)
+                def _():
+                    lane_chunks(half, functools.partial(activate, m, part, False))
 
             def column(i, s):
                 s = lanes_of(part, i)
@@ -635,11 +637,7 @@
             o_gain_t[:, s] += gain_sum
             normed = normed_own(m, s)
             slope = own_slope(m, s, normed)
-
-            @pl.when(last)
-            def _():
-                gs_out[m, :, s] = slope.astype(bf16)
-
+            gs_out[m, :, s] = slope.astype(bf16)
             scale = g_t[:, s] * fact_t[m, :, s]
             value = keep[m] * scale * (slope - (shift_sum + normed * gain_sum) / n)
             value = value.astype(bf16)
@@ -707,16 +705,15 @@
 
             @pl.when(jnp.logical_not(first))
             def _():
+                keeps = jnp.full((rows, 128), last.astype(f32))
+
                 def sums(i, s):
                     s = lanes_of(part, i)
                     normed = normed_prev(m, s)
                     slope = silu_slope(skipped_prev(m, s, preact_prev(m, s, normed)))
                     slope = ig_out[m, :, s].astype(f32) * keep[m] * slope
-
-                    @pl.when(section == 2)
-                    def _():
-                        gs_out[m, :, s] = slope.astype(bf16)
-
+                    held = gs_out[m, :, s].astype(f32)
+                    gs_out[m, :, s] = jnp.where(keeps > 0, held, slope).astype(bf16)
                     slope_sums(x_bp.at[m, 0], slope, normed, part * (half // 128) + i, s)
 
                 if part == 0:
@@ -994,8 +991,8 @@
 
 HUB_JOBS = (
     (0, 0, -1),
+    (1, 0, -1),
     (0, 1, 0),
-    (1, 0, -1),
     (2, 0, -1),
     (0, 2, 1),
     (2, 1, -1),

time: 296 us -> 294 us (level)
  Pallas kernels: 286 us -> 282 us
where the time goes in v10:
time: 294 us; the launch traced here: 290 us
  Pallas kernels  282 us (96%)
  local copies, waits for them, and re-layouts  7.09 us (2%)
    pallas_call x1, Pallas kernels, relay(): pl.pallas_call(functools.partial(relay_kernel, dims), out_shape=(shape(cl...  195 us
    pallas_call x1, Pallas kernels, gradients(): pl.pallas_call(functools.partial(gradient_kernel, dims), out_shape=(shape...  87.2 us
    unnamed x24, local copies, waits for them, and re-layouts  7.09 us

profile of v10, /device:TPU:0, one launch (start us, length us, event | category | flops | bytes accessed | tf_op | source)
XLA Modules:
  0.0 290.1 jit_solution(15893338436182430406)
XLA Ops:
  0.6 195.1 %shard_map.152 = (bf16[4,7,7,4,512]{4,3,2,1,0:T(4,128)(2,1)}, bf16[4,7,7,4,512]{4,3,2,1,0:T(4,128)(2,1)}, bf16[3,4,224,512]{3,2,1,0:T(8,128)(2,1)}, bf16[2,4,224...) custom-call(bf16[4,7,7,4,512]{4,3,2,1,0:T(4,128)(2,1)} %bitcast.26, ...), custom_call_target="tpu_custom_call" | custom-call | tf_op jit(solution)/shard_map/pallas_call | solution.py:904
  195.8 0.0 copy-start.3
  195.8 0.0 copy-start.2
  195.8 87.2 %shard_map.153 = (f32[576,1152]{1,0:T(8,128)}, f32[432,512]{1,0:T(8,128)}) custom-call(bf16[12,224,512]{2,1,0:T(8,128)(2,1)} %bitcast.20, bf16[8,224,1152]{2,1,0:T(8,128)(2,1)} %bitcast.18, bf16[12,224,1152]{2,1,0:T(8,128)(2,1)} %bitcast.17, bf16[8,224,512]{2,1,0:T(8,128)(2,1)} %bitcast.22), custom_call_target="tpu_custom_call" | custom-call | tf_op jit(solution)/shard_map/pallas_call | solution.py:1402
  283.0 0.0 copy-start
  283.0 0.0 copy-done.3
  283.0 0.9 copy.25
  283.9 0.0 copy-done.2
  283.9 0.0 copy-start.1
  283.9 0.9 copy.26
  284.8 0.5 copy-done
  285.3 0.0 copy-start.5
  285.3 0.0 copy-start.4
  285.3 0.0 copy-start.7
  285.3 0.0 copy-start.6
  285.3 1.5 copy.27
  286.8 0.0 copy-done.1
  286.8 0.9 copy.28
  287.7 0.0 copy-done.5
  287.7 0.6 copy.29
  288.3 0.0 copy-done.4
  288.3 0.6 copy.30
  288.9 0.0 copy-done.7
  288.9 0.6 copy.31
  289.5 0.0 copy-done.6
  289.5 0.6 copy.32
Async XLA Ops:
  195.8 87.2 %copy-start.3 = (bf16[4,7,7,4,512]{4,3,2,1,0:T(4,128)(2,1)S(1)}, bf16[4,7,7,4,512]{4,3,2,1,0:T(4,128)(2,1)}, u32[]{:S(2)}) copy-start(bf16[4,7,7,4,512]{4,3,2,1,0:T(4,128)(2,1)} %get-tuple-element.20) | copy-start | bytes 2408452
  195.8 88.1 %copy-start.2 = (bf16[4,7,7,4,512]{4,3,2,1,0:T(4,128)(2,1)S(1)}, bf16[4,7,7,4,512]{4,3,2,1,0:T(4,128)(2,1)}, u32[]{:S(2)}) copy-start(bf16[4,7,7,4,512]{4,3,2,1,0:T(4,128)(2,1)} %get-tuple-element.21) | copy-start | bytes 2408452
  283.0 2.3 copy-start
  283.9 2.9 %copy-start.1 = (f32[432,512]{1,0:T(8,128)S(1)}, f32[432,512]{1,0:T(8,128)}, u32[]{:S(2)}) copy-start(f32[432,512]{1,0:T(8,128)} %get-tuple-element.27) | copy-start | bytes 2654212
  285.3 2.4 copy-start.5
  285.3 3.0 %copy-start.4 = (f32[1,1152]{1,0:T(1,128)S(1)}, f32[1,1152]{1,0:T(1,128)}, u32[]{:S(2)}) copy-start(f32[1,1152]{1,0:T(1,128)} %get-tuple-element.45) | copy-start | bytes 13828
  285.3 3.6 %copy-start.7 = (f32[1,512]{1,0:T(1,128)S(1)}, f32[1,512]{1,0:T(1,128)}, u32[]{:S(2)}) copy-start(f32[1,512]{1,0:T(1,128)} %get-tuple-element.46) | copy-start | bytes 6148
  285.3 4.2 %copy-start.6 = (f32[1,512]{1,0:T(1,128)S(1)}, f32[1,512]{1,0:T(1,128)}, u32[]{:S(2)}) copy-start(f32[1,512]{1,0:T(1,128)} %get-tuple-element.47) | copy-start | bytes 6148

commit v11 on v10

--- a/solution.py
+++ b/solution.py
@@ -698,30 +698,30 @@
             to_pipe(1, gs_out, gs_in, m, -1).wait_recv()
 
         with_skip = even_inner.astype(f32)
+        keeps = jnp.full((rows, 128), last.astype(f32))
+
+        def sums(part, i, s):
+            s = lanes_of(part, i)
+            normed = normed_prev(m, s)
+            slope = silu_slope(skipped_prev(m, s, preact_prev(m, s, normed)))
+            slope = ig_out[m, :, s].astype(f32) * keep[m] * slope
+            held = gs_out[m, :, s].astype(f32)
+            gs_out[m, :, s] = jnp.where(keeps > 0, held, slope).astype(bf16)
+            slope_sums(x_bp.at[m, 0], slope, normed, part * (half // 128) + i, s)
+
         for part in range(2):
             s = slice(part * half, (part + 1) * half)
             value = jnp.dot(cols[...], w_s_back[:, s], preferred_element_type=f32)
+            if part == 1:
+                lane_chunks(half, functools.partial(sums, 0))
             ig_out[m, :, s] = (value + with_skip * gs_in[m, :, s].astype(f32)).astype(bf16)
 
             @pl.when(jnp.logical_not(first))
             def _():
-                keeps = jnp.full((rows, 128), last.astype(f32))
-
-                def sums(i, s):
-                    s = lanes_of(part, i)
-                    normed = normed_prev(m, s)
-                    slope = silu_slope(skipped_prev(m, s, preact_prev(m, s, normed)))
-                    slope = ig_out[m, :, s].astype(f32) * keep[m] * slope
-                    held = gs_out[m, :, s].astype(f32)
-                    gs_out[m, :, s] = jnp.where(keeps > 0, held, slope).astype(bf16)
-                    slope_sums(x_bp.at[m, 0], slope, normed, part * (half // 128) + i, s)
-
-                if part == 0:
-                    half_to_pipe(4, part, ig_out, ga_in, m, -1).start()
-                lane_chunks(half, sums)
                 if part == 1:
+                    lane_chunks(half, functools.partial(sums, 1))
                     cross(2, x_bp.at[m, 0], x_bt, m, -1)
-                    half_to_pipe(4, part, ig_out, ga_in, m, -1).start()
+                half_to_pipe(4, part, ig_out, ga_in, m, -1).start()
 
         pack(m, ig_out, raw_grad)
         store(1, raw_grad, o_grad, m).start()

time: 294 us -> 293 us (level)
  no operation moved by 1% of the time
where the time goes in v11:
time: 293 us; the launch traced here: 289 us
  Pallas kernels  281 us (96%)
  local copies, waits for them, and re-layouts  7.09 us (2%)
    pallas_call x1, Pallas kernels, relay(): pl.pallas_call(functools.partial(relay_kernel, dims), out_shape=(shape(cl...  194 us
    pallas_call x1, Pallas kernels, gradients(): pl.pallas_call(functools.partial(gradient_kernel, dims), out_shape=(shape...  87.2 us
    unnamed x24, local copies, waits for them, and re-layouts  7.09 us

profile of v11, /device:TPU:0, one launch (start us, length us, event | category | flops | bytes accessed | tf_op | source)
XLA Modules:
  0.0 289.0 jit_solution(14015442544433930834)
XLA Ops:
  0.6 194.0 %shard_map.152 = (bf16[4,7,7,4,512]{4,3,2,1,0:T(4,128)(2,1)}, bf16[4,7,7,4,512]{4,3,2,1,0:T(4,128)(2,1)}, bf16[3,4,224,512]{3,2,1,0:T(8,128)(2,1)}, bf16[2,4,224...) custom-call(bf16[4,7,7,4,512]{4,3,2,1,0:T(4,128)(2,1)} %bitcast.26, ...), custom_call_target="tpu_custom_call" | custom-call | tf_op jit(solution)/shard_map/pallas_call | solution.py:904
  194.7 0.0 copy-start.3
  194.7 0.0 copy-start.2
  194.7 87.2 %shard_map.153 = (f32[576,1152]{1,0:T(8,128)}, f32[432,512]{1,0:T(8,128)}) custom-call(bf16[12,224,512]{2,1,0:T(8,128)(2,1)} %bitcast.20, bf16[8,224,1152]{2,1,0:T(8,128)(2,1)} %bitcast.18, bf16[12,224,1152]{2,1,0:T(8,128)(2,1)} %bitcast.17, bf16[8,224,512]{2,1,0:T(8,128)(2,1)} %bitcast.22), custom_call_target="tpu_custom_call" | custom-call | tf_op jit(solution)/shard_map/pallas_call | solution.py:1402
  281.9 0.0 copy-start
  281.9 0.0 copy-done.3
  281.9 0.9 copy.25
  282.8 0.0 copy-done.2
  282.8 0.0 copy-start.1
  282.8 0.9 copy.26
  283.7 0.5 copy-done
  284.2 0.0 copy-start.5
  284.2 0.0 copy-start.4
  284.2 0.0 copy-start.7
  284.2 0.0 copy-start.6
  284.2 1.5 copy.27
  285.7 0.0 copy-done.1
  285.7 0.9 copy.28
  286.6 0.0 copy-done.5
  286.6 0.6 copy.29
  287.2 0.0 copy-done.4
  287.2 0.6 copy.30
  287.8 0.0 copy-done.7
  287.8 0.6 copy.31
  288.4 0.0 copy-done.6
  288.4 0.6 copy.32
Async XLA Ops:
  194.7 87.2 %copy-start.3 = (bf16[4,7,7,4,512]{4,3,2,1,0:T(4,128)(2,1)S(1)}, bf16[4,7,7,4,512]{4,3,2,1,0:T(4,128)(2,1)}, u32[]{:S(2)}) copy-start(bf16[4,7,7,4,512]{4,3,2,1,0:T(4,128)(2,1)} %get-tuple-element.20) | copy-start | bytes 2408452
  194.7 88.1 %copy-start.2 = (bf16[4,7,7,4,512]{4,3,2,1,0:T(4,128)(2,1)S(1)}, bf16[4,7,7,4,512]{4,3,2,1,0:T(4,128)(2,1)}, u32[]{:S(2)}) copy-start(bf16[4,7,7,4,512]{4,3,2,1,0:T(4,128)(2,1)} %get-tuple-element.21) | copy-start | bytes 2408452
  281.9 2.3 copy-start
  282.8 2.9 %copy-start.1 = (f32[432,512]{1,0:T(8,128)S(1)}, f32[432,512]{1,0:T(8,128)}, u32[]{:S(2)}) copy-start(f32[432,512]{1,0:T(8,128)} %get-tuple-element.27) | copy-start | bytes 2654212
  284.2 2.4 copy-start.5
  284.2 3.0 %copy-start.4 = (f32[1,1152]{1,0:T(1,128)S(1)}, f32[1,1152]{1,0:T(1,128)}, u32[]{:S(2)}) copy-start(f32[1,1152]{1,0:T(1,128)} %get-tuple-element.45) | copy-start | bytes 13828
  284.2 3.6 %copy-start.7 = (f32[1,512]{1,0:T(1,128)S(1)}, f32[1,512]{1,0:T(1,128)}, u32[]{:S(2)}) copy-start(f32[1,512]{1,0:T(1,128)} %get-tuple-element.46) | copy-start | bytes 6148
  284.2 4.2 %copy-start.6 = (f32[1,512]{1,0:T(1,128)S(1)}, f32[1,512]{1,0:T(1,128)}, u32[]{:S(2)}) copy-start(f32[1,512]{1,0:T(1,128)} %get-tuple-element.47) | copy-start | bytes 6148
